TPU v7x, 512 devices: a whole 4x8x8 slice. The times are simulated.
512 devices in a mesh: runs: 64 (over z_lo, y, core), terms: 8 (over z_hi, x).
Axes of the slice: x: 4, y: 8, z: 8 (z_hi: 2, z_lo: 4; z = z_hi * 4 + z_lo), core: 2. Of those that a mesh axis runs over, the one named last changes fastest.
Arguments:
- design: bfloat16 [16384, 53248], P('runs', 'terms'), may hold values from -6 to 6
- responses: float32 [8, 16384], P(None, 'runs'), may hold values from -6 to 6
- picks: int32 [2, 256], replicated, may hold values from 0 to 53247, as said below
Outputs:
- residual: float32 [8, 16384], P(None, 'runs')
- correlations: float32 [8, 53248], P(None, 'terms')
Inputs may be any that keep to these rules, and one draw needn't show every extreme that they name: `picks`: all 2 times 256 entries are distinct terms.
All inputs are finite; a program needn't handle non-finite values.
Results may differ from a plain program's by a relative error of at most 0.003.
Values may be sent and summed in bfloat16 or wider, within the bound.
No kernel may reach another device: no remote copies, remote signals or barrier semaphores. Data moves between devices by JAX's collectives and lax.ppermute only.
A program may use at most 64 MiB of HBM per device.

v0:
```python
import jax
import jax.numpy as jnp
from jax import lax
from jax.sharding import PartitionSpec as P

STEPS = 2


def fetch_columns(design, indices):
    local_terms = design.shape[1]
    offset = lax.axis_index("terms") * local_terms
    positions = lax.broadcasted_iota(jnp.int32, (indices.shape[0], local_terms), 1)
    wanted = (indices - offset)[:, None]
    selector = (positions == wanted).astype(jnp.bfloat16)
    partial_cols = lax.dot_general(
        selector, design, (((1,), (1,)), ((), ())), preferred_element_type=jnp.float32
    )
    return lax.psum(partial_cols.astype(jnp.bfloat16), "terms").astype(jnp.float32)


def local(design, responses, picks):
    high = lax.Precision.HIGHEST
    local_rows = design.shape[0]
    residual = responses
    basis = None
    for step in range(STEPS):
        block = fetch_columns(design, picks[step])
        if basis is not None:
            proj = lax.psum(jnp.dot(basis, block.T, precision=high), "runs")
            block = block - jnp.dot(proj.T, basis, precision=high)
        gram = lax.psum(jnp.dot(block, block.T, precision=high), "runs")
        lower = jnp.linalg.cholesky(gram)
        newq = jax.scipy.linalg.solve_triangular(lower, block, lower=True)
        coef = lax.psum(jnp.dot(residual, newq.T, precision=high), "runs")
        residual = residual - jnp.dot(coef, newq, precision=high)
        basis = newq if basis is None else jnp.concatenate([basis, newq], axis=0)
    rounded = residual.astype(jnp.bfloat16)
    scale_factor = jnp.float32(local_rows * lax.axis_size("runs")) ** (-0.5)
    local_corr = jnp.dot(rounded, design, preferred_element_type=jnp.float32) * scale_factor
    correlations = lax.psum(local_corr, "runs")
    return (residual, correlations)


def solution(mesh):
    placed = (P("runs", "terms"), P(None, "runs"), P())
    return jax.shard_map(
        local,
        mesh=mesh,
        in_specs=placed,
        out_specs=(P(None, "runs"), P(None, "terms")),
        check_vma=False,
    )
```

profile of v0, /device:TPU:1, one launch (start us, length us, event | category | flops | bytes accessed | tf_op | source)
XLA Modules:
  0.0 2387.7 jit_solution(11282480116618474576)
XLA Ops:
  8.1 1.1 copy-done
  9.2 1.8 fusion.5
  10.9 1.7 fusion.4
  12.7 112.9 %all-reduce.16.cloned.1.call-done = (bf16[256,256]{1,0:T(8,128)(2,1)}, bf16[256,256]{1,0:T(8,128)(2,1)}) async-done(((bf16[256,256]{1,0:T(8,128)(2,1)}, bf16[256,256]{1,0:T(8,128)(2,1)}), (bf16[256,256]{1,0:T(8,128)(2,1)}, bf16[256,256]{1,0:T(8,128)(2,1)})) %all-reduce.16.cloned.1.call-update) | async-done | bytes 262160 | tf_op jit(solution)/shard_map/psum | solution.py:18
  125.7 1.9 fusion.33
  128.4 1.6 convert_element_type.18
  130.0 491.6 %all-reduce.8.cloned.1.call-done = f32[256,256]{0,1:T(8,128)} async-done(((f32[256,256]{0,1:T(8,128)}), f32[256,256]{0,1:T(8,128)}) %all-reduce.8.cloned.1.call-update) | async-done | bytes 262160 | tf_op jit(solution)/shard_map/psum | solution.py:31
  621.5 1.8 copy.6
  625.1 11.7 cholesky.130
  637.5 9.8 custom-call.13
  647.4 1.7 constant_dynamic-update-slice_fusion.3
  649.0 1.1 convolution_subtract_fusion.4
  650.1 11.7 cholesky.147
  664.4 1.7 select_select_fusion.1
  666.8 5.9 while.4
  667.6 2.3 bitcast_dynamic-update-slice_fusion.4
  670.5 2.2 bitcast_dynamic-update-slice_fusion.4
  672.7 20.3 custom-call.14
  693.0 1.2 fusion.11
  694.2 1.2 convolution_subtract_fusion.2
  695.5 1.2 fusion.19
  697.3 1.9 fusion.13
  699.3 489.0 %all-reduce.10.cloned.1.call-done = f32[256,256]{1,0:T(8,128)} async-done(((f32[256,256]{1,0:T(8,128)}), f32[256,256]{1,0:T(8,128)}) %all-reduce.10.cloned.1.call-update) | async-done | bytes 262160 | tf_op jit(solution)/shard_map/psum | solution.py:29
  1188.3 1.6 convolution_subtract_fusion
  1190.7 1.1 fusion.34
  1191.9 1.9 convolution_bitcast_fusion
  1193.8 262.4 %psum.58 = f32[8,256]{0,1:T(8,128)} all-reduce(f32[8,256]{0,1:T(8,128)} %convolution_bitcast_fusion), channel_id=1, replica_groups=mesh['runs'=64,'terms'=8] {'runs'}, use_global_device_ids=true, to_apply=%region_6.0 | all-reduce | flops 2048 | bytes 16384 | tf_op jit(solution)/shard_map/psum | solution.py:34
  1456.2 1.3 convolution_subtract_fusion.6
  1457.5 223.4 %all-reduce.12.cloned.1.call-done = f32[256,256]{0,1:T(8,128)} async-done(((f32[256,256]{0,1:T(8,128)}), f32[256,256]{0,1:T(8,128)}) %all-reduce.12.cloned.1.call-update) | async-done | bytes 262160 | tf_op jit(solution)/shard_map/psum | solution.py:31
  1680.9 1.8 copy.8
  1684.5 11.7 cholesky.164
  1696.9 9.8 custom-call.15
  1706.8 1.7 constant_dynamic-update-slice_fusion.1
  1708.4 1.1 convolution_subtract_fusion.3
  1709.5 11.7 cholesky.181
  1724.5 1.7 select_select_fusion
  1726.2 7.2 while.5
  1727.5 2.3 bitcast_dynamic-update-slice_fusion.5
  1731.1 2.3 bitcast_dynamic-update-slice_fusion.5
  1733.4 20.6 custom-call.16
  1754.0 1.2 fusion.9
  1755.2 1.2 convolution_subtract_fusion.1
  1756.4 1.1 fusion.15
  1758.5 137.5 %psum.62 = f32[8,256]{1,0:T(8,128)} all-reduce(f32[8,256]{1,0:T(8,128)S(1)} %fusion.8), channel_id=1, replica_groups=mesh['runs'=64,'terms'=8] {'runs'}, use_global_device_ids=true, to_apply=%region_10.13 | all-reduce | flops 2048 | bytes 16384 | tf_op jit(solution)/shard_map/psum | solution.py:34
  1896.0 1.1 convolution_subtract_fusion.5
  1897.2 1.2 convolution_multiply_fusion
  1898.4 481.1 %all-reduce.14.cloned.1.call-done = f32[8,6656]{1,0:T(8,128)} async-done(((f32[8,6656]{1,0:T(8,128)}), f32[8,6656]{1,0:T(8,128)}) %all-reduce.14.cloned.1.call-update) | async-done | bytes 213008 | tf_op jit(solution)/shard_map/psum | solution.py:40
  2379.5 1.6 copy.39
  (54 shorter events, 16.9 us)
Async XLA Ops:
  7.2 2.0 copy-start
  7.2 118.5 %all-reduce.16.cloned.1.call-start = ((), (), s32[]{:S(2)}) async-start(), calls=%async_computation.4 | async-start | bytes 524288 | tf_op jit(solution)/shard_map/psum | solution.py:18
  12.7 608.8 %all-reduce.8.cloned.1.call-start = ((), (), s32[]{:S(2)}) async-start(), calls=%async_computation | async-start | bytes 524288 | tf_op jit(solution)/shard_map/psum | solution.py:31
  127.6 1060.7 %all-reduce.10.cloned.1.call-start = ((), (), s32[]{:S(2)}) async-start(), calls=%async_computation.1 | async-start | bytes 524288 | tf_op jit(solution)/shard_map/psum | solution.py:29
  624.4 0.7 copy-start.4
  625.1 566.8 %copy-start.7 = (f32[8,256]{1,0:T(8,128)S(1)}, f32[8,256]{1,0:T(8,128)}, u32[]{:S(2)}) copy-start(f32[8,256]{1,0:T(8,128)} %param.7) | copy-start | bytes 24580
  672.7 521.1 %copy-start.8 = (s32[2,2]{1,0:T(2,128)}, s32[2,2]{1,0:T(2,128)S(1)}, u32[]{:S(2)}) copy-start(s32[2,2]{1,0:T(2,128)S(1)} %get-tuple-element.176) | copy-start | bytes 52
  696.6 0.7 copy-start.2
  699.2 981.7 %all-reduce.12.cloned.1.call-start = ((), (), s32[]{:S(2)}) async-start(), calls=%async_computation.2 | async-start | bytes 524288 | tf_op jit(solution)/shard_map/psum | solution.py:31
  1190.0 0.7 copy-start.1
  1191.8 1187.7 %all-reduce.14.cloned.1.call-start = ((), (), s32[]{:S(2)}) async-start(), calls=%async_computation.3 | async-start | bytes 425984 | tf_op jit(solution)/shard_map/psum | solution.py:40
  1683.8 0.7 copy-start.5
  1757.6 0.7 copy-start.3
  1897.1 484.1 %copy-start.6 = (f32[8,256]{1,0:T(8,128)}, f32[8,256]{1,0:T(8,128)S(1)}, u32[]{:S(2)}) copy-start(f32[8,256]{1,0:T(8,128)S(1)} %convolution_subtract_fusion.5) | copy-start | bytes 24580
Sparse Core Ops, SparseCore 0:
  12.8 112.8 all-reduce.15
  128.8 492.6 all-reduce.7
  699.4 488.9 all-reduce.9
  1191.9 488.9 all-reduce.11
  1898.6 480.9 all-reduce.13
where the time goes:
time: 2390 us
  waiting for transfers between devices  1800 us (75%)
  blocking collectives  400 us (17%)
  other arithmetic  119 us (5%)
  matrix products  28.6 us (1%)
  local copies, waits for them, and re-layouts  24.7 us (1%)
    psum x2, waiting for transfers between devices, local(): gram = lax.psum(jnp.dot(block, block.T, precision=high), 'runs')  715 us
    psum x1, waiting for transfers between devices, local(): proj = lax.psum(jnp.dot(basis, block.T, precision=high), 'runs')  489 us
    psum x1, waiting for transfers between devices, local(): correlations = lax.psum(local_corr, 'runs')  481 us
    psum x2, blocking collectives, local(): coef = lax.psum(jnp.dot(residual, newq.T, precision=high), 'runs')  400 us
    psum x1, waiting for transfers between devices, fetch_columns(): lax.psum(partial_cols.astype(jnp.bfloat16), 'terms').astype(jnp.float32)  113 us
    another operation x13, other arithmetic, local(): lower = jnp.linalg.cholesky(gram)  69.8 us
  transfers between devices with their start and end apart: 5, of which 5 were waited for; matrix products, arithmetic and copies ran while one was open for 0% of the time, Pallas kernels for 0%

commit v1 on v0

v1 whole, which is shorter than its diff:
```python
import jax
import jax.numpy as jnp
from jax import lax
from jax.sharding import PartitionSpec as P

LANES = 128


def exchange(pieces, axis):
    return lax.all_to_all(pieces, axis, 0, 0)


def share(piece, axis):
    count = lax.axis_size(axis)
    return exchange(jnp.broadcast_to(piece[None], (count, *piece.shape)), axis)


def fetch_columns(design, indices):
    local_terms = design.shape[1]
    devices = lax.axis_size("terms")
    count = indices.shape[0]
    offset = lax.axis_index("terms") * local_terms
    positions = lax.broadcasted_iota(jnp.int32, (count, local_terms), 1)
    selector = (positions == (indices - offset)[:, None]).astype(jnp.bfloat16)
    partial_cols = lax.dot_general(
        selector, design, (((1,), (1,)), ((), ())), preferred_element_type=jnp.float32
    ).astype(jnp.bfloat16)
    pieces = exchange(partial_cols.reshape(devices, count // devices, -1), "terms")
    own = jnp.sum(pieces.astype(jnp.float32), axis=0).astype(jnp.bfloat16)
    return own, share(own, "terms").reshape(count, -1)


def local(design, responses, picks):
    high = lax.Precision.HIGHEST
    run_devices = lax.axis_size("runs")
    resp, local_rows = responses.shape
    indices = picks.reshape(-1)
    count = indices.shape[0]
    own, basis = fetch_columns(design, indices)
    basis32 = basis.astype(jnp.float32)
    gram_rows = lax.dot_general(
        own, basis, (((1,), (1,)), ((), ())), preferred_element_type=jnp.float32
    )
    inner_rows = lax.dot_general(
        own.astype(jnp.float32), responses, (((1,), (1,)), ((), ())), precision=high
    )
    rows = jnp.concatenate([gram_rows, inner_rows], axis=1)
    rows = jnp.pad(rows, ((0, 0), (0, -rows.shape[1] % LANES)))
    per = rows.shape[0] // run_devices
    summed = jnp.sum(exchange(rows.reshape(run_devices, per, -1), "runs"), axis=0)
    block = share(summed, "runs").reshape(rows.shape)
    system = share(block, "terms").reshape(count, -1)
    gram, inner = system[:, :count], system[:, count : count + resp]
    lower = jnp.linalg.cholesky(gram)
    half = jax.scipy.linalg.solve_triangular(lower, inner, lower=True)
    coef = jax.scipy.linalg.solve_triangular(lower, half, lower=True, trans=1).T
    residual = responses - jnp.dot(coef, basis32, precision=high)
    rounded = residual.astype(jnp.bfloat16)
    scale_factor = jnp.float32(local_rows * run_devices) ** (-0.5)
    partial_corr = jnp.dot(rounded, design, preferred_element_type=jnp.float32) * scale_factor
    tiles = partial_corr.shape[1] // LANES
    pieces = partial_corr.reshape(resp, tiles, LANES).transpose(1, 0, 2)
    pieces = jnp.pad(pieces, ((0, run_devices - tiles), (0, 0), (0, 0)))
    total = jnp.sum(exchange(pieces, "runs"), axis=0)
    gathered = share(total, "runs")[:tiles]
    correlations = gathered.transpose(1, 0, 2).reshape(resp, -1)
    return (residual, correlations)


def solution(mesh):
    placed = (P("runs", "terms"), P(None, "runs"), P())
    return jax.shard_map(
        local,
        mesh=mesh,
        in_specs=placed,
        out_specs=(P(None, "runs"), P(None, "terms")),
        check_vma=False,
    )
```

time: 2390 us -> 359 us (0.15)
  waiting for transfers between devices: 1800 us -> 28.9 us
  blocking collectives: 400 us -> 115 us
    psum x5 -> x0, waiting for transfers between devices: 1800 us -> none  [the longest x2 715 us: local(): gram = lax.psum(jnp.dot(block, block.T, precision=high), 'runs')]
    psum x2 -> x0, blocking collectives: 400 us -> none  [local(): coef = lax.psum(jnp.dot(residual, newq.T, precision=high), 'runs')]
    all_to_all x0 -> x5, blocking collectives: none -> 115 us  [exchange(): return lax.all_to_all(pieces, axis, 0, 0)]
    all_to_all x0 -> x2, waiting for transfers between devices: none -> 28.9 us  [exchange(): return lax.all_to_all(pieces, axis, 0, 0)]
    another operation x13 -> x14, other arithmetic: 69.8 us -> 86.7 us  [local(): lower = jnp.linalg.cholesky(gram)]
  transfers between devices with their start and end apart: 5 -> 2, of which waited for: 5 -> 2; matrix products, arithmetic and copies ran while one was open for 0% -> 0% of each run, Pallas kernels for 0% -> 0%
where the time goes in v1:
time: 359 us; the launch traced here: 353 us
  other arithmetic  136 us (38%)
  blocking collectives  115 us (32%)
  matrix products  30.7 us (9%)
  local copies, waits for them, and re-layouts  29.7 us (8%)
  waiting for transfers between devices  28.9 us (8%)
  starting transfers between devices  8.76 us (2%)
  between operations  3.62 us (1%)
    all_to_all x5, blocking collectives, exchange(): return lax.all_to_all(pieces, axis, 0, 0)  115 us
    another operation x14, other arithmetic, local(): lower = jnp.linalg.cholesky(gram)  86.7 us
    another operation x3, other arithmetic, local(): coef = jax.scipy.linalg.solve_triangular(lower, half, lower=True, trans=1).T  43.6 us
    all_to_all x2, waiting for transfers between devices, exchange(): return lax.all_to_all(pieces, axis, 0, 0)  28.9 us
    another operation x12, local copies, waits for them, and re-layouts  13.6 us
    another operation x6, matrix products, local(): lower = jnp.linalg.cholesky(gram)  10.2 us
    all_to_all x2, starting transfers between devices, exchange(): return lax.all_to_all(pieces, axis, 0, 0)  8.76 us
    another operation x7, matrix products, local(): half = jax.scipy.linalg.solve_triangular(lower, inner, lower=True)  7.55 us
  transfers between devices with their start and end apart: 2, of which 2 were waited for; matrix products, arithmetic and copies ran while one was open for 0% of the time, Pallas kernels for 0%

profile of v1, /device:TPU:1, one launch (start us, length us, event | category | flops | bytes accessed | tf_op | source)
XLA Modules:
  0.0 352.7 jit_solution(16914645112511507770)
XLA Ops:
  1.5 1.1 copy-done
  2.6 2.4 fusion.2
  5.0 23.2 %all_to_all.35 = bf16[8,64,256]{2,1,0:T(8,128)(2,1)} all-to-all(bf16[8,64,256]{2,1,0:T(8,128)(2,1)S(1)} %bitcast.84), channel_id=1, replica_groups=mesh['runs'=64,'terms'=8] {'terms'}, dimensions={0} | all-to-all | bytes 524288 | tf_op jit(solution)/shard_map/all_to_all | solution.py:10
  29.9 4.0 %all-to-all-start.1 = ((bf16[8,64,256]{2,1,0:T(8,128)(2,1)}), bf16[8,64,256]{2,1,0:T(8,128)(2,1)}, u32[]{:S(2)}, u32[]{:S(2)}) async-start(bf16[8,64,256]{2,1,0:T(8,128)(2,1)} %broadcast_in_dim.11), calls=%async_computation.1 | async-start | bytes 524288 | tf_op jit(solution)/shard_map/all_to_all | solution.py:10
  34.1 9.8 %all-to-all-done.1 = bf16[8,64,256]{2,1,0:T(8,128)(2,1)} async-done(((bf16[8,64,256]{2,1,0:T(8,128)(2,1)}), bf16[8,64,256]{2,1,0:T(8,128)(2,1)}, u32[]{:S(2)}, u32[]{:S(2)}) %all-to-all-start.1) | async-done | bytes 262176 | tf_op jit(solution)/shard_map/all_to_all | solution.py:10
  44.0 1.1 fusion.63
  45.3 26.0 %all_to_all.36 = f32[64,1,640]{2,1,0:T(1,128)} all-to-all(f32[64,1,640]{2,1,0:T(1,128)S(1)} %copy.11), channel_id=1, replica_groups=mesh['runs'=64,'terms'=8] {'runs'}, dimensions={0} | all-to-all | bytes 327680 | tf_op jit(solution)/shard_map/all_to_all | solution.py:10
  71.3 1.0 reduce_sum.31
  72.4 15.4 %all_to_all.37 = f32[64,1,640]{2,1,0:T(1,128)S(1)} all-to-all(f32[64,1,640]{2,1,0:T(1,128)S(1)} %broadcast_in_dim.12), channel_id=1, replica_groups=mesh['runs'=64,'terms'=8] {'runs'}, dimensions={0} | all-to-all | bytes 327680 | tf_op jit(solution)/shard_map/all_to_all | solution.py:10
  87.9 1.2 broadcast_in_dim.15
  89.0 4.7 %all-to-all-start.4 = ((f32[8,64,640]{2,1,0:T(8,128)}), f32[8,64,640]{2,1,0:T(8,128)}, u32[]{:S(2)}, u32[]{:S(2)}) async-start(f32[8,64,640]{2,1,0:T(8,128)} %broadcast_in_dim.15), calls=%async_computation.4 | async-start | bytes 2621440 | tf_op jit(solution)/shard_map/all_to_all | solution.py:10
  94.3 19.1 %all-to-all-done.4 = f32[8,64,640]{2,1,0:T(8,128)} async-done(((f32[8,64,640]{2,1,0:T(8,128)}), f32[8,64,640]{2,1,0:T(8,128)}, u32[]{:S(2)}, u32[]{:S(2)}) %all-to-all-start.4) | async-done | bytes 1310752 | tf_op jit(solution)/shard_map/all_to_all | solution.py:10
  113.4 2.3 slice.171
  115.7 2.5 copy.19
  118.2 1.8 fusion.4
  121.0 11.7 %cholesky.104 = f32[128,128]{1,0:T(8,128)S(1)} custom-call(f32[128,128]{1,0:T(8,128)S(1)} %cholesky.266), custom_call_target="Cholesky" | custom-call | tf_op jit(solution)/shard_map/jit(cholesky)/cholesky | solution.py:54
  132.8 1.1 cholesky.224
  133.9 1.6 fusion.62
  135.4 9.8 %custom-call.34 = f32[1,128,128]{1,2,0:T(8,128)S(1)} custom-call(f32[1,128,128]{2,1,0:T(8,128)S(1)} %get-tuple-element.32), custom_call_target="InvertDiagBlocksLowerTriangular" | custom-call | tf_op jit(solution)/shard_map/jit(cholesky)/cholesky | solution.py:54
  145.3 1.9 constant_dynamic-update-slice_fusion.3
  147.2 1.3 convolution_subtract_fusion
  149.1 11.7 %cholesky.217 = f32[128,128]{1,0:T(8,128)S(1)} custom-call(f32[128,128]{1,0:T(8,128)S(1)} %cholesky.270), custom_call_target="Cholesky" | custom-call | tf_op jit(solution)/shard_map/jit(cholesky)/cholesky | solution.py:54
  161.5 10.0 %custom-call.35 = f32[1,128,128]{1,2,0:T(8,128)S(1)} custom-call(f32[1,128,128]{2,1,0:T(8,128)S(1)} %get-tuple-element.29), custom_call_target="InvertDiagBlocksLowerTriangular" | custom-call | tf_op jit(solution)/shard_map/jit(cholesky)/cholesky | solution.py:54
  171.4 1.8 convolution_dynamic-update-slice_fusion
  173.3 1.4 convolution_subtract_fusion.1
  175.3 13.2 %cholesky.238 = f32[128,128]{1,0:T(8,128)} custom-call(f32[128,128]{1,0:T(8,128)} %cholesky.275), custom_call_target="Cholesky" | custom-call | tf_op jit(solution)/shard_map/jit(cholesky)/cholesky | solution.py:54
  188.5 1.5 select_reduce_fusion.1
  190.7 11.3 %custom-call.36 = f32[1,128,128]{1,2,0:T(8,128)} custom-call(f32[1,128,128]{2,1,0:T(8,128)} %get-tuple-element.26), custom_call_target="InvertDiagBlocksLowerTriangular" | custom-call | tf_op jit(solution)/shard_map/jit(cholesky)/cholesky | solution.py:54
  201.9 1.7 convolution_dynamic-update-slice_fusion.1
  203.6 2.1 convolution_subtract_fusion.2
  205.7 13.2 %cholesky.255 = f32[128,128]{1,0:T(8,128)} custom-call(f32[128,128]{1,0:T(8,128)} %convolution_subtract_fusion.2), custom_call_target="Cholesky" | custom-call | tf_op jit(solution)/shard_map/jit(cholesky)/cholesky | solution.py:54
  218.9 1.5 select_reduce_fusion
  224.5 2.4 select_select_fusion
  227.5 13.6 %while.1 = (s32[]{:T(128)}, f32[512,512]{1,0:T(8,128)}, s32[4,2]{0,1:T(2,128)S(1)}, f32[4,128,128]{2,1,0:T(8,128)}, s32[]{:T(128)}) while((s32[]{:T(128)}, f32[512,512]{1,0:T(8,128)}, s32[4,2]{0,1:T(2,128)S(1)}, f32[4,128,128]{2,1,0:T(8,128)}, s32[]{:T(128)}) %tuple.33), condition=%wide.while_cond, body=%wide.while_body.sunk | while | flops 2 | bytes 132705 | solution.py:56
  228.1 2.8 bitcast_dynamic-update-slice_fusion.2
  231.5 2.8 bitcast_dynamic-update-slice_fusion.2
  234.9 2.8 bitcast_dynamic-update-slice_fusion.2
  238.3 2.8 bitcast_dynamic-update-slice_fusion.2
  241.1 40.7 %custom-call.37 = f32[4,128,128]{1,2,0:T(8,128)} custom-call(f32[4,128,128]{2,1,0:T(8,128)} %get-tuple-element.9), custom_call_target="InvertDiagBlocksLowerTriangular" | custom-call | tf_op jit(solution)/shard_map/jit(_solve_triangular)/triangular_solve | solution.py:56
  281.8 1.1 fusion.18
  286.6 1.1 convolution_subtract_fusion.8
  288.8 1.2 convolution_subtract_fusion.7
  290.0 1.1 fusion.31
  294.2 1.1 convolution_subtract_fusion.5
  296.3 1.2 convolution_subtract_fusion.4
  298.5 1.2 convolution_subtract_fusion.3
  300.3 32.9 %all_to_all.38 = f32[64,8,128]{2,1,0:T(8,128)} all-to-all(f32[64,8,128]{2,1,0:T(8,128)S(1)} %pad.10), channel_id=1, replica_groups=mesh['runs'=64,'terms'=8] {'runs'}, dimensions={0} | all-to-all | bytes 524288 | tf_op jit(solution)/shard_map/all_to_all | solution.py:10
  334.2 17.5 %all_to_all.39 = f32[64,8,128]{2,1,0:T(8,128)S(1)} all-to-all(f32[64,8,128]{2,1,0:T(8,128)S(1)} %broadcast_in_dim.16), channel_id=1, replica_groups=mesh['runs'=64,'terms'=8] {'runs'}, dimensions={0} | all-to-all | bytes 524288 | tf_op jit(solution)/shard_map/all_to_all | solution.py:10
  (57 shorter events, 24.0 us)
Async XLA Ops:
  0.6 2.0 copy-start
  2.6 31.3 %copy-start.6 = (f32[8,256]{1,0:T(8,128)S(1)}, f32[8,256]{1,0:T(8,128)}, u32[]{:S(2)}) copy-start(f32[8,256]{1,0:T(8,128)} %param.4) | copy-start | bytes 24580
  29.9 14.0 %all-to-all-start.1 = ((bf16[8,64,256]{2,1,0:T(8,128)(2,1)}), bf16[8,64,256]{2,1,0:T(8,128)(2,1)}, u32[]{:S(2)}, u32[]{:S(2)}) async-start(bf16[8,64,256]{2,1,0:T(8,128)(2,1)} %broadcast_in_dim.11), calls=%async_computation.1 | async-start | bytes 524288 | tf_op jit(solution)/shard_map/all_to_all | solution.py:10
  89.0 24.4 %all-to-all-start.4 = ((f32[8,64,640]{2,1,0:T(8,128)}), f32[8,64,640]{2,1,0:T(8,128)}, u32[]{:S(2)}, u32[]{:S(2)}) async-start(f32[8,64,640]{2,1,0:T(8,128)} %broadcast_in_dim.15), calls=%async_computation.4 | async-start | bytes 2621440 | tf_op jit(solution)/shard_map/all_to_all | solution.py:10
  120.0 1.0 copy-start.1
  148.4 0.7 copy-start.2
  203.6 82.3 %copy-start.4 = (f32[128,8]{1,0:T(8,128)S(1)}, f32[128,8]{1,0:T(8,128)}, u32[]{:S(2)}) copy-start(f32[128,8]{1,0:T(8,128)} %get-tuple-element.21) | copy-start | bytes 12292
  203.6 85.1 %copy-start.3 = (f32[128,8]{1,0:T(8,128)S(1)}, f32[128,8]{1,0:T(8,128)}, u32[]{:S(2)}) copy-start(f32[128,8]{1,0:T(8,128)} %get-tuple-element.22) | copy-start | bytes 12292
  299.7 52.8 %copy-start.5 = (f32[8,256]{1,0:T(8,128)}, f32[8,256]{1,0:T(8,128)S(1)}, u32[]{:S(2)}) copy-start(f32[8,256]{1,0:T(8,128)S(1)} %convolution_subtract_fusion.3) | copy-start | bytes 24580

commit v2 on v1

v2 whole, which is shorter than its diff:
```python
import functools

import jax
import jax.numpy as jnp
from jax import lax
from jax.experimental import pallas as pl
from jax.experimental.pallas import tpu as pltpu
from jax.sharding import PartitionSpec as P

LANES = 128
SUB = 8
BLOCK = 128
HIGH = lax.Precision.HIGHEST


def exchange(pieces, axis):
    return lax.all_to_all(pieces, axis, 0, 0)


def share(piece, axis):
    count = lax.axis_size(axis)
    return exchange(jnp.broadcast_to(piece[None], (count, *piece.shape)), axis)


def fetch_columns(design, indices):
    local_terms = design.shape[1]
    devices = lax.axis_size("terms")
    count = indices.shape[0]
    offset = lax.axis_index("terms") * local_terms
    positions = lax.broadcasted_iota(jnp.int32, (count, local_terms), 1)
    selector = (positions == (indices - offset)[:, None]).astype(jnp.bfloat16)
    partial_cols = lax.dot_general(
        selector, design, (((1,), (1,)), ((), ())), preferred_element_type=jnp.float32
    ).astype(jnp.bfloat16)
    pieces = exchange(partial_cols.reshape(devices, count // devices, -1), "terms")
    own = jnp.sum(pieces.astype(jnp.float32), axis=0).astype(jnp.bfloat16)
    return own, share(own, "terms").reshape(count, -1)


def spread(piece):
    return jnp.broadcast_to(piece, (SUB, LANES))


def dot(left, right):
    return jnp.dot(left, right, precision=HIGH, preferred_element_type=jnp.float32)


def invert_small(columns, sub):
    for i in range(SUB):
        pivot = 1.0 / spread(columns[i][i : i + 1, :])
        column, here = columns[i], sub == i
        after = []
        for j in range(SUB):
            if j == i:
                after.append(jnp.where(here, pivot, -column * pivot))
            else:
                factor = spread(columns[j][i : i + 1, :]) * pivot
                after.append(jnp.where(here, factor, columns[j] - column * factor))
        columns = after
    return columns


def invert_block(groups):
    lane = lax.broadcasted_iota(jnp.int32, (SUB, LANES), 1)
    sub = lax.broadcasted_iota(jnp.int32, (SUB, LANES), 0)
    groups = list(groups)
    count = len(groups)
    for k in range(count):
        first = SUB * k
        mine = groups[k]
        small = invert_small(
            [spread(mine[:, first + j : first + j + 1]) for j in range(SUB)], sub
        )
        inside = (lane >= first) & (lane < first + SUB)
        unit = jnp.where(lane - first == sub, 1.0, 0.0)
        mine = jnp.where(inside, unit, mine)
        top = small[0] * spread(mine[0:1, :])
        for j in range(1, SUB):
            top = top + small[j] * spread(mine[j : j + 1, :])
        rows = [spread(top[j : j + 1, :]) for j in range(SUB)]
        for step in range(1, count):
            g = (k + step) % count
            new = jnp.where(inside, 0.0, groups[g])
            for j in range(SUB):
                new = new - spread(groups[g][:, first + j : first + j + 1]) * rows[j]
            groups[g] = new
        groups[k] = top
    return groups


def finish_kernel(
    scale, system, responses, basis, design, residual, pieces, work, inverse, held, sem
):
    count = basis.shape[0]
    resp = responses.shape[0]
    blocks = count // BLOCK
    copy = pltpu.make_async_copy(design, held, sem)
    copy.start()
    work[...] = system[...]

    def eliminate(k):
        start, stop = k * BLOCK, (k + 1) * BLOCK
        lead = dot(inverse[...], work[start:stop, stop:])
        work[:, stop:] = work[:, stop:] - dot(work[:, start:stop], lead)
        work[start:stop, stop:] = lead

    def step(k, carry):
        start = pl.multiple_of(k * BLOCK, BLOCK)
        groups = [
            work[pl.ds(pl.multiple_of(start + SUB * g, SUB), SUB), pl.ds(start, BLOCK)]
            for g in range(BLOCK // SUB)
        ]
        for g, group in enumerate(invert_block(groups)):
            inverse[SUB * g : SUB * (g + 1), :] = group
        for known in range(blocks):
            pl.when(k == known)(functools.partial(eliminate, known))
        return carry

    lax.fori_loop(0, blocks, step, 0)
    fitted = lax.dot_general(
        work[:, count : count + LANES],
        basis[...].astype(jnp.float32),
        (((0,), (0,)), ((), ())),
        precision=HIGH,
        preferred_element_type=jnp.float32,
    )
    left = responses[...] - fitted[:resp, :]
    residual[...] = left
    rounded = left.astype(jnp.bfloat16)
    copy.wait()
    tiles = held.shape[1] // LANES
    for tile in range(0, tiles, 2):
        part = held[:, tile * LANES : (tile + 2) * LANES]
        both = jnp.dot(rounded, part, preferred_element_type=jnp.float32) * scale
        pieces[tile] = both[:, :LANES]
        pieces[tile + 1] = both[:, LANES:]
    pieces[tiles:] = jnp.zeros((pieces.shape[0] - tiles, resp, LANES), jnp.float32)


def finish(system, responses, basis, design, pieces, scale):
    resp, rows = responses.shape
    whole = pl.BlockSpec(memory_space=pltpu.VMEM)
    return pl.pallas_call(
        functools.partial(finish_kernel, scale),
        out_shape=(
            jax.ShapeDtypeStruct((resp, rows), jnp.float32),
            jax.ShapeDtypeStruct((pieces, resp, LANES), jnp.float32),
        ),
        in_specs=[whole, whole, whole, pl.BlockSpec(memory_space=pl.ANY)],
        out_specs=(whole, whole),
        scratch_shapes=[
            pltpu.VMEM(system.shape, jnp.float32),
            pltpu.VMEM((BLOCK, BLOCK), jnp.float32),
            pltpu.VMEM(design.shape, design.dtype),
            pltpu.SemaphoreType.DMA,
        ],
        compiler_params=pltpu.CompilerParams(vmem_limit_bytes=32 * 2**20),
        name="finish",
    )(system, responses, basis, design)


def local(design, responses, picks):
    run_devices = lax.axis_size("runs")
    resp, local_rows = responses.shape
    indices = picks.reshape(-1)
    count = indices.shape[0]
    own, basis = fetch_columns(design, indices)
    gram_rows = lax.dot_general(
        own, basis, (((1,), (1,)), ((), ())), preferred_element_type=jnp.float32
    )
    inner_rows = lax.dot_general(
        own.astype(jnp.float32), responses, (((1,), (1,)), ((), ())), precision=HIGH
    )
    rows = jnp.concatenate([gram_rows, inner_rows], axis=1)
    rows = jnp.pad(rows, ((0, 0), (0, -rows.shape[1] % LANES)))
    per = rows.shape[0] // run_devices
    summed = jnp.sum(exchange(rows.reshape(run_devices, per, -1), "runs"), axis=0)
    block = share(summed, "runs").reshape(rows.shape)
    system = share(block, "terms").reshape(count, -1)
    scale = float(local_rows * run_devices) ** -0.5
    residual, pieces = finish(system, responses, basis, design, run_devices, scale)
    total = jnp.sum(exchange(pieces, "runs"), axis=0)
    tiles = design.shape[1] // LANES
    gathered = share(total, "runs")[:tiles]
    correlations = gathered.transpose(1, 0, 2).reshape(resp, -1)
    return (residual, correlations)


def solution(mesh):
    placed = (P("runs", "terms"), P(None, "runs"), P())
    return jax.shard_map(
        local,
        mesh=mesh,
        in_specs=placed,
        out_specs=(P(None, "runs"), P(None, "terms")),
        check_vma=False,
    )
```

time: 359 us -> 186 us (0.52); the launches traced: 353 us -> 185 us
  other arithmetic: 136 us -> 1.86 us
  local copies, waits for them, and re-layouts: 29.7 us -> 1.81 us
  matrix products: 30.7 us -> 5.64 us
  blocking collectives: 115 us -> 139 us
  Pallas kernels: 0 us -> 22.6 us
  waiting for transfers between devices: 28.9 us -> 9.81 us
  starting transfers between devices: 8.76 us -> 4.04 us
    another operation x17 -> x0, other arithmetic: 130 us -> none  [the longest x14 86.7 us: local(): lower = jnp.linalg.cholesky(gram)]
    another operation x20 -> x0, matrix products: 25.2 us -> none  [the longest x6 10.2 us: local(): lower = jnp.linalg.cholesky(gram)]
    all_to_all x5 -> x6, blocking collectives: 115 us -> 139 us  [exchange(): return lax.all_to_all(pieces, axis, 0, 0)]
    pallas_call x0 -> x1, Pallas kernels: none -> 22.6 us  [finish(): pl.pallas_call(functools.partial(finish_kernel, scale), out_shape=(jax.Sh...]
    all_to_all x2 -> x1, waiting for transfers between devices: 28.9 us -> 9.81 us  [exchange(): return lax.all_to_all(pieces, axis, 0, 0)]
    another operation x18 -> x0, local copies, waits for them, and re-layouts: 17.6 us -> none
    unnamed x20 -> x6, local copies, waits for them, and re-layouts: 7.02 us -> 0.03 us
    all_to_all x2 -> x1, starting transfers between devices: 8.76 us -> 4.04 us  [exchange(): return lax.all_to_all(pieces, axis, 0, 0)]
  transfers between devices with their start and end apart: 2 -> 1, of which waited for: 2 -> 1; matrix products, arithmetic and copies ran while one was open for 0% -> 0% of each run, Pallas kernels for 0% -> 0%
where the time goes in v2:
time: 186 us; the launch traced here: 185 us
  blocking collectives  139 us (75%)
  Pallas kernels  22.6 us (12%)
  waiting for transfers between devices  9.81 us (5%)
  matrix products  5.64 us (3%)
  starting transfers between devices  4.04 us (2%)
  other arithmetic  1.86 us (1%)
    all_to_all x6, blocking collectives, exchange(): return lax.all_to_all(pieces, axis, 0, 0)  139 us
    pallas_call x1, Pallas kernels, finish(): pl.pallas_call(functools.partial(finish_kernel, scale), out_shape=(jax.Sh...  22.6 us
    all_to_all x1, waiting for transfers between devices, exchange(): return lax.all_to_all(pieces, axis, 0, 0)  9.81 us
    dot_general x1, matrix products, fetch_columns(): lax.dot_general(selector, design, (((1,), (1,)), ((), ())), preferred_ele...  4.34 us
    all_to_all x1, starting transfers between devices, exchange(): return lax.all_to_all(pieces, axis, 0, 0)  4.04 us
  transfers between devices with their start and end apart: 1, of which 1 were waited for; matrix products, arithmetic and copies ran while one was open for 0% of the time, Pallas kernels for 0%

profile of v2, /device:TPU:1, one launch (start us, length us, event | category | flops | bytes accessed | tf_op | source)
XLA Modules:
  0.0 185.2 jit_solution(8626483953553323537)
XLA Ops:
  0.6 0.7 subtract_bitcast_fusion
  1.3 0.0 copy-start.1
  1.3 4.3 %fusion.2 = bf16[512,256]{1,0:T(8,128)(2,1)S(1)} fusion(bf16[256,6656]{1,0:T(8,128)(2,1)} %design.1, s32[512]{0:T(512)S(1)} %bitcast.23), kind=kOutput, calls=%fused_computation.3 | convolution fusion | flops 1748369408 | bytes 3672064 | tf_op jit(solution)/shard_map/dot_general | solution.py:32
  5.7 23.1 %all_to_all.35 = bf16[8,64,256]{2,1,0:T(8,128)(2,1)S(1)} all-to-all(bf16[8,64,256]{2,1,0:T(8,128)(2,1)S(1)} %bitcast.22), channel_id=1, replica_groups=mesh['runs'=64,'terms'=8] {'terms'}, dimensions={0} | all-to-all | bytes 524288 | tf_op jit(solution)/shard_map/all_to_all | solution.py:17
  28.8 0.7 broadcast_in_dim.10
  29.5 4.0 %all-to-all-start.1 = ((bf16[8,64,256]{2,1,0:T(8,128)(2,1)}), bf16[8,64,256]{2,1,0:T(8,128)(2,1)}, u32[]{:S(2)}, u32[]{:S(2)}) async-start(bf16[8,64,256]{2,1,0:T(8,128)(2,1)} %broadcast_in_dim.10), calls=%async_computation.1 | async-start | bytes 524288 | tf_op jit(solution)/shard_map/all_to_all | solution.py:17
  33.6 0.0 copy-done.1
  33.6 0.0 copy-start
  33.6 0.2 fusion.5
  33.8 9.8 %all-to-all-done.1 = bf16[8,64,256]{2,1,0:T(8,128)(2,1)} async-done(((bf16[8,64,256]{2,1,0:T(8,128)(2,1)}), bf16[8,64,256]{2,1,0:T(8,128)(2,1)}, u32[]{:S(2)}, u32[]{:S(2)}) %all-to-all-start.1) | async-done | bytes 262176 | tf_op jit(solution)/shard_map/all_to_all | solution.py:17
  43.6 1.1 fusion.4
  44.8 0.2 copy.7
  44.9 26.0 %all_to_all.36 = f32[64,1,640]{2,1,0:T(1,128)} all-to-all(f32[64,1,640]{2,1,0:T(1,128)S(1)} %copy.7), channel_id=1, replica_groups=mesh['runs'=64,'terms'=8] {'runs'}, dimensions={0} | all-to-all | bytes 327680 | tf_op jit(solution)/shard_map/all_to_all | solution.py:17
  70.9 1.0 reduce_sum.31
  72.0 0.1 broadcast_in_dim.11
  72.1 15.4 %all_to_all.37 = f32[64,1,640]{2,1,0:T(1,128)S(1)} all-to-all(f32[64,1,640]{2,1,0:T(1,128)S(1)} %broadcast_in_dim.11), channel_id=1, replica_groups=mesh['runs'=64,'terms'=8] {'runs'}, dimensions={0} | all-to-all | bytes 327680 | tf_op jit(solution)/shard_map/all_to_all | solution.py:17
  87.5 0.1 broadcast_in_dim.13
  87.6 24.1 %all_to_all.38 = f32[8,64,640]{2,1,0:T(8,128)S(1)} all-to-all(f32[8,64,640]{2,1,0:T(8,128)S(1)} %broadcast_in_dim.13), channel_id=1, replica_groups=mesh['runs'=64,'terms'=8] {'terms'}, dimensions={0} | all-to-all | bytes 2621440 | tf_op jit(solution)/shard_map/all_to_all | solution.py:17
  111.7 0.0 copy-done
  111.7 22.6 %finish.1 = (f32[8,256]{1,0:T(8,128)}, f32[64,8,128]{2,1,0:T(8,128)S(1)}) custom-call(f32[512,640]{1,0:T(8,128)S(1)} %bitcast.20, f32[8,256]{1,0:T(8,128)S(1)} %copy-done.1, bf16[512,256]{1,0:T(8,128)(2,1)} %bitcast.1.basis, bf16[256,6656]{1,0:T(8,128)(2,1)S(1)} %copy-done), custom_call_target="tpu_custom_call" | custom-call | tf_op jit(solution)/shard_map/finish/pallas_call | solution.py:143
  134.3 32.6 %all_to_all.39 = f32[64,8,128]{2,1,0:T(8,128)S(1)} all-to-all(f32[64,8,128]{2,1,0:T(8,128)S(1)} %get-tuple-element.5), channel_id=1, replica_groups=mesh['runs'=64,'terms'=8] {'runs'}, dimensions={0} | all-to-all | bytes 524288 | tf_op jit(solution)/shard_map/all_to_all | solution.py:17
  166.9 0.1 reduce_sum.32
  167.0 17.5 %all_to_all.40 = f32[64,8,128]{2,1,0:T(8,128)S(1)} all-to-all(f32[64,8,128]{2,1,0:T(8,128)S(1)} %broadcast_in_dim.14), channel_id=1, replica_groups=mesh['runs'=64,'terms'=8] {'runs'}, dimensions={0} | all-to-all | bytes 524288 | tf_op jit(solution)/shard_map/all_to_all | solution.py:17
  184.5 0.7 slice_bitcast_fusion
  (5 shorter events, 0.1 us)
Async XLA Ops:
  1.3 32.3 %copy-start.1 = (f32[8,256]{1,0:T(8,128)S(1)}, f32[8,256]{1,0:T(8,128)}, u32[]{:S(2)}) copy-start(f32[8,256]{1,0:T(8,128)} %responses.1) | copy-start | bytes 24580
  29.5 14.0 %all-to-all-start.1 = ((bf16[8,64,256]{2,1,0:T(8,128)(2,1)}), bf16[8,64,256]{2,1,0:T(8,128)(2,1)}, u32[]{:S(2)}, u32[]{:S(2)}) async-start(bf16[8,64,256]{2,1,0:T(8,128)(2,1)} %broadcast_in_dim.10), calls=%async_computation.1 | async-start | bytes 524288 | tf_op jit(solution)/shard_map/all_to_all | solution.py:17
  33.6 78.1 %copy-start = (bf16[256,6656]{1,0:T(8,128)(2,1)S(1)}, bf16[256,6656]{1,0:T(8,128)(2,1)}, u32[]{:S(2)}) copy-start(bf16[256,6656]{1,0:T(8,128)(2,1)} %design.1) | copy-start | bytes 10223620

commit v3 on v2

v3 whole, which is shorter than its diff:
```python
import functools

import jax
import jax.numpy as jnp
from jax import lax
from jax.experimental import pallas as pl
from jax.experimental.pallas import tpu as pltpu
from jax.sharding import PartitionSpec as P

LANES = 128
SUB = 8
BLOCK = 128
SLOTS = 96
CHUNKS = 4
HIGH = lax.Precision.HIGHEST
F32 = jnp.float32
BF16 = jnp.bfloat16


def call(kernel, name, out_shape, in_specs, out_specs, scratch=(), **more):
    return pl.pallas_call(
        kernel,
        out_shape=out_shape,
        in_specs=in_specs,
        out_specs=out_specs,
        scratch_shapes=scratch,
        compiler_params=pltpu.CompilerParams(vmem_limit_bytes=32 * 2**20),
        name=name,
        **more,
    )


WHOLE = pl.BlockSpec(memory_space=pltpu.VMEM)
SCALAR = pl.BlockSpec(memory_space=pltpu.SMEM)


def exchange(pieces, axis, groups=None):
    return lax.all_to_all(pieces, axis, 0, 0, axis_index_groups=groups)


def owners(picks, devices, local_terms):
    count = picks.shape[1]
    first = lax.broadcasted_iota(jnp.int32, (devices, count), 0) * local_terms
    owned = ((picks >= first) & (picks < first + local_terms)).astype(F32)
    before = lax.broadcasted_iota(jnp.int32, (count, count), 0)
    after = lax.broadcasted_iota(jnp.int32, (count, count), 1)
    rank = jnp.dot(
        owned.astype(BF16),
        (before < after).astype(F32).astype(BF16),
        preferred_element_type=F32,
    )
    return owned, rank


def pack_kernel(local_terms, place, picks, design, packed, most, where, total):
    step = pl.program_id(0)
    devices = packed.shape[0]
    chunk = design.shape[1]

    @pl.when(step == 0)
    def _():
        owned, rank = owners(picks[...], devices, local_terms)
        counts = jnp.sum(owned, axis=1, keepdims=True)
        most[0] = jnp.max(counts).astype(jnp.int32)
        me = lax.broadcasted_iota(jnp.int32, owned.shape, 0) == place[0]
        mine = jnp.where(me, owned, 0.0)
        slot = jnp.sum(mine * rank, axis=0, keepdims=True)
        slot = slot - (place[1] * SLOTS).astype(F32)
        slot = jnp.where(jnp.sum(mine, axis=0, keepdims=True) > 0.0, slot, -1.0)
        slots = lax.broadcasted_iota(jnp.int32, (SLOTS, slot.shape[1]), 0).astype(F32)
        inner = (picks[...] - place[0] * local_terms + 1).astype(F32)
        held = jnp.where(slots == slot, inner, 0.0)
        where[...] = jnp.sum(held, axis=1, keepdims=True).astype(jnp.int32) - 1
        total[...] = jnp.zeros_like(total)

    columns = lax.broadcasted_iota(jnp.int32, (SLOTS, chunk), 1) + step * chunk
    chosen = (columns == where[...]).astype(F32).astype(BF16)
    total[...] += lax.dot_general(
        chosen, design[...], (((1,), (1,)), ((), ())), preferred_element_type=F32
    )

    @pl.when(step == CHUNKS - 1)
    def _():
        value = total[...].astype(BF16)
        for partner in range(devices):
            packed[partner] = value


def pack(place, picks, design, devices):
    rows, local_terms = design.shape
    chunk = local_terms // CHUNKS
    return call(
        functools.partial(pack_kernel, local_terms),
        "pack",
        (
            jax.ShapeDtypeStruct((devices, SLOTS, rows), BF16),
            jax.ShapeDtypeStruct((1,), jnp.int32),
        ),
        [SCALAR, WHOLE, pl.BlockSpec((rows, chunk), lambda step: (0, step))],
        (WHOLE, SCALAR),
        [pltpu.VMEM((SLOTS, 1), jnp.int32), pltpu.VMEM((SLOTS, rows), F32)],
        grid=(CHUNKS,),
    )(place, picks, design)


def upper_blocks(blocks):
    return [(i, j) for i in range(blocks) for j in range(i, blocks)]


def gram_kernel(local_terms, devices, place, picks, slots, responses, *refs):
    *prior, basis, keep, send, packed = refs
    owned, rank = owners(picks[...], devices, local_terms)
    first = lax.broadcasted_iota(jnp.int32, owned.shape, 0).astype(F32) * SLOTS
    slot = jnp.sum(owned * rank, axis=0, keepdims=True)
    slot = slot - (place[1] * SLOTS).astype(F32)
    target = slot + jnp.sum(owned * first, axis=0, keepdims=True)
    target = jnp.where((slot >= 0.0) & (slot < SLOTS), target, -1.0)
    count = picks.shape[1]
    lines = lax.broadcasted_iota(jnp.int32, (devices * SLOTS, count), 0).astype(F32)
    moved = (lines == target).astype(F32).astype(BF16)
    columns = lax.dot_general(
        moved, slots[...], (((0,), (0,)), ((), ())), preferred_element_type=F32
    )
    if prior:
        columns = columns + prior[0][...].astype(F32)
    columns = columns.astype(BF16)
    basis[...] = columns
    blocks = count // BLOCK
    row = 0
    for i in range(blocks):
        strip = lax.dot_general(
            columns[i * BLOCK : (i + 1) * BLOCK],
            columns[i * BLOCK :],
            (((1,), (1,)), ((), ())),
            preferred_element_type=F32,
        )
        for j in range(blocks - i):
            packed[row : row + BLOCK, :] = strip[:, j * BLOCK : (j + 1) * BLOCK]
            row += BLOCK
    resp = responses.shape[0]
    rest, parts = responses[...], []
    for _ in range(3):
        part = rest.astype(BF16).astype(F32)
        parts.append(part)
        rest = rest - part
    inner = lax.dot_general(
        jnp.concatenate(parts, axis=0).astype(BF16),
        columns,
        (((1,), (1,)), ((), ())),
        preferred_element_type=F32,
    )
    inner = inner[2 * resp :] + inner[resp : 2 * resp] + inner[:resp]
    for j in range(blocks):
        packed[row : row + resp, :] = inner[:, j * BLOCK : (j + 1) * BLOCK]
        row += resp
    packed[row:, :] = jnp.zeros((packed.shape[0] - row, LANES), F32)
    half = keep.shape[0]
    core = place[2]
    keep[...] = packed[pl.ds(pl.multiple_of(core * half, SUB), half), :]
    send[...] = packed[pl.ds(pl.multiple_of((1 - core) * half, SUB), half), :]


def gram(place, picks, slots, responses, prior, local_terms, half):
    devices, _, rows = slots.shape
    count = picks.shape[1]
    operands = (place, picks, slots.reshape(-1, rows), responses, *prior)
    return call(
        functools.partial(gram_kernel, local_terms, devices),
        "gram",
        (
            jax.ShapeDtypeStruct((count, rows), BF16),
            jax.ShapeDtypeStruct((half, LANES), F32),
            jax.ShapeDtypeStruct((half, LANES), F32),
        ),
        [SCALAR] + [WHOLE] * (len(operands) - 1),
        (WHOLE, WHOLE, WHOLE),
        [pltpu.VMEM((2 * half, LANES), F32)],
    )(*operands)


def spread(piece):
    return jnp.broadcast_to(piece, (SUB, LANES))


def dot(left, right):
    return jnp.dot(left, right, precision=HIGH, preferred_element_type=F32)


def dot_first(left, right):
    return lax.dot_general(
        left,
        right,
        (((0,), (0,)), ((), ())),
        precision=HIGH,
        preferred_element_type=F32,
    )


def invert_small(columns, sub):
    for i in range(SUB):
        pivot = 1.0 / spread(columns[i][i : i + 1, :])
        column, here = columns[i], sub == i
        after = []
        for j in range(SUB):
            if j == i:
                after.append(jnp.where(here, pivot, -column * pivot))
            else:
                factor = spread(columns[j][i : i + 1, :]) * pivot
                after.append(jnp.where(here, factor, columns[j] - column * factor))
        columns = after
    return columns


def invert_block(groups):
    lane = lax.broadcasted_iota(jnp.int32, (SUB, LANES), 1)
    sub = lax.broadcasted_iota(jnp.int32, (SUB, LANES), 0)
    groups = list(groups)
    count = len(groups)
    for k in range(count):
        first = SUB * k
        mine = groups[k]
        small = invert_small(
            [spread(mine[:, first + j : first + j + 1]) for j in range(SUB)], sub
        )
        inside = (lane >= first) & (lane < first + SUB)
        unit = jnp.where(lane - first == sub, 1.0, 0.0)
        mine = jnp.where(inside, unit, mine)
        top = small[0] * spread(mine[0:1, :])
        for j in range(1, SUB):
            top = top + small[j] * spread(mine[j : j + 1, :])
        rows = [spread(top[j : j + 1, :]) for j in range(SUB)]
        for step in range(1, count):
            g = (k + step) % count
            new = jnp.where(inside, 0.0, groups[g])
            for j in range(SUB):
                new = new - spread(groups[g][:, first + j : first + j + 1]) * rows[j]
            groups[g] = new
        groups[k] = top
    return groups


def finish_kernel(scale, place, *refs):
    mine, other, responses, basis, design, residual, pieces = refs[:7]
    packed, work, inverse, coef = refs[7:]
    half = mine.shape[0]
    count = basis.shape[0]
    resp = responses.shape[0]
    blocks = count // BLOCK
    core = place[2]
    packed[pl.ds(pl.multiple_of(core * half, SUB), half), :] = mine[...]
    packed[pl.ds(pl.multiple_of((1 - core) * half, SUB), half), :] = other[...]
    row = 0
    for i, j in upper_blocks(blocks):
        work[i * BLOCK : (i + 1) * BLOCK, j * BLOCK : (j + 1) * BLOCK] = packed[
            row : row + BLOCK, :
        ]
        row += BLOCK
    for i in range(blocks):
        inner = packed[row : row + resp, :]
        tall = jnp.concatenate([inner, jnp.zeros((BLOCK - resp, BLOCK), F32)], axis=0)
        work[i * BLOCK : (i + 1) * BLOCK, count:] = tall.T
        row += resp

    def eliminate(k):
        start, stop = k * BLOCK, (k + 1) * BLOCK
        right = work[start:stop, stop:]
        lead = dot(inverse[...], right)
        if stop < count:
            work[stop:, stop:] = work[stop:, stop:] - dot_first(
                right[:, : count - stop], lead
            )
        work[start:stop, stop:] = lead

    def step(k, carry):
        start = pl.multiple_of(k * BLOCK, BLOCK)
        groups = [
            work[pl.ds(pl.multiple_of(start + SUB * g, SUB), SUB), pl.ds(start, BLOCK)]
            for g in range(BLOCK // SUB)
        ]
        for g, group in enumerate(invert_block(groups)):
            inverse[SUB * g : SUB * (g + 1), :] = group
        for known in range(blocks):
            pl.when(k == known)(functools.partial(eliminate, known))
        return carry

    lax.fori_loop(0, blocks, step, 0)
    coef[count - BLOCK :, :] = work[count - BLOCK :, count:]
    for k in reversed(range(blocks - 1)):
        start, stop = k * BLOCK, (k + 1) * BLOCK
        coef[start:stop, :] = work[start:stop, count:] - dot(
            work[start:stop, stop:count], coef[stop:, :]
        )
    fitted = dot_first(coef[...], basis[...].astype(F32))
    left = responses[...] - fitted[:resp, :]
    residual[...] = left
    rounded = left.astype(BF16)
    tiles = design.shape[1] // LANES
    for tile in range(0, tiles, 2):
        part = design[:, tile * LANES : (tile + 2) * LANES]
        both = jnp.dot(rounded, part, preferred_element_type=F32) * scale
        pieces[tile] = both[:, :LANES]
        pieces[tile + 1] = both[:, LANES:]
    pieces[tiles:] = jnp.zeros((pieces.shape[0] - tiles, resp, LANES), F32)


def finish(place, mine, other, responses, basis, design, pieces, scale):
    resp, rows = responses.shape
    count = basis.shape[0]
    return call(
        functools.partial(finish_kernel, scale),
        "finish",
        (
            jax.ShapeDtypeStruct((resp, rows), F32),
            jax.ShapeDtypeStruct((pieces, resp, LANES), F32),
        ),
        [SCALAR] + [WHOLE] * 5,
        (WHOLE, WHOLE),
        [
            pltpu.VMEM((2 * mine.shape[0], LANES), F32),
            pltpu.VMEM((count, count + LANES), F32),
            pltpu.VMEM((BLOCK, BLOCK), F32),
            pltpu.VMEM((count, LANES), F32),
        ],
    )(place, mine, other, responses, basis, design)


def summed_everywhere(pieces, axis, groups=None):
    total = jnp.sum(exchange(pieces, axis, groups), axis=0)
    return exchange(jnp.broadcast_to(total[None], pieces.shape), axis, groups)


def local(design, responses, picks):
    run_devices, term_devices = lax.axis_size("runs"), lax.axis_size("terms")
    resp, local_rows = responses.shape
    local_terms = design.shape[1]
    chips = run_devices // 2
    core = lax.axis_index("runs") % 2
    place = [lax.axis_index("terms"), 0, core]
    picks = picks.reshape(1, -1)
    count = picks.shape[1]

    blocks = count // BLOCK
    lines = len(upper_blocks(blocks)) * BLOCK + blocks * resp
    lines += -lines % (run_devices * SUB)
    half = lines // 2

    def fetch(turn):
        at = jnp.stack([jnp.int32(v) for v in (place[0], turn, place[2])])
        packed, most = pack(at, picks, design, term_devices)
        return at, exchange(packed, "terms"), most

    at, slots, most = fetch(0)
    state = gram(at, picks, slots, responses, (), local_terms, half)

    def another(carry):
        turn, basis, _, _ = carry
        where, more, _ = fetch(turn)
        return turn + 1, *gram(
            where, picks, more, responses, (basis,), local_terms, half
        )

    _, basis, keep, send = lax.while_loop(
        lambda carry: carry[0] * SLOTS < most[0], another, (jnp.int32(1), *state)
    )

    swap = [(i, i ^ 1) for i in range(run_devices)]
    sides = [list(range(side, run_devices, 2)) for side in range(2)]
    part = keep + lax.ppermute(send, "runs", swap)
    mine = summed_everywhere(part.reshape(chips, -1, LANES), "runs", sides)
    mine = mine.reshape(half, LANES)
    other = lax.ppermute(mine, "runs", swap)

    scale = float(local_rows * run_devices) ** -0.5
    residual, pieces = finish(
        at, mine, other, responses, basis, design, run_devices, scale
    )
    gathered = summed_everywhere(pieces, "runs")[: local_terms // LANES]
    correlations = gathered.transpose(1, 0, 2).reshape(resp, -1)
    return (residual, correlations)


def solution(mesh):
    placed = (P("runs", "terms"), P(None, "runs"), P())
    return jax.shard_map(
        local,
        mesh=mesh,
        in_specs=placed,
        out_specs=(P(None, "runs"), P(None, "terms")),
        check_vma=False,
    )
```

time: 186 us -> 151 us (0.81)
  blocking collectives: 139 us -> 76.8 us
  starting transfers between devices: 4.04 us -> 25.5 us
  Pallas kernels: 22.6 us -> 29.3 us
  matrix products: 5.64 us -> 0 us
  waiting for transfers between devices: 9.81 us -> 13.5 us
    all_to_all x6 -> x4, blocking collectives: 139 us -> 76.8 us  [exchange(): return lax.all_to_all(pieces, axis, 0, 0, axis_index_groups=groups)]
    ppermute x0 -> x2, starting transfers between devices: none -> 12.2 us  [the longest x1 7.22 us: local(): part = keep + lax.ppermute(send, 'runs', swap)]
    all_to_all x1, starting transfers between devices: 4.04 us -> 13.3 us  [exchange(): return lax.all_to_all(pieces, axis, 0, 0, axis_index_groups=groups)]
    pallas_call x1 -> x3, Pallas kernels: 22.6 us -> 29.3 us  [the longest x1 21.9 us: finish(): call(functools.partial(finish_kernel, scale), 'finish', (jax.ShapeDtypeSt...]
    dot_general x3 -> x0, matrix products: 5.64 us -> none  [the longest x1 4.34 us: fetch_columns(): lax.dot_general(selector, design, (((1,), (1,)), ((), ())), preferred_ele...]
    ppermute x0 -> x2, waiting for transfers between devices: none -> 2.87 us  [the longest x1 1.54 us: local(): part = keep + lax.ppermute(send, 'runs', swap)]
  transfers between devices with their start and end apart: 1 -> 3, of which waited for: 1 -> 3; matrix products, arithmetic and copies ran while one was open for 0% -> 0% of each run, Pallas kernels for 0% -> 0%
where the time goes in v3:
time: 151 us; the launch traced here: 150 us
  blocking collectives  76.8 us (51%)
  Pallas kernels  29.3 us (19%)
  starting transfers between devices  25.5 us (17%)
  waiting for transfers between devices  13.5 us (9%)
  other arithmetic  2.24 us (1%)
    all_to_all x4, blocking collectives, exchange(): return lax.all_to_all(pieces, axis, 0, 0, axis_index_groups=groups)  76.8 us
    pallas_call x1, Pallas kernels, finish(): call(functools.partial(finish_kernel, scale), 'finish', (jax.ShapeDtypeSt...  21.9 us
    all_to_all x1, starting transfers between devices, exchange(): return lax.all_to_all(pieces, axis, 0, 0, axis_index_groups=groups)  13.3 us
    all_to_all x1, waiting for transfers between devices, exchange(): return lax.all_to_all(pieces, axis, 0, 0, axis_index_groups=groups)  10.6 us
    ppermute x1, starting transfers between devices, local(): part = keep + lax.ppermute(send, 'runs', swap)  7.22 us
    ppermute x1, starting transfers between devices, local(): other = lax.ppermute(mine, 'runs', swap)  4.97 us
    pallas_call x1, Pallas kernels, pack(): call(functools.partial(pack_kernel, local_terms), 'pack', (jax.ShapeDtype...  4.75 us
  transfers between devices with their start and end apart: 3, of which 3 were waited for; matrix products, arithmetic and copies ran while one was open for 0% of the time, Pallas kernels for 0%

profile of v3, /device:TPU:1, one launch (start us, length us, event | category | flops | bytes accessed | tf_op | source)
XLA Modules:
  0.0 150.1 jit_solution(6336109630862611067)
XLA Ops:
  0.6 0.0 copy-start.1
  0.6 0.7 copy.5
  1.3 0.1 pad_add_fusion.1.place
  1.4 4.8 %pack.2 = (bf16[8,96,256]{2,1,0:T(8,128)(2,1)}, s32[1]{0:T(128)}) custom-call(s32[3]{0:T(128)S(1)} %pad_add_fusion.1.place, s32[1,512]{1,0:T(1,128)S(1)} %bitcast.31, bf16[256,6656]{1,0:T(8,128)(2,1)} %refs_4_.1), custom_call_target="tpu_custom_call" | custom-call | tf_op jit(solution)/shard_map/pack/pallas_call | solution.py:92
  6.2 13.3 %all-to-all-start.1 = ((bf16[8,96,256]{2,1,0:T(8,128)(2,1)}), bf16[8,96,256]{2,1,0:T(8,128)(2,1)S(1)}, u32[]{:S(2)}, u32[]{:S(2)}) async-start(bf16[8,96,256]{2,1,0:T(8,128)(2,1)} %get-tuple-element.66), calls=%async_computation.1 | async-start | bytes 786432 | tf_op jit(solution)/shard_map/all_to_all | solution.py:38
  19.5 10.6 %all-to-all-done.1 = bf16[8,96,256]{2,1,0:T(8,128)(2,1)S(1)} async-done(((bf16[8,96,256]{2,1,0:T(8,128)(2,1)}), bf16[8,96,256]{2,1,0:T(8,128)(2,1)S(1)}, u32[]{:S(2)}, u32[]{:S(2)}) %all-to-all-start.1) | async-done | bytes 393248 | tf_op jit(solution)/shard_map/all_to_all | solution.py:38
  30.1 0.0 copy-done.1
  30.1 2.6 %gram.2 = (bf16[512,256]{1,0:T(8,128)(2,1)}, f32[768,128]{1,0:T(8,128)}, f32[768,128]{1,0:T(8,128)}) custom-call(s32[3]{0:T(128)S(1)} %pad_add_fusion.1.place, s32[1,512]{1,0:T(1,128)S(1)} %bitcast.32, bf16[768,256]{1,0:T(8,128)(2,1)S(1)} %bitcast.27, f32[8,256]{1,0:T(8,128)S(1)} %copy-done.1), custom_call_target="tpu_custom_call" | custom-call | tf_op jit(solution)/shard_map/gram/pallas_call | solution.py:167
  32.7 0.6 while.14
  33.3 0.0 copy-start
  33.3 7.2 %collective-permute-start = (f32[768,128]{1,0:T(8,128)}, f32[768,128]{1,0:T(8,128)S(1)}, u32[]{:S(2)}, u32[]{:S(2)}) collective-permute-start(f32[768,128]{1,0:T(8,128)} %get-tuple-element.72), channel_id=1, source_target_pairs={{0,8},{8,0},{16,24},{24,16},{32,40},{40,32},{48,56},{56,48},{64,72... | collective-permute-start | bytes 1179656 | tf_op jit(solution)/shard_map/ppermute | solution.py:368
  40.6 1.5 %collective-permute-done = f32[768,128]{1,0:T(8,128)S(1)} collective-permute-done((f32[768,128]{1,0:T(8,128)}, f32[768,128]{1,0:T(8,128)S(1)}, u32[]{:S(2)}, u32[]{:S(2)}) %collective-permute-start) | collective-permute-done | bytes 393248 | tf_op jit(solution)/shard_map/ppermute | solution.py:368
  42.1 1.1 add.11
  43.2 22.6 %all_to_all.31 = f32[32,24,128]{2,1,0:T(8,128)} all-to-all(f32[32,24,128]{2,1,0:T(8,128)S(1)} %bitcast.30), channel_id=1, replica_groups={{0,16,32,48,64,80,96,112,128,144,160,176,192,208,224,240,256,272,288,30..., dimensions={0} | all-to-all | bytes 786432 | tf_op jit(solution)/shard_map/all_to_all | solution.py:38
  65.8 1.0 reduce_sum.18
  66.9 19.0 %all_to_all.32 = f32[32,24,128]{2,1,0:T(8,128)S(1)} all-to-all(f32[32,24,128]{2,1,0:T(8,128)S(1)} %broadcast_in_dim.4), channel_id=1, replica_groups={{0,16,32,48,64,80,96,112,128,144,160,176,192,208,224,240,256,272,288,30..., dimensions={0} | all-to-all | bytes 786432 | tf_op jit(solution)/shard_map/all_to_all | solution.py:38
  85.9 5.0 %collective-permute-start.1 = (f32[768,128]{1,0:T(8,128)S(1)}, f32[768,128]{1,0:T(8,128)S(1)}, u32[]{:S(2)}, u32[]{:S(2)}) collective-permute-start(f32[768,128]{1,0:T(8,128)S(1)} %bitcast.28), channel_id=1, source_target_pairs={{0,8},{8,0},{16,24},{24,16},{32,40},{40,32},{48,56},{56,48},{64,72... | collective-permute-start | bytes 1179656 | tf_op jit(solution)/shard_map/ppermute | solution.py:371
  90.9 1.3 collective-permute-done.1.refs_1_
  92.2 0.0 copy-done
  92.2 21.9 %finish.1 = (f32[8,256]{1,0:T(8,128)}, f32[64,8,128]{2,1,0:T(8,128)S(1)}) custom-call(s32[3]{0:T(128)S(1)} %pad_add_fusion.1.place, f32[768,128]{1,0:T(8,128)S(1)} %bitcast.29, f32[768,128]{1,0:T(8,128)S(1)} %collective-permute-done.1.refs_1_, f32[8,256]{1,0:T(8,128)S(1)} %get-tuple-element.200, bf16[512,256]{1,0:T(8,128)(2,1)} %get-tuple-element.73.refs_3_, ...), custom_call_target="tpu_custom_call" | custom-call | tf_op jit(solution)/shard_map/finish/pallas_call | solution.py:309
  114.1 17.7 %all_to_all.33 = f32[64,8,128]{2,1,0:T(8,128)S(1)} all-to-all(f32[64,8,128]{2,1,0:T(8,128)S(1)} %get-tuple-element.75), channel_id=1, replica_groups=mesh['runs'=64,'terms'=8] {'runs'}, dimensions={0} | all-to-all | bytes 524288 | tf_op jit(solution)/shard_map/all_to_all | solution.py:38
  131.8 0.1 reduce_sum.19
  131.9 17.5 %all_to_all.34 = f32[64,8,128]{2,1,0:T(8,128)S(1)} all-to-all(f32[64,8,128]{2,1,0:T(8,128)S(1)} %broadcast_in_dim.5), channel_id=1, replica_groups=mesh['runs'=64,'terms'=8] {'runs'}, dimensions={0} | all-to-all | bytes 524288 | tf_op jit(solution)/shard_map/all_to_all | solution.py:38
  149.4 0.7 slice_bitcast_fusion
  (2 shorter events, 0.0 us)
Async XLA Ops:
  0.6 29.4 %copy-start.1 = (f32[8,256]{1,0:T(8,128)S(1)}, f32[8,256]{1,0:T(8,128)}, u32[]{:S(2)}) copy-start(f32[8,256]{1,0:T(8,128)} %refs_2_.1) | copy-start | bytes 24580
  6.2 23.9 %all-to-all-start.1 = ((bf16[8,96,256]{2,1,0:T(8,128)(2,1)}), bf16[8,96,256]{2,1,0:T(8,128)(2,1)S(1)}, u32[]{:S(2)}, u32[]{:S(2)}) async-start(bf16[8,96,256]{2,1,0:T(8,128)(2,1)} %get-tuple-element.66), calls=%async_computation.1 | async-start | bytes 786432 | tf_op jit(solution)/shard_map/all_to_all | solution.py:38
  33.3 58.9 %copy-start = (bf16[256,6656]{1,0:T(8,128)(2,1)S(1)}, bf16[256,6656]{1,0:T(8,128)(2,1)}, u32[]{:S(2)}) copy-start(bf16[256,6656]{1,0:T(8,128)(2,1)} %get-tuple-element.199) | copy-start | bytes 10223620
  33.3 8.8 %collective-permute-start = (f32[768,128]{1,0:T(8,128)}, f32[768,128]{1,0:T(8,128)S(1)}, u32[]{:S(2)}, u32[]{:S(2)}) collective-permute-start(f32[768,128]{1,0:T(8,128)} %get-tuple-element.72), channel_id=1, source_target_pairs={{0,8},{8,0},{16,24},{24,16},{32,40},{40,32},{48,56},{56,48},{64,72... | collective-permute-start | bytes 1179656 | tf_op jit(solution)/shard_map/ppermute | solution.py:368
  85.9 6.3 %collective-permute-start.1 = (f32[768,128]{1,0:T(8,128)S(1)}, f32[768,128]{1,0:T(8,128)S(1)}, u32[]{:S(2)}, u32[]{:S(2)}) collective-permute-start(f32[768,128]{1,0:T(8,128)S(1)} %bitcast.28), channel_id=1, source_target_pairs={{0,8},{8,0},{16,24},{24,16},{32,40},{40,32},{48,56},{56,48},{64,72... | collective-permute-start | bytes 1179656 | tf_op jit(solution)/shard_map/ppermute | solution.py:371

commit v4 on v3

v4 whole, which is shorter than its diff:
```python
import functools

import jax
import jax.numpy as jnp
from jax import lax
from jax.experimental import pallas as pl
from jax.experimental.pallas import tpu as pltpu
from jax.sharding import PartitionSpec as P

LANES = 128
SUB = 8
BLOCK = 128
SLOTS = 96
CHUNKS = 4
HALVES = (
    ((0, 128, 0, 512), (128, 256, 128, 256), (128, 192, 256, 384)),
    (
        (0, 128, 0, 128),
        (192, 256, 256, 384),
        (128, 256, 384, 512),
        (256, 384, 256, 512),
        (384, 512, 384, 512),
    ),
)
HIGH = lax.Precision.HIGHEST
F32 = jnp.float32
BF16 = jnp.bfloat16


def call(kernel, name, out_shape, in_specs, out_specs, scratch=(), **more):
    return pl.pallas_call(
        kernel,
        out_shape=out_shape,
        in_specs=in_specs,
        out_specs=out_specs,
        scratch_shapes=scratch,
        compiler_params=pltpu.CompilerParams(vmem_limit_bytes=32 * 2**20),
        name=name,
        **more,
    )


WHOLE = pl.BlockSpec(memory_space=pltpu.VMEM)
SCALAR = pl.BlockSpec(memory_space=pltpu.SMEM)


def exchange(pieces, axis, groups=None):
    return lax.all_to_all(pieces, axis, 0, 0, axis_index_groups=groups)


def as_line(picks):
    return jnp.concatenate([picks[i : i + 1, :] for i in range(picks.shape[0])], axis=1)


def owners(picks, devices, local_terms):
    count = picks.shape[1]
    first = lax.broadcasted_iota(jnp.int32, (devices, count), 0) * local_terms
    owned = ((picks >= first) & (picks < first + local_terms)).astype(F32)
    before = lax.broadcasted_iota(jnp.int32, (count, count), 0)
    after = lax.broadcasted_iota(jnp.int32, (count, count), 1)
    rank = jnp.dot(
        owned.astype(BF16),
        (before < after).astype(F32).astype(BF16),
        preferred_element_type=F32,
    )
    return owned, rank


def pack_kernel(place, picks, design, packed, most, held, where, sems):
    devices = packed.shape[0]
    local_terms = design.shape[1]
    chunk = local_terms // CHUNKS

    def part(step):
        columns = pl.ds(step * chunk, chunk)
        return pltpu.make_async_copy(
            design.at[:, columns], held.at[:, columns], sems.at[step]
        )

    for step in range(CHUNKS):
        part(step).start()
    line = as_line(picks)
    owned, rank = owners(line, devices, local_terms)
    counts = jnp.sum(owned, axis=1, keepdims=True)
    most[0] = jnp.max(counts).astype(jnp.int32)
    me = lax.broadcasted_iota(jnp.int32, owned.shape, 0) == place[0]
    mine = jnp.where(me, owned, 0.0)
    slot = jnp.sum(mine * rank, axis=0, keepdims=True)
    slot = slot - (place[1] * SLOTS).astype(F32)
    slot = jnp.where(jnp.sum(mine, axis=0, keepdims=True) > 0.0, slot, -1.0)
    slots = lax.broadcasted_iota(jnp.int32, (SLOTS, slot.shape[1]), 0).astype(F32)
    inner = (line - place[0] * local_terms + 1).astype(F32)
    inner = jnp.where(slots == slot, inner, 0.0)
    where[...] = jnp.sum(inner, axis=1, keepdims=True).astype(jnp.int32) - 1
    total = jnp.zeros((SLOTS, design.shape[0]), F32)
    for step in range(CHUNKS):
        columns = lax.broadcasted_iota(jnp.int32, (SLOTS, chunk), 1) + step * chunk
        chosen = (columns == where[...]).astype(F32).astype(BF16)
        part(step).wait()
        total = total + lax.dot_general(
            chosen,
            held[:, step * chunk : (step + 1) * chunk],
            (((1,), (1,)), ((), ())),
            preferred_element_type=F32,
        )
    value = total.astype(BF16)
    for partner in range(devices):
        packed[partner] = value


def pack(place, picks, design, devices):
    rows = design.shape[0]
    return call(
        pack_kernel,
        "pack",
        (
            jax.ShapeDtypeStruct((devices, SLOTS, rows), BF16),
            jax.ShapeDtypeStruct((1,), jnp.int32),
        ),
        [SCALAR, WHOLE, pl.BlockSpec(memory_space=pltpu.HBM)],
        (WHOLE, SCALAR),
        [
            pltpu.VMEM(design.shape, design.dtype),
            pltpu.VMEM((SLOTS, 1), jnp.int32),
            pltpu.SemaphoreType.DMA((CHUNKS,)),
        ],
    )(place, picks, design)


def gram_kernel(local_terms, devices, has_prior, place, picks, slots, other, *refs):
    own = other.shape[0] != refs[-1].shape[0]
    prior = refs[0] if has_prior else None
    basis, sums = refs[-2:]
    owned, rank = owners(as_line(picks), devices, local_terms)
    first = lax.broadcasted_iota(jnp.int32, owned.shape, 0).astype(F32) * SLOTS
    slot = jnp.sum(owned * rank, axis=0, keepdims=True)
    slot = slot - (place[1] * SLOTS).astype(F32)
    target = slot + jnp.sum(owned * first, axis=0, keepdims=True)
    target = jnp.where((slot >= 0.0) & (slot < SLOTS), target, -1.0)
    count = target.shape[1]
    lines = lax.broadcasted_iota(jnp.int32, (devices * SLOTS, count), 0).astype(F32)
    moved = (lines == target).astype(F32).astype(BF16)
    columns = lax.dot_general(
        moved, slots[...], (((0,), (0,)), ((), ())), preferred_element_type=F32
    )
    if has_prior:
        columns = columns + prior[...].astype(F32)
    basis[...] = columns.astype(BF16)

    def fill(side):
        row = 0
        for top, bottom, start, stop in HALVES[side]:
            strip = lax.dot_general(
                basis[top:bottom],
                basis[start:stop],
                (((1,), (1,)), ((), ())),
                preferred_element_type=F32,
            )
            for j in range(0, stop - start, BLOCK):
                after = row + bottom - top
                piece = strip[:, j : j + BLOCK]
                sums[row:after, :] = piece if own else piece + other[row:after, :]
                row = after
        if not own:
            sums[row:, :] = other[row:, :]
            return
        resp = other.shape[0]
        rest, parts = other[...], []
        for _ in range(3):
            part = rest.astype(BF16).astype(F32)
            parts.append(part)
            rest = rest - part
        inner = lax.dot_general(
            jnp.concatenate(parts, axis=0).astype(BF16),
            basis[...],
            (((1,), (1,)), ((), ())),
            preferred_element_type=F32,
        )
        inner = inner[2 * resp :] + inner[resp : 2 * resp] + inner[:resp]
        for j in range(0, count, BLOCK):
            sums[row : row + resp, :] = inner[:, j : j + BLOCK]
            row += resp
        sums[row:, :] = jnp.zeros((sums.shape[0] - row, LANES), F32)

    for side in range(2):
        pl.when(place[2] == side)(functools.partial(fill, side))


def gram(place, picks, slots, other, local_terms, half, prior=None):
    devices, _, rows = slots.shape
    count = picks.size
    extra = () if prior is None else (prior,)
    operands = (place, picks, slots.reshape(-1, rows), other, *extra)
    return call(
        functools.partial(gram_kernel, local_terms, devices, prior is not None),
        "gram",
        (
            jax.ShapeDtypeStruct((count, rows), BF16),
            jax.ShapeDtypeStruct((half, LANES), F32),
        ),
        [SCALAR] + [WHOLE] * (len(operands) - 1),
        (WHOLE, WHOLE),
        cost_estimate=pl.CostEstimate(
            flops=2 * count * rows * (devices * SLOTS + count),
            bytes_accessed=2 * count * rows,
            transcendentals=0,
        ),
    )(*operands)


def total_kernel(pieces, totals):
    total = jnp.sum(pieces[...], axis=0)
    for piece in range(totals.shape[0]):
        totals[piece] = total


def totals(pieces):
    shape = jax.ShapeDtypeStruct(pieces.shape, pieces.dtype)
    return call(total_kernel, "totals", shape, [WHOLE], WHOLE)(pieces)


def spread(piece):
    return jnp.broadcast_to(piece, (SUB, LANES))


def dot(left, right):
    return jnp.dot(left, right, precision=HIGH, preferred_element_type=F32)


def dot_first(left, right):
    return lax.dot_general(
        left,
        right,
        (((0,), (0,)), ((), ())),
        precision=HIGH,
        preferred_element_type=F32,
    )


def across(group, lane):
    index = jnp.full((SUB, LANES), lane, jnp.int32)
    return jnp.take_along_axis(group, index, axis=1, mode="promise_in_bounds")


def invert_small(columns, sub):
    for i in range(SUB):
        pivot = 1.0 / spread(columns[i][i : i + 1, :])
        column, here = columns[i], sub == i
        after = []
        for j in range(SUB):
            if j == i:
                after.append(jnp.where(here, pivot, -column * pivot))
            else:
                factor = spread(columns[j][i : i + 1, :]) * pivot
                after.append(jnp.where(here, factor, columns[j] - column * factor))
        columns = after
    return columns


def invert_block(groups):
    lane = lax.broadcasted_iota(jnp.int32, (SUB, LANES), 1)
    sub = lax.broadcasted_iota(jnp.int32, (SUB, LANES), 0)
    groups = list(groups)
    count = len(groups)
    for k in range(count):
        first = SUB * k
        mine = groups[k]
        small = invert_small(
            [across(mine, first + j) for j in range(SUB)], sub
        )
        inside = (lane >= first) & (lane < first + SUB)
        unit = jnp.where(lane - first == sub, 1.0, 0.0)
        mine = jnp.where(inside, unit, mine)
        top = small[0] * spread(mine[0:1, :])
        for j in range(1, SUB):
            top = top + small[j] * spread(mine[j : j + 1, :])
        rows = [spread(top[j : j + 1, :]) for j in range(SUB)]
        for step in range(1, count):
            g = (k + step) % count
            new = jnp.where(inside, 0.0, groups[g])
            for j in range(SUB):
                new = new - across(groups[g], first + j) * rows[j]
            groups[g] = new
        groups[k] = top
    return groups


def groups_of(block):
    return [block[SUB * g : SUB * (g + 1), :] for g in range(BLOCK // SUB)]


def first_kernel(sums, inverse):
    for g, group in enumerate(invert_block(groups_of(sums[:BLOCK, :]))):
        inverse[SUB * g : SUB * (g + 1), :] = group


def first_inverse(sums):
    return call(
        first_kernel,
        "first_inverse",
        jax.ShapeDtypeStruct((BLOCK, BLOCK), F32),
        [WHOLE],
        WHOLE,
        cost_estimate=pl.CostEstimate(
            flops=2 * 10**9, bytes_accessed=10**5, transcendentals=0
        ),
    )(sums)


def finish_kernel(scale, place, *refs):
    mine, other, known_inverse, responses, basis, design, residual, pieces = refs[:8]
    packed, work, inverse, coef = refs[8:]
    half = mine.shape[0]
    count = basis.shape[0]
    resp = responses.shape[0]
    blocks = count // BLOCK
    core = place[2]
    packed[pl.ds(pl.multiple_of(core * half, SUB), half), :] = mine[...]
    packed[pl.ds(pl.multiple_of((1 - core) * half, SUB), half), :] = other[...]
    ends = []
    for side in range(2):
        row = side * half
        for top, bottom, start, stop in HALVES[side]:
            for j in range(start, stop, BLOCK):
                after = row + bottom - top
                work[top:bottom, j : j + BLOCK] = packed[row:after, :]
                row = after
        ends.append(row)
    for i in range(blocks):
        inner = [packed[end + i * resp : end + (i + 1) * resp, :] for end in ends]
        tall = [inner[0] + inner[1], jnp.zeros((BLOCK - resp, BLOCK), F32)]
        work[i * BLOCK : (i + 1) * BLOCK, count:] = jnp.concatenate(tall, axis=0).T

    def eliminate(k):
        start, stop = k * BLOCK, (k + 1) * BLOCK
        right = work[start:stop, stop:]
        lead = dot(inverse[...], right)
        if stop < count:
            work[stop:, stop:] = work[stop:, stop:] - dot_first(
                right[:, : count - stop], lead
            )
        work[start:stop, stop:] = lead

    def step(k, carry):
        start = pl.multiple_of(k * BLOCK, BLOCK)
        groups = [
            work[pl.ds(pl.multiple_of(start + SUB * g, SUB), SUB), pl.ds(start, BLOCK)]
            for g in range(BLOCK // SUB)
        ]
        for g, group in enumerate(invert_block(groups)):
            inverse[SUB * g : SUB * (g + 1), :] = group
        for known in range(1, blocks):
            pl.when(k == known)(functools.partial(eliminate, known))
        return carry

    inverse[...] = known_inverse[...]
    eliminate(0)
    lax.fori_loop(1, blocks, step, 0)
    coef[count - BLOCK :, :] = work[count - BLOCK :, count:]
    for k in reversed(range(blocks - 1)):
        start, stop = k * BLOCK, (k + 1) * BLOCK
        coef[start:stop, :] = work[start:stop, count:] - dot(
            work[start:stop, stop:count], coef[stop:, :]
        )
    fitted = dot_first(coef[...], basis[...].astype(F32))
    left = responses[...] - fitted[:resp, :]
    residual[...] = left
    rounded = left.astype(BF16)
    tiles = design.shape[1] // LANES
    for tile in range(0, tiles, 2):
        part = design[:, tile * LANES : (tile + 2) * LANES]
        both = jnp.dot(rounded, part, preferred_element_type=F32) * scale
        pieces[tile] = both[:, :LANES]
        pieces[tile + 1] = both[:, LANES:]
    pieces[tiles:] = jnp.zeros((pieces.shape[0] - tiles, resp, LANES), F32)


def finish(place, mine, other, inverse, responses, basis, design, pieces, scale):
    resp, rows = responses.shape
    count = basis.shape[0]
    return call(
        functools.partial(finish_kernel, scale),
        "finish",
        (
            jax.ShapeDtypeStruct((resp, rows), F32),
            jax.ShapeDtypeStruct((pieces, resp, LANES), F32),
        ),
        [SCALAR] + [WHOLE] * 6,
        (WHOLE, WHOLE),
        [
            pltpu.VMEM((2 * mine.shape[0], LANES), F32),
            pltpu.VMEM((count, count + LANES), F32),
            pltpu.VMEM((BLOCK, BLOCK), F32),
            pltpu.VMEM((count, LANES), F32),
        ],
    )(place, mine, other, inverse, responses, basis, design)


def summed_everywhere(pieces, axis, groups=None):
    return exchange(totals(exchange(pieces, axis, groups)), axis, groups)


def local(design, responses, picks):
    run_devices, term_devices = lax.axis_size("runs"), lax.axis_size("terms")
    resp, local_rows = responses.shape
    local_terms = design.shape[1]
    chips = run_devices // 2
    core = lax.axis_index("runs") % 2
    swap = [(i, i ^ 1) for i in range(run_devices)]
    sides = [list(range(side, run_devices, 2)) for side in range(2)]
    count = picks.size
    half = (4 + 2) * BLOCK

    def fetch(turn):
        where = jnp.stack([lax.axis_index("terms"), jnp.int32(turn), core])
        packed, most = pack(where, picks, design, term_devices)
        return where, exchange(packed, "terms"), most

    def grams(where, slots, prior=(None, None)):
        partner_slots = lax.ppermute(slots, "runs", swap)
        basis, sums = gram(
            where, picks, slots, responses, local_terms, half, prior[0]
        )
        partner_basis, sums = gram(
            where, picks, partner_slots, sums, local_terms, half, prior[1]
        )
        return basis, partner_basis, sums

    at, slots, most = fetch(0)
    state = grams(at, slots)

    def another(carry):
        turn, basis, partner_basis, _ = carry
        where, more, _ = fetch(turn)
        return turn + 1, *grams(where, more, (basis, partner_basis))

    _, basis, _, sums = lax.while_loop(
        lambda carry: carry[0] * SLOTS < most[0], another, (jnp.int32(1), *state)
    )

    mine = summed_everywhere(sums.reshape(chips, -1, LANES), "runs", sides)
    mine = mine.reshape(half, LANES)
    other = lax.ppermute(mine, "runs", swap)
    inverse = first_inverse(mine)

    scale = float(local_rows * run_devices) ** -0.5
    residual, pieces = finish(
        at, mine, other, inverse, responses, basis, design, run_devices, scale
    )
    gathered = summed_everywhere(pieces, "runs")[: local_terms // LANES]
    correlations = gathered.transpose(1, 0, 2).reshape(resp, -1)
    return (residual, correlations)


def solution(mesh):
    placed = (P("runs", "terms"), P(None, "runs"), P())
    return jax.shard_map(
        local,
        mesh=mesh,
        in_specs=placed,
        out_specs=(P(None, "runs"), P(None, "terms")),
        check_vma=False,
    )
```

time: 151 us -> 144 us (0.954)
  blocking collectives: 76.8 us -> 102 us
  starting transfers between devices: 25.5 us -> 11.4 us
  waiting for transfers between devices: 13.5 us -> 0.01 us
  other arithmetic: 2.24 us -> 0.08 us
    all_to_all x4 -> x5, blocking collectives: 76.8 us -> 102 us  [exchange(): return lax.all_to_all(pieces, axis, 0, 0, axis_index_groups=groups)]
    all_to_all x1 -> x0, starting transfers between devices: 13.3 us -> none  [exchange(): return lax.all_to_all(pieces, axis, 0, 0, axis_index_groups=groups)]
    all_to_all x1 -> x0, waiting for transfers between devices: 10.6 us -> none  [exchange(): return lax.all_to_all(pieces, axis, 0, 0, axis_index_groups=groups)]
    pallas_call x1, Pallas kernels: 21.9 us -> 16.5 us  [finish(): call(functools.partial(finish_kernel, scale), 'finish', (jax.ShapeDtypeSt...]
    pallas_call x2 -> x6, Pallas kernels: 7.36 us -> 11.4 us  [the longest x1 4.13 us: pack(): call(pack_kernel, 'pack', (jax.ShapeDtypeStruct((devices, SLOTS, rows), B...]
    ppermute x1, waiting for transfers between devices: 1.54 us -> 0.01 us  [grams(): partner_slots = lax.ppermute(slots, 'runs', swap)]
  transfers between devices with their start and end apart: 3 -> 2, of which waited for: 3 -> 0; matrix products, arithmetic and copies ran while one was open for 0% -> 0% of each run, Pallas kernels for 0% -> 4%
where the time goes in v4:
time: 144 us
  blocking collectives  102 us (71%)
  Pallas kernels  28 us (19%)
  starting transfers between devices  11.4 us (8%)
    all_to_all x5, blocking collectives, exchange(): return lax.all_to_all(pieces, axis, 0, 0, axis_index_groups=groups)  102 us
    pallas_call x1, Pallas kernels, finish(): call(functools.partial(finish_kernel, scale), 'finish', (jax.ShapeDtypeSt...  16.5 us
    ppermute x1, starting transfers between devices, grams(): partner_slots = lax.ppermute(slots, 'runs', swap)  6.02 us
    ppermute x1, starting transfers between devices, local(): other = lax.ppermute(mine, 'runs', swap)  5.41 us
    pallas_call x1, Pallas kernels, pack(): call(pack_kernel, 'pack', (jax.ShapeDtypeStruct((devices, SLOTS, rows), B...  4.13 us
    pallas_call x1, Pallas kernels, first_inverse(): call(first_kernel, 'first_inverse', jax.ShapeDtypeStruct((BLOCK, BLOCK),...  3.66 us
    pallas_call x2, Pallas kernels, gram(): call(functools.partial(gram_kernel, local_terms, devices, prior is not No...  3.52 us
  transfers between devices with their start and end apart: 2, of which 0 were waited for; matrix products, arithmetic and copies ran while one was open for 0% of the time, Pallas kernels for 4%

profile of v4, /device:TPU:1, one launch (start us, length us, event | category | flops | bytes accessed | tf_op | source)
XLA Modules:
  0.0 143.6 jit_solution(12161087506297323463)
XLA Ops:
  0.6 0.0 copy-start.1
  0.6 0.0 copy-start.2
  0.7 0.1 pad_add_fusion.1.place
  0.7 4.1 %pack.2 = (bf16[8,96,256]{2,1,0:T(8,128)(2,1)S(1)}, s32[1]{0:T(128)}) custom-call(s32[3]{0:T(128)S(1)} %pad_add_fusion.1.place, s32[2,256]{1,0:T(2,128)} %picks.5, bf16[256,6656]{1,0:T(8,128)(2,1)} %refs_5_.1), custom_call_target="tpu_custom_call" | custom-call | tf_op jit(solution)/shard_map/pack/pallas_call | solution.py:113
  4.9 24.6 %all_to_all.31 = bf16[8,96,256]{2,1,0:T(8,128)(2,1)S(1)} all-to-all(bf16[8,96,256]{2,1,0:T(8,128)(2,1)S(1)} %get-tuple-element.63), channel_id=1, replica_groups=mesh['runs'=64,'terms'=8] {'terms'}, dimensions={0} | all-to-all | bytes 786432 | tf_op jit(solution)/shard_map/all_to_all | solution.py:48
  29.5 6.0 %collective-permute-start.1 = (bf16[8,96,256]{2,1,0:T(8,128)(2,1)S(1)}, bf16[8,96,256]{2,1,0:T(8,128)(2,1)S(1)}, u32[]{:S(2)}, u32[]{:S(2)}) collective-permute-start(bf16[8,96,256]{2,1,0:T(8,128)(2,1)S(1)} %all_to_all.31), channel_id=1, source_target_pairs={{0,8},{8,0},{16,24},{24,16},{32,40},{40,32},{48,56},{56,48},{64,72... | collective-permute-start | bytes 1179656 | tf_op jit(solution)/shard_map/ppermute | solution.py:420
  35.5 0.0 copy-done.1
  35.5 0.0 copy-done.2
  35.5 1.4 gram.4
  36.9 0.0 collective-permute-done.1
  37.0 2.1 %gram.5 = (bf16[512,256]{1,0:T(8,128)(2,1)S(1)}, f32[768,128]{1,0:T(8,128)}) custom-call(s32[3]{0:T(128)S(1)} %pad_add_fusion.1.place, s32[2,256]{1,0:T(2,128)S(1)} %copy-done.1, bf16[768,256]{1,0:T(8,128)(2,1)S(1)} %bitcast.33, f32[768,128]{1,0:T(8,128)S(1)} %get-tuple-element.65.other), custom_call_target="tpu_custom_call" | custom-call | flops 335544320 | bytes 262144 | tf_op jit(solution)/shard_map/gram/pallas_call | solution.py:194
  39.1 0.7 while.14
  39.8 23.4 %all_to_all.32.pieces = f32[32,24,128]{2,1,0:T(8,128)S(1)} all-to-all(f32[32,24,128]{2,1,0:T(8,128)} %bitcast.34), channel_id=1, replica_groups={{0,16,32,48,64,80,96,112,128,144,160,176,192,208,224,240,256,272,288,30..., dimensions={0} | all-to-all | bytes 786432 | tf_op jit(solution)/shard_map/all_to_all | solution.py:48
  63.2 0.1 totals.2
  63.2 19.0 %all_to_all.33 = f32[32,24,128]{2,1,0:T(8,128)S(1)} all-to-all(f32[32,24,128]{2,1,0:T(8,128)S(1)} %totals.2), channel_id=1, replica_groups={{0,16,32,48,64,80,96,112,128,144,160,176,192,208,224,240,256,272,288,30..., dimensions={0} | all-to-all | bytes 786432 | tf_op jit(solution)/shard_map/all_to_all | solution.py:48
  82.2 0.0 copy-start
  82.2 5.4 %collective-permute-start.2 = (f32[768,128]{1,0:T(8,128)S(1)}, f32[768,128]{1,0:T(8,128)S(1)}, u32[]{:S(2)}, u32[]{:S(2)}) collective-permute-start(f32[768,128]{1,0:T(8,128)S(1)} %bitcast.28), channel_id=1, source_target_pairs={{0,8},{8,0},{16,24},{24,16},{32,40},{40,32},{48,56},{56,48},{64,72... | collective-permute-start | bytes 1179656 | tf_op jit(solution)/shard_map/ppermute | solution.py:443
  87.7 3.7 %first_inverse.1.refs_2_ = f32[128,128]{1,0:T(8,128)S(1)} custom-call(f32[768,128]{1,0:T(8,128)S(1)} %bitcast.29), custom_call_target="tpu_custom_call" | custom-call | flops 2000000000 | bytes 100000 | tf_op jit(solution)/shard_map/first_inverse/pallas_call | solution.py:298
  91.3 0.0 collective-permute-done.2.refs_1_
  91.3 0.0 copy-done
  91.3 16.5 %finish.1 = (f32[8,256]{1,0:T(8,128)}, f32[64,8,128]{2,1,0:T(8,128)S(1)}) custom-call(s32[3]{0:T(128)S(1)} %pad_add_fusion.1.place, f32[768,128]{1,0:T(8,128)S(1)} %bitcast.30, f32[768,128]{1,0:T(8,128)S(1)} %collective-permute-done.2.refs_1_, f32[128,128]{1,0:T(8,128)S(1)} %first_inverse.1.refs_2_, f32[8,256]{1,0:T(8,128)S(1)} %get-tuple-element.195, ...), custom_call_target="tpu_custom_call" | custom-call | tf_op jit(solution)/shard_map/finish/pallas_call | solution.py:381
  107.9 17.4 %all_to_all.34.pieces = f32[64,8,128]{2,1,0:T(8,128)S(1)} all-to-all(f32[64,8,128]{2,1,0:T(8,128)S(1)} %get-tuple-element.72), channel_id=1, replica_groups=mesh['runs'=64,'terms'=8] {'runs'}, dimensions={0} | all-to-all | bytes 524288 | tf_op jit(solution)/shard_map/all_to_all | solution.py:48
  125.3 0.1 totals.3
  125.4 17.5 %all_to_all.35 = f32[64,8,128]{2,1,0:T(8,128)S(1)} all-to-all(f32[64,8,128]{2,1,0:T(8,128)S(1)} %totals.3), channel_id=1, replica_groups=mesh['runs'=64,'terms'=8] {'runs'}, dimensions={0} | all-to-all | bytes 524288 | tf_op jit(solution)/shard_map/all_to_all | solution.py:48
  142.9 0.7 slice_bitcast_fusion
Async XLA Ops:
  0.6 34.9 %copy-start.1 = (s32[2,256]{1,0:T(2,128)S(1)}, s32[2,256]{1,0:T(2,128)}, u32[]{:S(2)}) copy-start(s32[2,256]{1,0:T(2,128)} %picks.5) | copy-start | bytes 6148
  0.6 34.9 %copy-start.2 = (f32[8,256]{1,0:T(8,128)S(1)}, f32[8,256]{1,0:T(8,128)}, u32[]{:S(2)}) copy-start(f32[8,256]{1,0:T(8,128)} %refs_3_.1) | copy-start | bytes 24580
  29.5 7.5 %collective-permute-start.1 = (bf16[8,96,256]{2,1,0:T(8,128)(2,1)S(1)}, bf16[8,96,256]{2,1,0:T(8,128)(2,1)S(1)}, u32[]{:S(2)}, u32[]{:S(2)}) collective-permute-start(bf16[8,96,256]{2,1,0:T(8,128)(2,1)S(1)} %all_to_all.31), channel_id=1, source_target_pairs={{0,8},{8,0},{16,24},{24,16},{32,40},{40,32},{48,56},{56,48},{64,72... | collective-permute-start | bytes 1179656 | tf_op jit(solution)/shard_map/ppermute | solution.py:420
  82.2 9.1 %copy-start = (bf16[256,6656]{1,0:T(8,128)(2,1)S(1)}, bf16[256,6656]{1,0:T(8,128)(2,1)}, u32[]{:S(2)}) copy-start(bf16[256,6656]{1,0:T(8,128)(2,1)} %get-tuple-element.194) | copy-start | bytes 10223620
  82.2 9.1 %collective-permute-start.2 = (f32[768,128]{1,0:T(8,128)S(1)}, f32[768,128]{1,0:T(8,128)S(1)}, u32[]{:S(2)}, u32[]{:S(2)}) collective-permute-start(f32[768,128]{1,0:T(8,128)S(1)} %bitcast.28), channel_id=1, source_target_pairs={{0,8},{8,0},{16,24},{24,16},{32,40},{40,32},{48,56},{56,48},{64,72... | collective-permute-start | bytes 1179656 | tf_op jit(solution)/shard_map/ppermute | solution.py:443

commit v5 on v4

--- a/solution.py
+++ b/solution.py
@@ -22,19 +22,20 @@
         (384, 512, 384, 512),
     ),
 )
+INNER = 704
 HIGH = lax.Precision.HIGHEST
 F32 = jnp.float32
 BF16 = jnp.bfloat16
 
 
-def call(kernel, name, out_shape, in_specs, out_specs, scratch=(), **more):
+def call(kernel, name, out_shape, in_specs, out_specs, scratch=(), vmem=32, **more):
     return pl.pallas_call(
         kernel,
         out_shape=out_shape,
         in_specs=in_specs,
         out_specs=out_specs,
         scratch_shapes=scratch,
-        compiler_params=pltpu.CompilerParams(vmem_limit_bytes=32 * 2**20),
+        compiler_params=pltpu.CompilerParams(vmem_limit_bytes=vmem * 2**20),
         name=name,
         **more,
     )
@@ -124,6 +125,7 @@
             pltpu.VMEM((SLOTS, 1), jnp.int32),
             pltpu.SemaphoreType.DMA((CHUNKS,)),
         ],
+        vmem=61,
     )(place, picks, design)
 
 
@@ -165,18 +167,7 @@
             sums[row:, :] = other[row:, :]
             return
         resp = other.shape[0]
-        rest, parts = other[...], []
-        for _ in range(3):
-            part = rest.astype(BF16).astype(F32)
-            parts.append(part)
-            rest = rest - part
-        inner = lax.dot_general(
-            jnp.concatenate(parts, axis=0).astype(BF16),
-            basis[...],
-            (((1,), (1,)), ((), ())),
-            preferred_element_type=F32,
-        )
-        inner = inner[2 * resp :] + inner[resp : 2 * resp] + inner[:resp]
+        inner = split_dot(other[...], basis[...], ((1,), (1,)))
         for j in range(0, count, BLOCK):
             sums[row : row + resp, :] = inner[:, j : j + BLOCK]
             row += resp
@@ -208,6 +199,22 @@
     )(*operands)
 
 
+def split_dot(left, right, dims):
+    rows = left.shape[0]
+    rest, parts = left, []
+    for _ in range(3):
+        part = rest.astype(BF16).astype(F32)
+        parts.append(part)
+        rest = rest - part
+    out = lax.dot_general(
+        jnp.concatenate(parts, axis=0).astype(BF16),
+        right,
+        (dims, ((), ())),
+        preferred_element_type=F32,
+    )
+    return out[2 * rows :] + out[rows : 2 * rows] + out[:rows]
+
+
 def total_kernel(pieces, totals):
     total = jnp.sum(pieces[...], axis=0)
     for piece in range(totals.shape[0]):
@@ -309,26 +316,28 @@
 
 def finish_kernel(scale, place, *refs):
     mine, other, known_inverse, responses, basis, design, residual, pieces = refs[:8]
-    packed, work, inverse, coef = refs[8:]
-    half = mine.shape[0]
+    work, inverse, coef, held, sem = refs[8:]
     count = basis.shape[0]
     resp = responses.shape[0]
     blocks = count // BLOCK
     core = place[2]
-    packed[pl.ds(pl.multiple_of(core * half, SUB), half), :] = mine[...]
-    packed[pl.ds(pl.multiple_of((1 - core) * half, SUB), half), :] = other[...]
-    ends = []
-    for side in range(2):
-        row = side * half
+    copy = pltpu.make_async_copy(design, held, sem)
+    copy.start()
+
+    def place_side(side, source):
+        row = 0
         for top, bottom, start, stop in HALVES[side]:
             for j in range(start, stop, BLOCK):
                 after = row + bottom - top
-                work[top:bottom, j : j + BLOCK] = packed[row:after, :]
+                work[top:bottom, j : j + BLOCK] = source[row:after, :]
                 row = after
-        ends.append(row)
+
+    for side in range(2):
+        pl.when(core == side)(functools.partial(place_side, side, mine))
+        pl.when(core != side)(functools.partial(place_side, side, other))
     for i in range(blocks):
-        inner = [packed[end + i * resp : end + (i + 1) * resp, :] for end in ends]
-        tall = [inner[0] + inner[1], jnp.zeros((BLOCK - resp, BLOCK), F32)]
+        at = pl.ds(INNER + i * resp, resp)
+        tall = [mine[at, :] + other[at, :], jnp.zeros((BLOCK - resp, BLOCK), F32)]
         work[i * BLOCK : (i + 1) * BLOCK, count:] = jnp.concatenate(tall, axis=0).T
 
     def eliminate(k):
@@ -362,13 +371,14 @@
         coef[start:stop, :] = work[start:stop, count:] - dot(
             work[start:stop, stop:count], coef[stop:, :]
         )
-    fitted = dot_first(coef[...], basis[...].astype(F32))
-    left = responses[...] - fitted[:resp, :]
+    fitted = split_dot(coef[...].T[:resp, :], basis[...], ((1,), (0,)))
+    left = responses[...] - fitted
     residual[...] = left
     rounded = left.astype(BF16)
     tiles = design.shape[1] // LANES
+    copy.wait()
     for tile in range(0, tiles, 2):
-        part = design[:, tile * LANES : (tile + 2) * LANES]
+        part = held[:, tile * LANES : (tile + 2) * LANES]
         both = jnp.dot(rounded, part, preferred_element_type=F32) * scale
         pieces[tile] = both[:, :LANES]
         pieces[tile + 1] = both[:, LANES:]
@@ -385,13 +395,14 @@
             jax.ShapeDtypeStruct((resp, rows), F32),
             jax.ShapeDtypeStruct((pieces, resp, LANES), F32),
         ),
-        [SCALAR] + [WHOLE] * 6,
+        [SCALAR] + [WHOLE] * 5 + [pl.BlockSpec(memory_space=pltpu.HBM)],
         (WHOLE, WHOLE),
         [
-            pltpu.VMEM((2 * mine.shape[0], LANES), F32),
             pltpu.VMEM((count, count + LANES), F32),
             pltpu.VMEM((BLOCK, BLOCK), F32),
             pltpu.VMEM((count, LANES), F32),
+            pltpu.VMEM(design.shape, design.dtype),
+            pltpu.SemaphoreType.DMA,
         ],
     )(place, mine, other, inverse, responses, basis, design)
 

time: 144 us -> 145 us (level)
  transfers between devices with their start and end apart: 2 -> 2, of which waited for: 0 -> 0; matrix products, arithmetic and copies ran while one was open for 0% -> 0% of each run, Pallas kernels for 4% -> 3%
where the time goes in v5:
time: 145 us
  blocking collectives  102 us (70%)
  Pallas kernels  28.8 us (20%)
  starting transfers between devices  11.3 us (8%)
    all_to_all x5, blocking collectives, exchange(): return lax.all_to_all(pieces, axis, 0, 0, axis_index_groups=groups)  102 us
    pallas_call x1, Pallas kernels, finish(): call(functools.partial(finish_kernel, scale), 'finish', (jax.ShapeDtypeSt...  16.6 us
    ppermute x1, starting transfers between devices, grams(): partner_slots = lax.ppermute(slots, 'runs', swap)  6.02 us
    ppermute x1, starting transfers between devices, local(): other = lax.ppermute(mine, 'runs', swap)  5.23 us
    pallas_call x1, Pallas kernels, pack(): call(pack_kernel, 'pack', (jax.ShapeDtypeStruct((devices, SLOTS, rows), B...  4.92 us
    pallas_call x1, Pallas kernels, first_inverse(): call(first_kernel, 'first_inverse', jax.ShapeDtypeStruct((BLOCK, BLOCK),...  3.66 us
    pallas_call x2, Pallas kernels, gram(): call(functools.partial(gram_kernel, local_terms, devices, prior is not No...  3.52 us
  transfers between devices with their start and end apart: 2, of which 0 were waited for; matrix products, arithmetic and copies ran while one was open for 0% of the time, Pallas kernels for 3%

profile of v5, /device:TPU:1, one launch (start us, length us, event | category | flops | bytes accessed | tf_op | source)
XLA Modules:
  0.0 145.0 jit_solution(15808795375516503036)
XLA Ops:
  0.6 0.0 copy-start.3
  0.6 0.0 copy-start.4
  0.7 0.6 pad_add_fusion.1.place
  1.3 0.0 copy-start.1
  1.3 4.9 %pack.2 = (bf16[8,96,256]{2,1,0:T(8,128)(2,1)}, s32[1]{0:T(128)}) custom-call(s32[3]{0:T(128)} %pad_add_fusion.1.place, s32[2,256]{1,0:T(2,128)} %picks.5, bf16[256,6656]{1,0:T(8,128)(2,1)} %refs_5_.1), custom_call_target="tpu_custom_call" | custom-call | tf_op jit(solution)/shard_map/pack/pallas_call | solution.py:114
  6.2 24.8 %all_to_all.31 = bf16[8,96,256]{2,1,0:T(8,128)(2,1)S(1)} all-to-all(bf16[8,96,256]{2,1,0:T(8,128)(2,1)} %get-tuple-element.63), channel_id=1, replica_groups=mesh['runs'=64,'terms'=8] {'terms'}, dimensions={0} | all-to-all | bytes 786432 | tf_op jit(solution)/shard_map/all_to_all | solution.py:49
  31.1 6.0 %collective-permute-start.1 = (bf16[8,96,256]{2,1,0:T(8,128)(2,1)S(1)}, bf16[8,96,256]{2,1,0:T(8,128)(2,1)S(1)}, u32[]{:S(2)}, u32[]{:S(2)}) collective-permute-start(bf16[8,96,256]{2,1,0:T(8,128)(2,1)S(1)} %all_to_all.31), channel_id=1, source_target_pairs={{0,8},{8,0},{16,24},{24,16},{32,40},{40,32},{48,56},{56,48},{64,72... | collective-permute-start | bytes 1179656 | tf_op jit(solution)/shard_map/ppermute | solution.py:431
  37.1 0.0 copy-done.3
  37.1 0.0 copy-done.4
  37.1 0.0 copy-done.1
  37.1 1.4 gram.4
  38.5 0.0 collective-permute-done.1
  38.5 2.1 %gram.5 = (bf16[512,256]{1,0:T(8,128)(2,1)S(1)}, f32[768,128]{1,0:T(8,128)}) custom-call(s32[3]{0:T(128)S(1)} %copy-done.1, s32[2,256]{1,0:T(2,128)S(1)} %copy-done.3, bf16[768,256]{1,0:T(8,128)(2,1)S(1)} %bitcast.33, f32[768,128]{1,0:T(8,128)S(1)} %get-tuple-element.65.other), custom_call_target="tpu_custom_call" | custom-call | flops 335544320 | bytes 262144 | tf_op jit(solution)/shard_map/gram/pallas_call | solution.py:185
  40.7 0.6 while.14
  41.3 23.4 %all_to_all.32.pieces = f32[32,24,128]{2,1,0:T(8,128)S(1)} all-to-all(f32[32,24,128]{2,1,0:T(8,128)} %bitcast.34), channel_id=1, replica_groups={{0,16,32,48,64,80,96,112,128,144,160,176,192,208,224,240,256,272,288,30..., dimensions={0} | all-to-all | bytes 786432 | tf_op jit(solution)/shard_map/all_to_all | solution.py:49
  64.7 0.1 totals.2
  64.8 19.0 %all_to_all.33 = f32[32,24,128]{2,1,0:T(8,128)S(1)} all-to-all(f32[32,24,128]{2,1,0:T(8,128)S(1)} %totals.2), channel_id=1, replica_groups={{0,16,32,48,64,80,96,112,128,144,160,176,192,208,224,240,256,272,288,30..., dimensions={0} | all-to-all | bytes 786432 | tf_op jit(solution)/shard_map/all_to_all | solution.py:49
  83.8 0.0 copy-start.2
  83.8 5.2 %collective-permute-start.2 = (f32[768,128]{1,0:T(8,128)S(1)}, f32[768,128]{1,0:T(8,128)S(1)}, u32[]{:S(2)}, u32[]{:S(2)}) collective-permute-start(f32[768,128]{1,0:T(8,128)S(1)} %bitcast.28), channel_id=1, source_target_pairs={{0,8},{8,0},{16,24},{24,16},{32,40},{40,32},{48,56},{56,48},{64,72... | collective-permute-start | bytes 1179656 | tf_op jit(solution)/shard_map/ppermute | solution.py:454
  89.0 3.7 %first_inverse.1.refs_2_ = f32[128,128]{1,0:T(8,128)S(1)} custom-call(f32[768,128]{1,0:T(8,128)S(1)} %bitcast.29), custom_call_target="tpu_custom_call" | custom-call | flops 2000000000 | bytes 100000 | tf_op jit(solution)/shard_map/first_inverse/pallas_call | solution.py:305
  92.7 0.0 collective-permute-done.2.refs_1_
  92.7 0.0 copy-done.2
  92.7 16.6 %finish.1 = (f32[8,256]{1,0:T(8,128)}, f32[64,8,128]{2,1,0:T(8,128)S(1)}) custom-call(s32[3]{0:T(128)S(1)} %copy-done.1, f32[768,128]{1,0:T(8,128)S(1)} %bitcast.30, f32[768,128]{1,0:T(8,128)S(1)} %collective-permute-done.2.refs_1_, f32[128,128]{1,0:T(8,128)S(1)} %first_inverse.1.refs_2_, f32[8,256]{1,0:T(8,128)S(1)} %get-tuple-element.195, ...), custom_call_target="tpu_custom_call" | custom-call | tf_op jit(solution)/shard_map/finish/pallas_call | solution.py:391
  109.2 17.4 %all_to_all.34.pieces = f32[64,8,128]{2,1,0:T(8,128)S(1)} all-to-all(f32[64,8,128]{2,1,0:T(8,128)S(1)} %get-tuple-element.72), channel_id=1, replica_groups=mesh['runs'=64,'terms'=8] {'runs'}, dimensions={0} | all-to-all | bytes 524288 | tf_op jit(solution)/shard_map/all_to_all | solution.py:49
  126.7 0.1 totals.3
  126.7 17.5 %all_to_all.35 = f32[64,8,128]{2,1,0:T(8,128)S(1)} all-to-all(f32[64,8,128]{2,1,0:T(8,128)S(1)} %totals.3), channel_id=1, replica_groups=mesh['runs'=64,'terms'=8] {'runs'}, dimensions={0} | all-to-all | bytes 524288 | tf_op jit(solution)/shard_map/all_to_all | solution.py:49
  144.3 0.7 slice_bitcast_fusion
Async XLA Ops:
  0.6 36.5 %copy-start.3 = (s32[2,256]{1,0:T(2,128)S(1)}, s32[2,256]{1,0:T(2,128)}, u32[]{:S(2)}) copy-start(s32[2,256]{1,0:T(2,128)} %picks.5) | copy-start | bytes 6148
  0.6 36.5 %copy-start.4 = (f32[8,256]{1,0:T(8,128)S(1)}, f32[8,256]{1,0:T(8,128)}, u32[]{:S(2)}) copy-start(f32[8,256]{1,0:T(8,128)} %refs_3_.1) | copy-start | bytes 24580
  1.3 35.8 %copy-start.1 = (s32[3]{0:T(128)S(1)}, s32[3]{0:T(128)}, u32[]{:S(2)}) copy-start(s32[3]{0:T(128)} %pad_add_fusion.1.place) | copy-start | bytes 40
  31.1 7.5 %collective-permute-start.1 = (bf16[8,96,256]{2,1,0:T(8,128)(2,1)S(1)}, bf16[8,96,256]{2,1,0:T(8,128)(2,1)S(1)}, u32[]{:S(2)}, u32[]{:S(2)}) collective-permute-start(bf16[8,96,256]{2,1,0:T(8,128)(2,1)S(1)} %all_to_all.31), channel_id=1, source_target_pairs={{0,8},{8,0},{16,24},{24,16},{32,40},{40,32},{48,56},{56,48},{64,72... | collective-permute-start | bytes 1179656 | tf_op jit(solution)/shard_map/ppermute | solution.py:431
  83.8 8.9 %copy-start.2 = (bf16[256,6656]{1,0:T(8,128)(2,1)S(1)}, bf16[256,6656]{1,0:T(8,128)(2,1)}, u32[]{:S(2)}) copy-start(bf16[256,6656]{1,0:T(8,128)(2,1)} %get-tuple-element.194) | copy-start | bytes 10223620
  83.8 8.9 %collective-permute-start.2 = (f32[768,128]{1,0:T(8,128)S(1)}, f32[768,128]{1,0:T(8,128)S(1)}, u32[]{:S(2)}, u32[]{:S(2)}) collective-permute-start(f32[768,128]{1,0:T(8,128)S(1)} %bitcast.28), channel_id=1, source_target_pairs={{0,8},{8,0},{16,24},{24,16},{32,40},{40,32},{48,56},{56,48},{64,72... | collective-permute-start | bytes 1179656 | tf_op jit(solution)/shard_map/ppermute | solution.py:454

commit v6 on v5

--- a/solution.py
+++ b/solution.py
@@ -11,7 +11,7 @@
 SUB = 8
 BLOCK = 128
 SLOTS = 96
-CHUNKS = 4
+CHUNKS = 2
 HALVES = (
     ((0, 128, 0, 512), (128, 256, 128, 256), (128, 192, 256, 384)),
     (
@@ -23,7 +23,6 @@
     ),
 )
 INNER = 704
-HIGH = lax.Precision.HIGHEST
 F32 = jnp.float32
 BF16 = jnp.bfloat16
 
@@ -125,7 +124,6 @@
             pltpu.VMEM((SLOTS, 1), jnp.int32),
             pltpu.SemaphoreType.DMA((CHUNKS,)),
         ],
-        vmem=61,
     )(place, picks, design)
 
 
@@ -199,15 +197,38 @@
     )(*operands)
 
 
+def split(value):
+    parts = []
+    for _ in range(3):
+        parts.append(value.astype(BF16).astype(F32))
+        value = value - parts[-1]
+    return parts
+
+
+def left_parts(value, axis):
+    a, b, c = split(value)
+    return jnp.concatenate([a, a, a, b, b, c], axis=axis).astype(BF16)
+
+
+def right_parts(value):
+    a, b, c = split(value)
+    return jnp.concatenate([a, b, c, a, b, a], axis=0).astype(BF16)
+
+
+def dot_parts(left, right, axis=1):
+    return lax.dot_general(
+        left, right, (((axis,), (0,)), ((), ())), preferred_element_type=F32
+    )
+
+
+def dot(left, right):
+    return dot_parts(left_parts(left, 1), right_parts(right))
+
+
 def split_dot(left, right, dims):
     rows = left.shape[0]
-    rest, parts = left, []
-    for _ in range(3):
-        part = rest.astype(BF16).astype(F32)
-        parts.append(part)
-        rest = rest - part
     out = lax.dot_general(
-        jnp.concatenate(parts, axis=0).astype(BF16),
+        jnp.concatenate(split(left), axis=0).astype(BF16),
         right,
         (dims, ((), ())),
         preferred_element_type=F32,
@@ -228,20 +249,6 @@
 
 def spread(piece):
     return jnp.broadcast_to(piece, (SUB, LANES))
-
-
-def dot(left, right):
-    return jnp.dot(left, right, precision=HIGH, preferred_element_type=F32)
-
-
-def dot_first(left, right):
-    return lax.dot_general(
-        left,
-        right,
-        (((0,), (0,)), ((), ())),
-        precision=HIGH,
-        preferred_element_type=F32,
-    )
 
 
 def across(group, lane):
@@ -272,21 +279,24 @@
     for k in range(count):
         first = SUB * k
         mine = groups[k]
-        small = invert_small(
-            [across(mine, first + j) for j in range(SUB)], sub
-        )
+        turned = left_parts(jnp.where(lane < first, -mine, mine), 0)
+        small = invert_small([across(mine, first + j) for j in range(SUB)], sub)
         inside = (lane >= first) & (lane < first + SUB)
         unit = jnp.where(lane - first == sub, 1.0, 0.0)
         mine = jnp.where(inside, unit, mine)
-        top = small[0] * spread(mine[0:1, :])
-        for j in range(1, SUB):
-            top = top + small[j] * spread(mine[j : j + 1, :])
-        rows = [spread(top[j : j + 1, :]) for j in range(SUB)]
-        for step in range(1, count):
-            g = (k + step) % count
+        terms = [small[j] * spread(mine[j : j + 1, :]) for j in range(SUB)]
+        while len(terms) > 1:
+            terms = [terms[i] + terms[i + 1] for i in range(0, len(terms), 2)]
+        top = terms[0]
+        change = dot_parts(turned, right_parts(top), 0)
+        for g in range(count):
             new = jnp.where(inside, 0.0, groups[g])
-            for j in range(SUB):
-                new = new - across(groups[g], first + j) * rows[j]
+            if g == k + 1:
+                for j in range(SUB):
+                    row = spread(top[j : j + 1, :])
+                    new = new - across(groups[g], first + j) * row
+            else:
+                new = new - change[SUB * g : SUB * (g + 1), :]
             groups[g] = new
         groups[k] = top
     return groups
@@ -316,13 +326,11 @@
 
 def finish_kernel(scale, place, *refs):
     mine, other, known_inverse, responses, basis, design, residual, pieces = refs[:8]
-    work, inverse, coef, held, sem = refs[8:]
+    work, inverse, coef = refs[8:]
     count = basis.shape[0]
     resp = responses.shape[0]
     blocks = count // BLOCK
     core = place[2]
-    copy = pltpu.make_async_copy(design, held, sem)
-    copy.start()
 
     def place_side(side, source):
         row = 0
@@ -345,9 +353,8 @@
         right = work[start:stop, stop:]
         lead = dot(inverse[...], right)
         if stop < count:
-            work[stop:, stop:] = work[stop:, stop:] - dot_first(
-                right[:, : count - stop], lead
-            )
+            turned = right[:, : count - stop].T
+            work[stop:, stop:] = work[stop:, stop:] - dot(turned, lead)
         work[start:stop, stop:] = lead
 
     def step(k, carry):
@@ -376,9 +383,8 @@
     residual[...] = left
     rounded = left.astype(BF16)
     tiles = design.shape[1] // LANES
-    copy.wait()
     for tile in range(0, tiles, 2):
-        part = held[:, tile * LANES : (tile + 2) * LANES]
+        part = design[:, tile * LANES : (tile + 2) * LANES]
         both = jnp.dot(rounded, part, preferred_element_type=F32) * scale
         pieces[tile] = both[:, :LANES]
         pieces[tile + 1] = both[:, LANES:]
@@ -395,14 +401,12 @@
             jax.ShapeDtypeStruct((resp, rows), F32),
             jax.ShapeDtypeStruct((pieces, resp, LANES), F32),
         ),
-        [SCALAR] + [WHOLE] * 5 + [pl.BlockSpec(memory_space=pltpu.HBM)],
+        [SCALAR] + [WHOLE] * 6,
         (WHOLE, WHOLE),
         [
             pltpu.VMEM((count, count + LANES), F32),
             pltpu.VMEM((BLOCK, BLOCK), F32),
             pltpu.VMEM((count, LANES), F32),
-            pltpu.VMEM(design.shape, design.dtype),
-            pltpu.SemaphoreType.DMA,
         ],
     )(place, mine, other, inverse, responses, basis, design)
 

time: 145 us -> 141 us (0.972)
  Pallas kernels: 28.8 us -> 24.7 us
    pallas_call x1, Pallas kernels: 16.6 us -> 14 us  [finish(): call(functools.partial(finish_kernel, scale), 'finish', (jax.ShapeDtypeSt...]
where the time goes in v6:
time: 141 us; the launch traced here: 140 us
  blocking collectives  102 us (72%)
  Pallas kernels  24.7 us (18%)
  starting transfers between devices  11.3 us (8%)
    all_to_all x5, blocking collectives, exchange(): return lax.all_to_all(pieces, axis, 0, 0, axis_index_groups=groups)  102 us
    pallas_call x1, Pallas kernels, finish(): call(functools.partial(finish_kernel, scale), 'finish', (jax.ShapeDtypeSt...  14 us
    ppermute x1, starting transfers between devices, grams(): partner_slots = lax.ppermute(slots, 'runs', swap)  6.02 us
    ppermute x1, starting transfers between devices, local(): other = lax.ppermute(mine, 'runs', swap)  5.23 us
    pallas_call x1, Pallas kernels, pack(): call(pack_kernel, 'pack', (jax.ShapeDtypeStruct((devices, SLOTS, rows), B...  3.86 us
    pallas_call x2, Pallas kernels, gram(): call(functools.partial(gram_kernel, local_terms, devices, prior is not No...  3.52 us
    pallas_call x1, Pallas kernels, first_inverse(): call(first_kernel, 'first_inverse', jax.ShapeDtypeStruct((BLOCK, BLOCK),...  3.18 us
  transfers between devices with their start and end apart: 2, of which 0 were waited for; matrix products, arithmetic and copies ran while one was open for 0% of the time, Pallas kernels for 3%

profile of v6, /device:TPU:1, one launch (start us, length us, event | category | flops | bytes accessed | tf_op | source)
XLA Modules:
  0.0 140.2 jit_solution(12958932014879391456)
XLA Ops:
  0.6 0.0 copy-start.1
  0.6 0.0 copy-start.2
  0.7 0.1 pad_add_fusion.1.place
  0.7 3.9 %pack.2 = (bf16[8,96,256]{2,1,0:T(8,128)(2,1)S(1)}, s32[1]{0:T(128)}) custom-call(s32[3]{0:T(128)S(1)} %pad_add_fusion.1.place, s32[2,256]{1,0:T(2,128)} %picks.5, bf16[256,6656]{1,0:T(8,128)(2,1)} %refs_5_.1), custom_call_target="tpu_custom_call" | custom-call | tf_op jit(solution)/shard_map/pack/pallas_call | solution.py:113
  4.6 24.6 %all_to_all.31 = bf16[8,96,256]{2,1,0:T(8,128)(2,1)S(1)} all-to-all(bf16[8,96,256]{2,1,0:T(8,128)(2,1)S(1)} %get-tuple-element.63), channel_id=1, replica_groups=mesh['runs'=64,'terms'=8] {'terms'}, dimensions={0} | all-to-all | bytes 786432 | tf_op jit(solution)/shard_map/all_to_all | solution.py:48
  29.2 6.0 %collective-permute-start.1 = (bf16[8,96,256]{2,1,0:T(8,128)(2,1)S(1)}, bf16[8,96,256]{2,1,0:T(8,128)(2,1)S(1)}, u32[]{:S(2)}, u32[]{:S(2)}) collective-permute-start(bf16[8,96,256]{2,1,0:T(8,128)(2,1)S(1)} %all_to_all.31), channel_id=1, source_target_pairs={{0,8},{8,0},{16,24},{24,16},{32,40},{40,32},{48,56},{56,48},{64,72... | collective-permute-start | bytes 1179656 | tf_op jit(solution)/shard_map/ppermute | solution.py:435
  35.2 0.0 copy-done.1
  35.3 0.0 copy-done.2
  35.3 1.4 %gram.4 = (bf16[512,256]{1,0:T(8,128)(2,1)S(1)}, f32[768,128]{1,0:T(8,128)S(1)}) custom-call(s32[3]{0:T(128)S(1)} %pad_add_fusion.1.place, s32[2,256]{1,0:T(2,128)S(1)} %copy-done.1, bf16[768,256]{1,0:T(8,128)(2,1)S(1)} %bitcast.31, f32[8,256]{1,0:T(8,128)S(1)} %copy-done.2), custom_call_target="tpu_custom_call" | custom-call | flops 335544320 | bytes 262144 | tf_op jit(solution)/shard_map/gram/pallas_call | solution.py:183
  36.7 0.0 collective-permute-done.1
  36.7 2.1 %gram.5 = (bf16[512,256]{1,0:T(8,128)(2,1)S(1)}, f32[768,128]{1,0:T(8,128)}) custom-call(s32[3]{0:T(128)S(1)} %pad_add_fusion.1.place, s32[2,256]{1,0:T(2,128)S(1)} %copy-done.1, bf16[768,256]{1,0:T(8,128)(2,1)S(1)} %bitcast.33, f32[768,128]{1,0:T(8,128)S(1)} %get-tuple-element.65.other), custom_call_target="tpu_custom_call" | custom-call | flops 335544320 | bytes 262144 | tf_op jit(solution)/shard_map/gram/pallas_call | solution.py:183
  38.8 0.7 while.14
  39.5 23.4 %all_to_all.32.pieces = f32[32,24,128]{2,1,0:T(8,128)S(1)} all-to-all(f32[32,24,128]{2,1,0:T(8,128)} %bitcast.34), channel_id=1, replica_groups={{0,16,32,48,64,80,96,112,128,144,160,176,192,208,224,240,256,272,288,30..., dimensions={0} | all-to-all | bytes 786432 | tf_op jit(solution)/shard_map/all_to_all | solution.py:48
  62.9 0.1 totals.2
  63.0 19.0 %all_to_all.33 = f32[32,24,128]{2,1,0:T(8,128)S(1)} all-to-all(f32[32,24,128]{2,1,0:T(8,128)S(1)} %totals.2), channel_id=1, replica_groups={{0,16,32,48,64,80,96,112,128,144,160,176,192,208,224,240,256,272,288,30..., dimensions={0} | all-to-all | bytes 786432 | tf_op jit(solution)/shard_map/all_to_all | solution.py:48
  82.0 0.0 copy-start
  82.0 5.2 %collective-permute-start.2 = (f32[768,128]{1,0:T(8,128)S(1)}, f32[768,128]{1,0:T(8,128)S(1)}, u32[]{:S(2)}, u32[]{:S(2)}) collective-permute-start(f32[768,128]{1,0:T(8,128)S(1)} %bitcast.28), channel_id=1, source_target_pairs={{0,8},{8,0},{16,24},{24,16},{32,40},{40,32},{48,56},{56,48},{64,72... | collective-permute-start | bytes 1179656 | tf_op jit(solution)/shard_map/ppermute | solution.py:458
  87.2 3.2 %first_inverse.1.refs_2_ = f32[128,128]{1,0:T(8,128)S(1)} custom-call(f32[768,128]{1,0:T(8,128)S(1)} %bitcast.29), custom_call_target="tpu_custom_call" | custom-call | flops 2000000000 | bytes 100000 | tf_op jit(solution)/shard_map/first_inverse/pallas_call | solution.py:315
  90.4 0.0 collective-permute-done.2.refs_1_
  90.4 0.0 copy-done
  90.4 14.0 %finish.1 = (f32[8,256]{1,0:T(8,128)}, f32[64,8,128]{2,1,0:T(8,128)S(1)}) custom-call(s32[3]{0:T(128)S(1)} %pad_add_fusion.1.place, f32[768,128]{1,0:T(8,128)S(1)} %bitcast.30, f32[768,128]{1,0:T(8,128)S(1)} %collective-permute-done.2.refs_1_, f32[128,128]{1,0:T(8,128)S(1)} %first_inverse.1.refs_2_, f32[8,256]{1,0:T(8,128)S(1)} %get-tuple-element.195, ...), custom_call_target="tpu_custom_call" | custom-call | tf_op jit(solution)/shard_map/finish/pallas_call | solution.py:397
  104.5 17.4 %all_to_all.34.pieces = f32[64,8,128]{2,1,0:T(8,128)S(1)} all-to-all(f32[64,8,128]{2,1,0:T(8,128)S(1)} %get-tuple-element.72), channel_id=1, replica_groups=mesh['runs'=64,'terms'=8] {'runs'}, dimensions={0} | all-to-all | bytes 524288 | tf_op jit(solution)/shard_map/all_to_all | solution.py:48
  121.9 0.1 totals.3
  121.9 17.5 %all_to_all.35 = f32[64,8,128]{2,1,0:T(8,128)S(1)} all-to-all(f32[64,8,128]{2,1,0:T(8,128)S(1)} %totals.3), channel_id=1, replica_groups=mesh['runs'=64,'terms'=8] {'runs'}, dimensions={0} | all-to-all | bytes 524288 | tf_op jit(solution)/shard_map/all_to_all | solution.py:48
  139.5 0.7 slice_bitcast_fusion
Async XLA Ops:
  0.6 34.6 %copy-start.1 = (s32[2,256]{1,0:T(2,128)S(1)}, s32[2,256]{1,0:T(2,128)}, u32[]{:S(2)}) copy-start(s32[2,256]{1,0:T(2,128)} %picks.5) | copy-start | bytes 6148
  0.6 34.6 %copy-start.2 = (f32[8,256]{1,0:T(8,128)S(1)}, f32[8,256]{1,0:T(8,128)}, u32[]{:S(2)}) copy-start(f32[8,256]{1,0:T(8,128)} %refs_3_.1) | copy-start | bytes 24580
  29.2 7.5 %collective-permute-start.1 = (bf16[8,96,256]{2,1,0:T(8,128)(2,1)S(1)}, bf16[8,96,256]{2,1,0:T(8,128)(2,1)S(1)}, u32[]{:S(2)}, u32[]{:S(2)}) collective-permute-start(bf16[8,96,256]{2,1,0:T(8,128)(2,1)S(1)} %all_to_all.31), channel_id=1, source_target_pairs={{0,8},{8,0},{16,24},{24,16},{32,40},{40,32},{48,56},{56,48},{64,72... | collective-permute-start | bytes 1179656 | tf_op jit(solution)/shard_map/ppermute | solution.py:435
  82.0 8.4 %copy-start = (bf16[256,6656]{1,0:T(8,128)(2,1)S(1)}, bf16[256,6656]{1,0:T(8,128)(2,1)}, u32[]{:S(2)}) copy-start(bf16[256,6656]{1,0:T(8,128)(2,1)} %get-tuple-element.194) | copy-start | bytes 10223620
  82.0 8.4 %collective-permute-start.2 = (f32[768,128]{1,0:T(8,128)S(1)}, f32[768,128]{1,0:T(8,128)S(1)}, u32[]{:S(2)}, u32[]{:S(2)}) collective-permute-start(f32[768,128]{1,0:T(8,128)S(1)} %bitcast.28), channel_id=1, source_target_pairs={{0,8},{8,0},{16,24},{24,16},{32,40},{40,32},{48,56},{56,48},{64,72... | collective-permute-start | bytes 1179656 | tf_op jit(solution)/shard_map/ppermute | solution.py:458

commit v7 on v6

--- a/solution.py
+++ b/solution.py
@@ -237,13 +237,12 @@
 
 
 def total_kernel(pieces, totals):
-    total = jnp.sum(pieces[...], axis=0)
-    for piece in range(totals.shape[0]):
-        totals[piece] = total
-
-
-def totals(pieces):
-    shape = jax.ShapeDtypeStruct(pieces.shape, pieces.dtype)
+    total = jnp.sum(pieces[...], axis=0).astype(totals.dtype)
+    totals[...] = jnp.broadcast_to(total, totals.shape)
+
+
+def totals(pieces, sent):
+    shape = jax.ShapeDtypeStruct(pieces.shape, sent)
     return call(total_kernel, "totals", shape, [WHOLE], WHOLE)(pieces)
 
 
@@ -411,8 +410,8 @@
     )(place, mine, other, inverse, responses, basis, design)
 
 
-def summed_everywhere(pieces, axis, groups=None):
-    return exchange(totals(exchange(pieces, axis, groups)), axis, groups)
+def summed_everywhere(pieces, axis, groups=None, sent=F32):
+    return exchange(totals(exchange(pieces, axis, groups), sent), axis, groups)
 
 
 def local(design, responses, picks):
@@ -462,8 +461,8 @@
     residual, pieces = finish(
         at, mine, other, inverse, responses, basis, design, run_devices, scale
     )
-    gathered = summed_everywhere(pieces, "runs")[: local_terms // LANES]
-    correlations = gathered.transpose(1, 0, 2).reshape(resp, -1)
+    gathered = summed_everywhere(pieces, "runs", sent=BF16)[: local_terms // LANES]
+    correlations = gathered.transpose(1, 0, 2).reshape(resp, -1).astype(F32)
     return (residual, correlations)
 
 

time: 141 us -> 138 us (0.979)
  blocking collectives: 102 us -> 99.7 us
    all_to_all x5, blocking collectives: 102 us -> 99.7 us  [exchange(): return lax.all_to_all(pieces, axis, 0, 0, axis_index_groups=groups)]
where the time goes in v7:
time: 138 us
  blocking collectives  99.7 us (72%)
  Pallas kernels  24.7 us (18%)
  starting transfers between devices  11.3 us (8%)
    all_to_all x5, blocking collectives, exchange(): return lax.all_to_all(pieces, axis, 0, 0, axis_index_groups=groups)  99.7 us
    pallas_call x1, Pallas kernels, finish(): call(functools.partial(finish_kernel, scale), 'finish', (jax.ShapeDtypeSt...  14 us
    ppermute x1, starting transfers between devices, grams(): partner_slots = lax.ppermute(slots, 'runs', swap)  6.02 us
    ppermute x1, starting transfers between devices, local(): other = lax.ppermute(mine, 'runs', swap)  5.23 us
    pallas_call x1, Pallas kernels, pack(): call(pack_kernel, 'pack', (jax.ShapeDtypeStruct((devices, SLOTS, rows), B...  3.86 us
    pallas_call x2, Pallas kernels, gram(): call(functools.partial(gram_kernel, local_terms, devices, prior is not No...  3.52 us
    pallas_call x1, Pallas kernels, first_inverse(): call(first_kernel, 'first_inverse', jax.ShapeDtypeStruct((BLOCK, BLOCK),...  3.18 us
  transfers between devices with their start and end apart: 2, of which 0 were waited for; matrix products, arithmetic and copies ran while one was open for 0% of the time, Pallas kernels for 3%

profile of v7, /device:TPU:1, one launch (start us, length us, event | category | flops | bytes accessed | tf_op | source)
XLA Modules:
  0.0 137.9 jit_solution(8498450169949392091)
XLA Ops:
  0.6 0.0 copy-start.1
  0.6 0.0 copy-start.2
  0.7 0.1 pad_add_fusion.1.place
  0.7 3.9 %pack.2 = (bf16[8,96,256]{2,1,0:T(8,128)(2,1)S(1)}, s32[1]{0:T(128)}) custom-call(s32[3]{0:T(128)S(1)} %pad_add_fusion.1.place, s32[2,256]{1,0:T(2,128)} %picks.5, bf16[256,6656]{1,0:T(8,128)(2,1)} %refs_5_.1), custom_call_target="tpu_custom_call" | custom-call | tf_op jit(solution)/shard_map/pack/pallas_call | solution.py:113
  4.6 24.6 %all_to_all.31 = bf16[8,96,256]{2,1,0:T(8,128)(2,1)S(1)} all-to-all(bf16[8,96,256]{2,1,0:T(8,128)(2,1)S(1)} %get-tuple-element.63), channel_id=1, replica_groups=mesh['runs'=64,'terms'=8] {'terms'}, dimensions={0} | all-to-all | bytes 786432 | tf_op jit(solution)/shard_map/all_to_all | solution.py:48
  29.2 6.0 %collective-permute-start.1 = (bf16[8,96,256]{2,1,0:T(8,128)(2,1)S(1)}, bf16[8,96,256]{2,1,0:T(8,128)(2,1)S(1)}, u32[]{:S(2)}, u32[]{:S(2)}) collective-permute-start(bf16[8,96,256]{2,1,0:T(8,128)(2,1)S(1)} %all_to_all.31), channel_id=1, source_target_pairs={{0,8},{8,0},{16,24},{24,16},{32,40},{40,32},{48,56},{56,48},{64,72... | collective-permute-start | bytes 1179656 | tf_op jit(solution)/shard_map/ppermute | solution.py:434
  35.2 0.0 copy-done.1
  35.3 0.0 copy-done.2
  35.3 1.4 %gram.4 = (bf16[512,256]{1,0:T(8,128)(2,1)S(1)}, f32[768,128]{1,0:T(8,128)S(1)}) custom-call(s32[3]{0:T(128)S(1)} %pad_add_fusion.1.place, s32[2,256]{1,0:T(2,128)S(1)} %copy-done.1, bf16[768,256]{1,0:T(8,128)(2,1)S(1)} %bitcast.31, f32[8,256]{1,0:T(8,128)S(1)} %copy-done.2), custom_call_target="tpu_custom_call" | custom-call | flops 335544320 | bytes 262144 | tf_op jit(solution)/shard_map/gram/pallas_call | solution.py:183
  36.7 0.0 collective-permute-done.1
  36.7 2.1 %gram.5 = (bf16[512,256]{1,0:T(8,128)(2,1)S(1)}, f32[768,128]{1,0:T(8,128)}) custom-call(s32[3]{0:T(128)S(1)} %pad_add_fusion.1.place, s32[2,256]{1,0:T(2,128)S(1)} %copy-done.1, bf16[768,256]{1,0:T(8,128)(2,1)S(1)} %bitcast.33, f32[768,128]{1,0:T(8,128)S(1)} %get-tuple-element.65.other), custom_call_target="tpu_custom_call" | custom-call | flops 335544320 | bytes 262144 | tf_op jit(solution)/shard_map/gram/pallas_call | solution.py:183
  38.8 0.7 while.14
  39.5 23.4 %all_to_all.32.pieces = f32[32,24,128]{2,1,0:T(8,128)S(1)} all-to-all(f32[32,24,128]{2,1,0:T(8,128)} %bitcast.34), channel_id=1, replica_groups={{0,16,32,48,64,80,96,112,128,144,160,176,192,208,224,240,256,272,288,30..., dimensions={0} | all-to-all | bytes 786432 | tf_op jit(solution)/shard_map/all_to_all | solution.py:48
  62.9 0.1 totals.2
  63.0 19.0 %all_to_all.33 = f32[32,24,128]{2,1,0:T(8,128)S(1)} all-to-all(f32[32,24,128]{2,1,0:T(8,128)S(1)} %totals.2), channel_id=1, replica_groups={{0,16,32,48,64,80,96,112,128,144,160,176,192,208,224,240,256,272,288,30..., dimensions={0} | all-to-all | bytes 786432 | tf_op jit(solution)/shard_map/all_to_all | solution.py:48
  82.0 0.0 copy-start
  82.0 5.2 %collective-permute-start.2 = (f32[768,128]{1,0:T(8,128)S(1)}, f32[768,128]{1,0:T(8,128)S(1)}, u32[]{:S(2)}, u32[]{:S(2)}) collective-permute-start(f32[768,128]{1,0:T(8,128)S(1)} %bitcast.28), channel_id=1, source_target_pairs={{0,8},{8,0},{16,24},{24,16},{32,40},{40,32},{48,56},{56,48},{64,72... | collective-permute-start | bytes 1179656 | tf_op jit(solution)/shard_map/ppermute | solution.py:457
  87.2 3.2 %first_inverse.1.refs_2_ = f32[128,128]{1,0:T(8,128)S(1)} custom-call(f32[768,128]{1,0:T(8,128)S(1)} %bitcast.29), custom_call_target="tpu_custom_call" | custom-call | flops 2000000000 | bytes 100000 | tf_op jit(solution)/shard_map/first_inverse/pallas_call | solution.py:314
  90.4 0.0 collective-permute-done.2.refs_1_
  90.4 0.0 copy-done
  90.4 14.0 %finish.1 = (f32[8,256]{1,0:T(8,128)}, f32[64,8,128]{2,1,0:T(8,128)S(1)}) custom-call(s32[3]{0:T(128)S(1)} %pad_add_fusion.1.place, f32[768,128]{1,0:T(8,128)S(1)} %bitcast.30, f32[768,128]{1,0:T(8,128)S(1)} %collective-permute-done.2.refs_1_, f32[128,128]{1,0:T(8,128)S(1)} %first_inverse.1.refs_2_, f32[8,256]{1,0:T(8,128)S(1)} %get-tuple-element.195, ...), custom_call_target="tpu_custom_call" | custom-call | tf_op jit(solution)/shard_map/finish/pallas_call | solution.py:396
  104.5 17.4 %all_to_all.34.pieces = f32[64,8,128]{2,1,0:T(8,128)S(1)} all-to-all(f32[64,8,128]{2,1,0:T(8,128)S(1)} %get-tuple-element.72), channel_id=1, replica_groups=mesh['runs'=64,'terms'=8] {'runs'}, dimensions={0} | all-to-all | bytes 524288 | tf_op jit(solution)/shard_map/all_to_all | solution.py:48
  121.9 0.1 totals.3
  121.9 15.3 %all_to_all.35 = bf16[64,8,128]{2,1,0:T(8,128)(2,1)S(1)} all-to-all(bf16[64,8,128]{2,1,0:T(8,128)(2,1)S(1)} %totals.3), channel_id=1, replica_groups=mesh['runs'=64,'terms'=8] {'runs'}, dimensions={0} | all-to-all | bytes 262144 | tf_op jit(solution)/shard_map/all_to_all | solution.py:48
  137.2 0.7 convert_bitcast_fusion
Async XLA Ops:
  0.6 34.6 %copy-start.1 = (s32[2,256]{1,0:T(2,128)S(1)}, s32[2,256]{1,0:T(2,128)}, u32[]{:S(2)}) copy-start(s32[2,256]{1,0:T(2,128)} %picks.5) | copy-start | bytes 6148
  0.6 34.6 %copy-start.2 = (f32[8,256]{1,0:T(8,128)S(1)}, f32[8,256]{1,0:T(8,128)}, u32[]{:S(2)}) copy-start(f32[8,256]{1,0:T(8,128)} %refs_3_.1) | copy-start | bytes 24580
  29.2 7.5 %collective-permute-start.1 = (bf16[8,96,256]{2,1,0:T(8,128)(2,1)S(1)}, bf16[8,96,256]{2,1,0:T(8,128)(2,1)S(1)}, u32[]{:S(2)}, u32[]{:S(2)}) collective-permute-start(bf16[8,96,256]{2,1,0:T(8,128)(2,1)S(1)} %all_to_all.31), channel_id=1, source_target_pairs={{0,8},{8,0},{16,24},{24,16},{32,40},{40,32},{48,56},{56,48},{64,72... | collective-permute-start | bytes 1179656 | tf_op jit(solution)/shard_map/ppermute | solution.py:434
  82.0 8.4 %copy-start = (bf16[256,6656]{1,0:T(8,128)(2,1)S(1)}, bf16[256,6656]{1,0:T(8,128)(2,1)}, u32[]{:S(2)}) copy-start(bf16[256,6656]{1,0:T(8,128)(2,1)} %get-tuple-element.194) | copy-start | bytes 10223620
  82.0 8.4 %collective-permute-start.2 = (f32[768,128]{1,0:T(8,128)S(1)}, f32[768,128]{1,0:T(8,128)S(1)}, u32[]{:S(2)}, u32[]{:S(2)}) collective-permute-start(f32[768,128]{1,0:T(8,128)S(1)} %bitcast.28), channel_id=1, source_target_pairs={{0,8},{8,0},{16,24},{24,16},{32,40},{40,32},{48,56},{56,48},{64,72... | collective-permute-start | bytes 1179656 | tf_op jit(solution)/shard_map/ppermute | solution.py:457

commit v8 on v7

--- a/solution.py
+++ b/solution.py
@@ -127,21 +127,24 @@
     )(place, picks, design)
 
 
-def gram_kernel(local_terms, devices, has_prior, place, picks, slots, other, *refs):
-    own = other.shape[0] != refs[-1].shape[0]
+def gram_kernel(local_terms, devices, own, has_prior, place, order, slots, other, *refs):
     prior = refs[0] if has_prior else None
-    basis, sums = refs[-2:]
-    owned, rank = owners(as_line(picks), devices, local_terms)
-    first = lax.broadcasted_iota(jnp.int32, owned.shape, 0).astype(F32) * SLOTS
-    slot = jnp.sum(owned * rank, axis=0, keepdims=True)
-    slot = slot - (place[1] * SLOTS).astype(F32)
-    target = slot + jnp.sum(owned * first, axis=0, keepdims=True)
-    target = jnp.where((slot >= 0.0) & (slot < SLOTS), target, -1.0)
-    count = target.shape[1]
-    lines = lax.broadcasted_iota(jnp.int32, (devices * SLOTS, count), 0).astype(F32)
-    moved = (lines == target).astype(F32).astype(BF16)
+    basis, sums = refs[has_prior : has_prior + 2]
+    if own:
+        moved = refs[-1]
+        owned, rank = owners(as_line(order), devices, local_terms)
+        first = lax.broadcasted_iota(jnp.int32, owned.shape, 0).astype(F32) * SLOTS
+        slot = jnp.sum(owned * rank, axis=0, keepdims=True)
+        slot = slot - (place[1] * SLOTS).astype(F32)
+        target = slot + jnp.sum(owned * first, axis=0, keepdims=True)
+        target = jnp.where((slot >= 0.0) & (slot < SLOTS), target, -1.0)
+        lines = lax.broadcasted_iota(jnp.int32, moved.shape, 0).astype(F32)
+        moved[...] = (lines == target).astype(F32).astype(BF16)
+    else:
+        moved = order
+    count = moved.shape[1]
     columns = lax.dot_general(
-        moved, slots[...], (((0,), (0,)), ((), ())), preferred_element_type=F32
+        moved[...], slots[...], (((0,), (0,)), ((), ())), preferred_element_type=F32
     )
     if has_prior:
         columns = columns + prior[...].astype(F32)
@@ -175,20 +178,23 @@
         pl.when(place[2] == side)(functools.partial(fill, side))
 
 
-def gram(place, picks, slots, other, local_terms, half, prior=None):
+def gram(place, order, slots, other, local_terms, half, own, prior=None):
     devices, _, rows = slots.shape
-    count = picks.size
+    count = order.size if own else order.shape[1]
     extra = () if prior is None else (prior,)
-    operands = (place, picks, slots.reshape(-1, rows), other, *extra)
+    operands = (place, order, slots.reshape(-1, rows), other, *extra)
+    shapes = (
+        jax.ShapeDtypeStruct((count, rows), BF16),
+        jax.ShapeDtypeStruct((half, LANES), F32),
+        jax.ShapeDtypeStruct((devices * SLOTS, count), BF16),
+    )
+    shapes = shapes if own else shapes[:2]
     return call(
-        functools.partial(gram_kernel, local_terms, devices, prior is not None),
+        functools.partial(gram_kernel, local_terms, devices, own, prior is not None),
         "gram",
-        (
-            jax.ShapeDtypeStruct((count, rows), BF16),
-            jax.ShapeDtypeStruct((half, LANES), F32),
-        ),
+        shapes,
         [SCALAR] + [WHOLE] * (len(operands) - 1),
-        (WHOLE, WHOLE),
+        (WHOLE,) * len(shapes),
         cost_estimate=pl.CostEstimate(
             flops=2 * count * rows * (devices * SLOTS + count),
             bytes_accessed=2 * count * rows,
@@ -432,11 +438,11 @@
 
     def grams(where, slots, prior=(None, None)):
         partner_slots = lax.ppermute(slots, "runs", swap)
-        basis, sums = gram(
-            where, picks, slots, responses, local_terms, half, prior[0]
+        basis, sums, order = gram(
+            where, picks, slots, responses, local_terms, half, True, prior[0]
         )
         partner_basis, sums = gram(
-            where, picks, partner_slots, sums, local_terms, half, prior[1]
+            where, order, partner_slots, sums, local_terms, half, False, prior[1]
         )
         return basis, partner_basis, sums
 

time: 138 us -> 138 us (level)
  no operation moved by 1% of the time
where the time goes in v8:
time: 138 us
  blocking collectives  99.8 us (72%)
  Pallas kernels  24.7 us (18%)
  starting transfers between devices  11.2 us (8%)
    all_to_all x5, blocking collectives, exchange(): return lax.all_to_all(pieces, axis, 0, 0, axis_index_groups=groups)  99.8 us
    pallas_call x1, Pallas kernels, finish(): call(functools.partial(finish_kernel, scale), 'finish', (jax.ShapeDtypeSt...  14 us
    ppermute x1, starting transfers between devices, grams(): partner_slots = lax.ppermute(slots, 'runs', swap)  6.02 us
    ppermute x1, starting transfers between devices, local(): other = lax.ppermute(mine, 'runs', swap)  5.17 us
    pallas_call x1, Pallas kernels, pack(): call(pack_kernel, 'pack', (jax.ShapeDtypeStruct((devices, SLOTS, rows), B...  3.86 us
    pallas_call x2, Pallas kernels, gram(): call(functools.partial(gram_kernel, local_terms, devices, own, prior is n...  3.46 us
    pallas_call x1, Pallas kernels, first_inverse(): call(first_kernel, 'first_inverse', jax.ShapeDtypeStruct((BLOCK, BLOCK),...  3.18 us
  transfers between devices with their start and end apart: 2, of which 0 were waited for; matrix products, arithmetic and copies ran while one was open for 0% of the time, Pallas kernels for 3%

profile of v8, /device:TPU:1, one launch (start us, length us, event | category | flops | bytes accessed | tf_op | source)
XLA Modules:
  0.0 137.9 jit_solution(11689090990000742410)
XLA Ops:
  0.6 0.0 copy-start.1
  0.6 0.0 copy-start.2
  0.7 0.1 pad_add_fusion.1.place
  0.7 3.9 %pack.2 = (bf16[8,96,256]{2,1,0:T(8,128)(2,1)S(1)}, s32[1]{0:T(128)}) custom-call(s32[3]{0:T(128)S(1)} %pad_add_fusion.1.place, s32[2,256]{1,0:T(2,128)} %order.1, bf16[256,6656]{1,0:T(8,128)(2,1)} %refs_5_.1), custom_call_target="tpu_custom_call" | custom-call | tf_op jit(solution)/shard_map/pack/pallas_call | solution.py:113
  4.6 24.6 %all_to_all.31 = bf16[8,96,256]{2,1,0:T(8,128)(2,1)S(1)} all-to-all(bf16[8,96,256]{2,1,0:T(8,128)(2,1)S(1)} %get-tuple-element.65), channel_id=1, replica_groups=mesh['runs'=64,'terms'=8] {'terms'}, dimensions={0} | all-to-all | bytes 786432 | tf_op jit(solution)/shard_map/all_to_all | solution.py:48
  29.2 6.0 %collective-permute-start.1 = (bf16[8,96,256]{2,1,0:T(8,128)(2,1)S(1)}, bf16[8,96,256]{2,1,0:T(8,128)(2,1)S(1)}, u32[]{:S(2)}, u32[]{:S(2)}) collective-permute-start(bf16[8,96,256]{2,1,0:T(8,128)(2,1)S(1)} %all_to_all.31), channel_id=1, source_target_pairs={{0,8},{8,0},{16,24},{24,16},{32,40},{40,32},{48,56},{56,48},{64,72... | collective-permute-start | bytes 1179656 | tf_op jit(solution)/shard_map/ppermute | solution.py:440
  35.2 0.0 copy-done.1
  35.3 0.0 copy-done.2
  35.3 1.5 %gram.4 = (bf16[512,256]{1,0:T(8,128)(2,1)S(1)}, f32[768,128]{1,0:T(8,128)S(1)}, bf16[768,512]{1,0:T(8,128)(2,1)S(1)}) custom-call(s32[3]{0:T(128)S(1)} %pad_add_fusion.1.place, s32[2,256]{1,0:T(2,128)S(1)} %copy-done.1, bf16[768,256]{1,0:T(8,128)(2,1)S(1)} %bitcast.32, f32[8,256]{1,0:T(8,128)S(1)} %copy-done.2), custom_call_target="tpu_custom_call" | custom-call | flops 335544320 | bytes 262144 | tf_op jit(solution)/shard_map/gram/pallas_call | solution.py:192
  36.8 0.0 collective-permute-done.1
  36.8 2.0 %gram.5 = (bf16[512,256]{1,0:T(8,128)(2,1)S(1)}, f32[768,128]{1,0:T(8,128)}) custom-call(s32[3]{0:T(128)S(1)} %pad_add_fusion.1.place, bf16[768,512]{1,0:T(8,128)(2,1)S(1)} %get-tuple-element.67.order, bf16[768,256]{1,0:T(8,128)(2,1)S(1)} %bitcast.33, f32[768,128]{1,0:T(8,128)S(1)} %get-tuple-element.68.other), custom_call_target="tpu_custom_call" | custom-call | flops 335544320 | bytes 262144 | tf_op jit(solution)/shard_map/gram/pallas_call | solution.py:192
  38.7 0.7 while.14
  39.4 23.3 %all_to_all.32.pieces = f32[32,24,128]{2,1,0:T(8,128)S(1)} all-to-all(f32[32,24,128]{2,1,0:T(8,128)} %bitcast.34), channel_id=1, replica_groups={{0,16,32,48,64,80,96,112,128,144,160,176,192,208,224,240,256,272,288,30..., dimensions={0} | all-to-all | bytes 786432 | tf_op jit(solution)/shard_map/all_to_all | solution.py:48
  62.8 0.1 totals.2
  62.8 19.2 %all_to_all.33 = f32[32,24,128]{2,1,0:T(8,128)S(1)} all-to-all(f32[32,24,128]{2,1,0:T(8,128)S(1)} %totals.2), channel_id=1, replica_groups={{0,16,32,48,64,80,96,112,128,144,160,176,192,208,224,240,256,272,288,30..., dimensions={0} | all-to-all | bytes 786432 | tf_op jit(solution)/shard_map/all_to_all | solution.py:48
  82.0 0.0 copy-start
  82.0 5.2 %collective-permute-start.2 = (f32[768,128]{1,0:T(8,128)S(1)}, f32[768,128]{1,0:T(8,128)S(1)}, u32[]{:S(2)}, u32[]{:S(2)}) collective-permute-start(f32[768,128]{1,0:T(8,128)S(1)} %bitcast.29), channel_id=1, source_target_pairs={{0,8},{8,0},{16,24},{24,16},{32,40},{40,32},{48,56},{56,48},{64,72... | collective-permute-start | bytes 1179656 | tf_op jit(solution)/shard_map/ppermute | solution.py:463
  87.2 3.2 %first_inverse.1.refs_2_ = f32[128,128]{1,0:T(8,128)S(1)} custom-call(f32[768,128]{1,0:T(8,128)S(1)} %bitcast.30), custom_call_target="tpu_custom_call" | custom-call | flops 2000000000 | bytes 100000 | tf_op jit(solution)/shard_map/first_inverse/pallas_call | solution.py:320
  90.4 0.0 collective-permute-done.2.refs_1_
  90.4 0.0 copy-done
  90.4 14.0 %finish.1 = (f32[8,256]{1,0:T(8,128)}, f32[64,8,128]{2,1,0:T(8,128)S(1)}) custom-call(s32[3]{0:T(128)S(1)} %pad_add_fusion.1.place, f32[768,128]{1,0:T(8,128)S(1)} %bitcast.31, f32[768,128]{1,0:T(8,128)S(1)} %collective-permute-done.2.refs_1_, f32[128,128]{1,0:T(8,128)S(1)} %first_inverse.1.refs_2_, f32[8,256]{1,0:T(8,128)S(1)} %get-tuple-element.200, ...), custom_call_target="tpu_custom_call" | custom-call | tf_op jit(solution)/shard_map/finish/pallas_call | solution.py:402
  104.4 17.4 %all_to_all.34.pieces = f32[64,8,128]{2,1,0:T(8,128)S(1)} all-to-all(f32[64,8,128]{2,1,0:T(8,128)S(1)} %get-tuple-element.75), channel_id=1, replica_groups=mesh['runs'=64,'terms'=8] {'runs'}, dimensions={0} | all-to-all | bytes 524288 | tf_op jit(solution)/shard_map/all_to_all | solution.py:48
  121.8 0.1 totals.3
  121.9 15.3 %all_to_all.35 = bf16[64,8,128]{2,1,0:T(8,128)(2,1)S(1)} all-to-all(bf16[64,8,128]{2,1,0:T(8,128)(2,1)S(1)} %totals.3), channel_id=1, replica_groups=mesh['runs'=64,'terms'=8] {'runs'}, dimensions={0} | all-to-all | bytes 262144 | tf_op jit(solution)/shard_map/all_to_all | solution.py:48
  137.2 0.7 convert_bitcast_fusion
Async XLA Ops:
  0.6 34.6 %copy-start.1 = (s32[2,256]{1,0:T(2,128)S(1)}, s32[2,256]{1,0:T(2,128)}, u32[]{:S(2)}) copy-start(s32[2,256]{1,0:T(2,128)} %order.1) | copy-start | bytes 6148
  0.6 34.6 %copy-start.2 = (f32[8,256]{1,0:T(8,128)S(1)}, f32[8,256]{1,0:T(8,128)}, u32[]{:S(2)}) copy-start(f32[8,256]{1,0:T(8,128)} %refs_3_.1) | copy-start | bytes 24580
  29.2 7.6 %collective-permute-start.1 = (bf16[8,96,256]{2,1,0:T(8,128)(2,1)S(1)}, bf16[8,96,256]{2,1,0:T(8,128)(2,1)S(1)}, u32[]{:S(2)}, u32[]{:S(2)}) collective-permute-start(bf16[8,96,256]{2,1,0:T(8,128)(2,1)S(1)} %all_to_all.31), channel_id=1, source_target_pairs={{0,8},{8,0},{16,24},{24,16},{32,40},{40,32},{48,56},{56,48},{64,72... | collective-permute-start | bytes 1179656 | tf_op jit(solution)/shard_map/ppermute | solution.py:440
  82.0 8.4 %copy-start = (bf16[256,6656]{1,0:T(8,128)(2,1)S(1)}, bf16[256,6656]{1,0:T(8,128)(2,1)}, u32[]{:S(2)}) copy-start(bf16[256,6656]{1,0:T(8,128)(2,1)} %get-tuple-element.199) | copy-start | bytes 10223620
  82.0 8.4 %collective-permute-start.2 = (f32[768,128]{1,0:T(8,128)S(1)}, f32[768,128]{1,0:T(8,128)S(1)}, u32[]{:S(2)}, u32[]{:S(2)}) collective-permute-start(f32[768,128]{1,0:T(8,128)S(1)} %bitcast.29), channel_id=1, source_target_pairs={{0,8},{8,0},{16,24},{24,16},{32,40},{40,32},{48,56},{56,48},{64,72... | collective-permute-start | bytes 1179656 | tf_op jit(solution)/shard_map/ppermute | solution.py:463

commit v9 on v7

--- a/solution.py
+++ b/solution.py
@@ -127,25 +127,39 @@
     )(place, picks, design)
 
 
-def gram_kernel(local_terms, devices, has_prior, place, picks, slots, other, *refs):
-    own = other.shape[0] != refs[-1].shape[0]
-    prior = refs[0] if has_prior else None
-    basis, sums = refs[-2:]
+def unpack_kernel(local_terms, devices, place, picks, slots, *refs):
     owned, rank = owners(as_line(picks), devices, local_terms)
     first = lax.broadcasted_iota(jnp.int32, owned.shape, 0).astype(F32) * SLOTS
     slot = jnp.sum(owned * rank, axis=0, keepdims=True)
     slot = slot - (place[1] * SLOTS).astype(F32)
     target = slot + jnp.sum(owned * first, axis=0, keepdims=True)
     target = jnp.where((slot >= 0.0) & (slot < SLOTS), target, -1.0)
-    count = target.shape[1]
-    lines = lax.broadcasted_iota(jnp.int32, (devices * SLOTS, count), 0).astype(F32)
+    shape = (slots.shape[0], target.shape[1])
+    lines = lax.broadcasted_iota(jnp.int32, shape, 0).astype(F32)
     moved = (lines == target).astype(F32).astype(BF16)
     columns = lax.dot_general(
         moved, slots[...], (((0,), (0,)), ((), ())), preferred_element_type=F32
     )
-    if has_prior:
-        columns = columns + prior[...].astype(F32)
-    basis[...] = columns.astype(BF16)
+    for earlier in refs[:-1]:
+        columns = columns + earlier[...].astype(F32)
+    refs[-1][...] = columns.astype(BF16)
+
+
+def unpack(place, picks, slots, local_terms, *earlier):
+    devices, _, rows = slots.shape
+    operands = (place, picks, slots.reshape(-1, rows), *earlier)
+    return call(
+        functools.partial(unpack_kernel, local_terms, devices),
+        "unpack",
+        jax.ShapeDtypeStruct((picks.size, rows), BF16),
+        [SCALAR] + [WHOLE] * (len(operands) - 1),
+        WHOLE,
+    )(*operands)
+
+
+def gram_kernel(place, basis, other, sums):
+    own = other.shape[0] != sums.shape[0]
+    count = basis.shape[0]
 
     def fill(side):
         row = 0
@@ -175,26 +189,20 @@
         pl.when(place[2] == side)(functools.partial(fill, side))
 
 
-def gram(place, picks, slots, other, local_terms, half, prior=None):
-    devices, _, rows = slots.shape
-    count = picks.size
-    extra = () if prior is None else (prior,)
-    operands = (place, picks, slots.reshape(-1, rows), other, *extra)
+def gram(place, basis, other, half):
+    count, rows = basis.shape
     return call(
-        functools.partial(gram_kernel, local_terms, devices, prior is not None),
+        gram_kernel,
         "gram",
-        (
-            jax.ShapeDtypeStruct((count, rows), BF16),
-            jax.ShapeDtypeStruct((half, LANES), F32),
-        ),
-        [SCALAR] + [WHOLE] * (len(operands) - 1),
-        (WHOLE, WHOLE),
+        jax.ShapeDtypeStruct((half, LANES), F32),
+        [SCALAR, WHOLE, WHOLE],
+        WHOLE,
         cost_estimate=pl.CostEstimate(
-            flops=2 * count * rows * (devices * SLOTS + count),
+            flops=2 * count * rows * 1024,
             bytes_accessed=2 * count * rows,
             transcendentals=0,
         ),
-    )(*operands)
+    )(place, basis, other)
 
 
 def split(value):
@@ -430,27 +438,21 @@
         packed, most = pack(where, picks, design, term_devices)
         return where, exchange(packed, "terms"), most
 
-    def grams(where, slots, prior=(None, None)):
-        partner_slots = lax.ppermute(slots, "runs", swap)
-        basis, sums = gram(
-            where, picks, slots, responses, local_terms, half, prior[0]
-        )
-        partner_basis, sums = gram(
-            where, picks, partner_slots, sums, local_terms, half, prior[1]
-        )
-        return basis, partner_basis, sums
-
     at, slots, most = fetch(0)
-    state = grams(at, slots)
 
     def another(carry):
-        turn, basis, partner_basis, _ = carry
+        turn, basis = carry
         where, more, _ = fetch(turn)
-        return turn + 1, *grams(where, more, (basis, partner_basis))
-
-    _, basis, _, sums = lax.while_loop(
-        lambda carry: carry[0] * SLOTS < most[0], another, (jnp.int32(1), *state)
-    )
+        return turn + 1, unpack(where, picks, more, local_terms, basis)
+
+    _, basis = lax.while_loop(
+        lambda carry: carry[0] * SLOTS < most[0],
+        another,
+        (jnp.int32(1), unpack(at, picks, slots, local_terms)),
+    )
+
+    partner = lax.ppermute(basis, "runs", swap)
+    sums = gram(at, partner, gram(at, basis, responses, half), half)
 
     mine = summed_everywhere(sums.reshape(chips, -1, LANES), "runs", sides)
     mine = mine.reshape(half, LANES)

time: 138 us -> 138 us (level)
  blocking collectives: 99.7 us -> 74.3 us
  starting transfers between devices: 11.3 us -> 25.5 us
  waiting for transfers between devices: 0.01 us -> 10.9 us
    all_to_all x5 -> x4, blocking collectives: 99.7 us -> 74.3 us  [exchange(): return lax.all_to_all(pieces, axis, 0, 0, axis_index_groups=groups)]
    all_to_all x0 -> x1, starting transfers between devices: none -> 13.3 us  [exchange(): return lax.all_to_all(pieces, axis, 0, 0, axis_index_groups=groups)]
    all_to_all x0 -> x1, waiting for transfers between devices: none -> 10.6 us  [exchange(): return lax.all_to_all(pieces, axis, 0, 0, axis_index_groups=groups)]
    pallas_call x2 -> x3, Pallas kernels: 3.52 us -> 2.77 us  [the longest x2 1.65 us: gram(): call(gram_kernel, 'gram', jax.ShapeDtypeStruct((half, LANES), F32), [SCAL...]
  transfers between devices with their start and end apart: 2 -> 3, of which waited for: 0 -> 2; matrix products, arithmetic and copies ran while one was open for 0% -> 0% of each run, Pallas kernels for 3% -> 3%
where the time goes in v9:
time: 138 us; the launch traced here: 137 us
  blocking collectives  74.3 us (54%)
  starting transfers between devices  25.5 us (18%)
  Pallas kernels  24.5 us (18%)
  waiting for transfers between devices  10.9 us (8%)
    all_to_all x4, blocking collectives, exchange(): return lax.all_to_all(pieces, axis, 0, 0, axis_index_groups=groups)  74.3 us
    pallas_call x1, Pallas kernels, finish(): call(functools.partial(finish_kernel, scale), 'finish', (jax.ShapeDtypeSt...  13.9 us
    all_to_all x1, starting transfers between devices, exchange(): return lax.all_to_all(pieces, axis, 0, 0, axis_index_groups=groups)  13.3 us
    all_to_all x1, waiting for transfers between devices, exchange(): return lax.all_to_all(pieces, axis, 0, 0, axis_index_groups=groups)  10.6 us
    ppermute x1, starting transfers between devices, local(): partner = lax.ppermute(basis, 'runs', swap)  6.96 us
    ppermute x1, starting transfers between devices, local(): other = lax.ppermute(mine, 'runs', swap)  5.23 us
    pallas_call x1, Pallas kernels, pack(): call(pack_kernel, 'pack', (jax.ShapeDtypeStruct((devices, SLOTS, rows), B...  4.6 us
    pallas_call x1, Pallas kernels, first_inverse(): call(first_kernel, 'first_inverse', jax.ShapeDtypeStruct((BLOCK, BLOCK),...  3.18 us
  transfers between devices with their start and end apart: 3, of which 2 were waited for; matrix products, arithmetic and copies ran while one was open for 0% of the time, Pallas kernels for 3%

profile of v9, /device:TPU:1, one launch (start us, length us, event | category | flops | bytes accessed | tf_op | source)
XLA Modules:
  0.0 137.4 jit_solution(4004455283091324525)
XLA Ops:
  0.6 0.0 copy-start.2
  0.7 0.1 pad_add_fusion.1.place
  0.7 4.6 %pack.2 = (bf16[8,96,256]{2,1,0:T(8,128)(2,1)}, s32[1]{0:T(128)}) custom-call(s32[3]{0:T(128)S(1)} %pad_add_fusion.1.place, s32[2,256]{1,0:T(2,128)} %picks.3, bf16[256,6656]{1,0:T(8,128)(2,1)} %refs_5_.1), custom_call_target="tpu_custom_call" | custom-call | tf_op jit(solution)/shard_map/pack/pallas_call | solution.py:113
  5.3 13.3 %all-to-all-start.1 = ((bf16[8,96,256]{2,1,0:T(8,128)(2,1)}), bf16[8,96,256]{2,1,0:T(8,128)(2,1)S(1)}, u32[]{:S(2)}, u32[]{:S(2)}) async-start(bf16[8,96,256]{2,1,0:T(8,128)(2,1)} %get-tuple-element.40), calls=%async_computation.1 | async-start | bytes 786432 | tf_op jit(solution)/shard_map/all_to_all | solution.py:48
  18.6 10.6 %all-to-all-done.1 = bf16[8,96,256]{2,1,0:T(8,128)(2,1)S(1)} async-done(((bf16[8,96,256]{2,1,0:T(8,128)(2,1)}), bf16[8,96,256]{2,1,0:T(8,128)(2,1)S(1)}, u32[]{:S(2)}, u32[]{:S(2)}) %all-to-all-start.1) | async-done | bytes 393248 | tf_op jit(solution)/shard_map/all_to_all | solution.py:48
  29.2 0.0 copy-done.2
  29.2 1.1 unpack.2
  30.4 0.0 copy-start
  30.4 0.7 while.10
  31.1 7.0 %collective-permute-start = (bf16[512,256]{1,0:T(8,128)(2,1)S(1)}, bf16[512,256]{1,0:T(8,128)(2,1)S(1)}, u32[]{:S(2)}, u32[]{:S(2)}) collective-permute-start(bf16[512,256]{1,0:T(8,128)(2,1)S(1)} %get-tuple-element.42.basis.refs_4_), channel_id=1, source_target_pairs={{0,8},{8,0},{16,24},{24,16},{32,40},{40,32},{48,56},{56,48},{64,72... | collective-permute-start | bytes 786440 | tf_op jit(solution)/shard_map/ppermute | solution.py:454
  38.0 0.0 copy-done
  38.0 0.8 gram.2.other
  38.9 0.3 collective-permute-done.basis
  39.2 0.8 gram.3
  40.0 22.5 %all_to_all.31.pieces = f32[32,24,128]{2,1,0:T(8,128)S(1)} all-to-all(f32[32,24,128]{2,1,0:T(8,128)S(1)} %bitcast.28), channel_id=1, replica_groups={{0,16,32,48,64,80,96,112,128,144,160,176,192,208,224,240,256,272,288,30..., dimensions={0} | all-to-all | bytes 786432 | tf_op jit(solution)/shard_map/all_to_all | solution.py:48
  62.5 0.1 totals.2
  62.6 19.0 %all_to_all.32 = f32[32,24,128]{2,1,0:T(8,128)S(1)} all-to-all(f32[32,24,128]{2,1,0:T(8,128)S(1)} %totals.2), channel_id=1, replica_groups={{0,16,32,48,64,80,96,112,128,144,160,176,192,208,224,240,256,272,288,30..., dimensions={0} | all-to-all | bytes 786432 | tf_op jit(solution)/shard_map/all_to_all | solution.py:48
  81.6 0.0 copy-start.1
  81.6 5.2 %collective-permute-start.1 = (f32[768,128]{1,0:T(8,128)S(1)}, f32[768,128]{1,0:T(8,128)S(1)}, u32[]{:S(2)}, u32[]{:S(2)}) collective-permute-start(f32[768,128]{1,0:T(8,128)S(1)} %bitcast.24), channel_id=1, source_target_pairs={{0,8},{8,0},{16,24},{24,16},{32,40},{40,32},{48,56},{56,48},{64,72... | collective-permute-start | bytes 1179656 | tf_op jit(solution)/shard_map/ppermute | solution.py:459
  86.8 3.2 %first_inverse.1.refs_2_ = f32[128,128]{1,0:T(8,128)S(1)} custom-call(f32[768,128]{1,0:T(8,128)S(1)} %bitcast.25), custom_call_target="tpu_custom_call" | custom-call | flops 2000000000 | bytes 100000 | tf_op jit(solution)/shard_map/first_inverse/pallas_call | solution.py:322
  90.0 0.0 collective-permute-done.1.refs_1_
  90.0 0.0 copy-done.1
  90.0 13.9 %finish.1 = (f32[8,256]{1,0:T(8,128)}, f32[64,8,128]{2,1,0:T(8,128)S(1)}) custom-call(s32[3]{0:T(128)S(1)} %pad_add_fusion.1.place, f32[768,128]{1,0:T(8,128)S(1)} %bitcast.26, f32[768,128]{1,0:T(8,128)S(1)} %collective-permute-done.1.refs_1_, f32[128,128]{1,0:T(8,128)S(1)} %first_inverse.1.refs_2_, f32[8,256]{1,0:T(8,128)S(1)} %copy-done, ...), custom_call_target="tpu_custom_call" | custom-call | tf_op jit(solution)/shard_map/finish/pallas_call | solution.py:404
  103.9 17.4 %all_to_all.33.pieces = f32[64,8,128]{2,1,0:T(8,128)S(1)} all-to-all(f32[64,8,128]{2,1,0:T(8,128)S(1)} %get-tuple-element.44), channel_id=1, replica_groups=mesh['runs'=64,'terms'=8] {'runs'}, dimensions={0} | all-to-all | bytes 524288 | tf_op jit(solution)/shard_map/all_to_all | solution.py:48
  121.3 0.1 totals.3
  121.4 15.3 %all_to_all.34 = bf16[64,8,128]{2,1,0:T(8,128)(2,1)S(1)} all-to-all(bf16[64,8,128]{2,1,0:T(8,128)(2,1)S(1)} %totals.3), channel_id=1, replica_groups=mesh['runs'=64,'terms'=8] {'runs'}, dimensions={0} | all-to-all | bytes 262144 | tf_op jit(solution)/shard_map/all_to_all | solution.py:48
  136.7 0.7 convert_bitcast_fusion
Async XLA Ops:
  0.6 28.6 %copy-start.2 = (s32[2,256]{1,0:T(2,128)S(1)}, s32[2,256]{1,0:T(2,128)}, u32[]{:S(2)}) copy-start(s32[2,256]{1,0:T(2,128)} %picks.3) | copy-start | bytes 6148
  5.3 23.9 %all-to-all-start.1 = ((bf16[8,96,256]{2,1,0:T(8,128)(2,1)}), bf16[8,96,256]{2,1,0:T(8,128)(2,1)S(1)}, u32[]{:S(2)}, u32[]{:S(2)}) async-start(bf16[8,96,256]{2,1,0:T(8,128)(2,1)} %get-tuple-element.40), calls=%async_computation.1 | async-start | bytes 786432 | tf_op jit(solution)/shard_map/all_to_all | solution.py:48
  30.4 7.7 %copy-start = (f32[8,256]{1,0:T(8,128)S(1)}, f32[8,256]{1,0:T(8,128)}, u32[]{:S(2)}) copy-start(f32[8,256]{1,0:T(8,128)} %refs_3_.1) | copy-start | bytes 24580
  31.1 8.1 %collective-permute-start = (bf16[512,256]{1,0:T(8,128)(2,1)S(1)}, bf16[512,256]{1,0:T(8,128)(2,1)S(1)}, u32[]{:S(2)}, u32[]{:S(2)}) collective-permute-start(bf16[512,256]{1,0:T(8,128)(2,1)S(1)} %get-tuple-element.42.basis.refs_4_), channel_id=1, source_target_pairs={{0,8},{8,0},{16,24},{24,16},{32,40},{40,32},{48,56},{56,48},{64,72... | collective-permute-start | bytes 786440 | tf_op jit(solution)/shard_map/ppermute | solution.py:454
  81.6 8.4 %copy-start.1 = (bf16[256,6656]{1,0:T(8,128)(2,1)S(1)}, bf16[256,6656]{1,0:T(8,128)(2,1)}, u32[]{:S(2)}) copy-start(bf16[256,6656]{1,0:T(8,128)(2,1)} %get-tuple-element.126) | copy-start | bytes 10223620
  81.6 8.4 %collective-permute-start.1 = (f32[768,128]{1,0:T(8,128)S(1)}, f32[768,128]{1,0:T(8,128)S(1)}, u32[]{:S(2)}, u32[]{:S(2)}) collective-permute-start(f32[768,128]{1,0:T(8,128)S(1)} %bitcast.24), channel_id=1, source_target_pairs={{0,8},{8,0},{16,24},{24,16},{32,40},{40,32},{48,56},{56,48},{64,72... | collective-permute-start | bytes 1179656 | tf_op jit(solution)/shard_map/ppermute | solution.py:459

commit v10 on v9

--- a/solution.py
+++ b/solution.py
@@ -439,6 +439,7 @@
         return where, exchange(packed, "terms"), most
 
     at, slots, most = fetch(0)
+    first, slots = lax.optimization_barrier((jnp.int32(1), slots))
 
     def another(carry):
         turn, basis = carry
@@ -448,7 +449,7 @@
     _, basis = lax.while_loop(
         lambda carry: carry[0] * SLOTS < most[0],
         another,
-        (jnp.int32(1), unpack(at, picks, slots, local_terms)),
+        (first, unpack(at, picks, slots, local_terms)),
     )
 
     partner = lax.ppermute(basis, "runs", swap)

time: 138 us -> 137 us (level)
  blocking collectives: 74.3 us -> 99.5 us
  starting transfers between devices: 25.5 us -> 11.3 us
  waiting for transfers between devices: 10.9 us -> 0.29 us
    all_to_all x4 -> x5, blocking collectives: 74.3 us -> 99.5 us  [exchange(): return lax.all_to_all(pieces, axis, 0, 0, axis_index_groups=groups)]
    all_to_all x1 -> x0, starting transfers between devices: 13.3 us -> none  [exchange(): return lax.all_to_all(pieces, axis, 0, 0, axis_index_groups=groups)]
    all_to_all x1 -> x0, waiting for transfers between devices: 10.6 us -> none  [exchange(): return lax.all_to_all(pieces, axis, 0, 0, axis_index_groups=groups)]
  transfers between devices with their start and end apart: 3 -> 2, of which waited for: 2 -> 1; matrix products, arithmetic and copies ran while one was open for 0% -> 0% of each run, Pallas kernels for 3% -> 3%
where the time goes in v10:
time: 137 us
  blocking collectives  99.5 us (73%)
  Pallas kernels  23.8 us (17%)
  starting transfers between devices  11.3 us (8%)
    all_to_all x5, blocking collectives, exchange(): return lax.all_to_all(pieces, axis, 0, 0, axis_index_groups=groups)  99.5 us
    pallas_call x1, Pallas kernels, finish(): call(functools.partial(finish_kernel, scale), 'finish', (jax.ShapeDtypeSt...  13.9 us
    ppermute x1, starting transfers between devices, local(): partner = lax.ppermute(basis, 'runs', swap)  6.03 us
    ppermute x1, starting transfers between devices, local(): other = lax.ppermute(mine, 'runs', swap)  5.23 us
    pallas_call x1, Pallas kernels, pack(): call(pack_kernel, 'pack', (jax.ShapeDtypeStruct((devices, SLOTS, rows), B...  3.86 us
    pallas_call x1, Pallas kernels, first_inverse(): call(first_kernel, 'first_inverse', jax.ShapeDtypeStruct((BLOCK, BLOCK),...  3.18 us
  transfers between devices with their start and end apart: 2, of which 1 were waited for; matrix products, arithmetic and copies ran while one was open for 0% of the time, Pallas kernels for 3%

profile of v10, /device:TPU:1, one launch (start us, length us, event | category | flops | bytes accessed | tf_op | source)
XLA Modules:
  0.0 137.0 jit_solution(2070567353974653723)
XLA Ops:
  0.6 0.0 copy-start.2
  0.7 0.1 pad_add_fusion.1.place
  0.7 3.9 %pack.2 = (bf16[8,96,256]{2,1,0:T(8,128)(2,1)S(1)}, s32[1]{0:T(128)}) custom-call(s32[3]{0:T(128)S(1)} %pad_add_fusion.1.place, s32[2,256]{1,0:T(2,128)} %picks.3, bf16[256,6656]{1,0:T(8,128)(2,1)} %refs_5_.1), custom_call_target="tpu_custom_call" | custom-call | tf_op jit(solution)/shard_map/pack/pallas_call | solution.py:113
  4.6 24.6 %all_to_all.31 = bf16[8,96,256]{2,1,0:T(8,128)(2,1)S(1)} all-to-all(bf16[8,96,256]{2,1,0:T(8,128)(2,1)S(1)} %get-tuple-element.42), channel_id=1, replica_groups=mesh['runs'=64,'terms'=8] {'terms'}, dimensions={0} | all-to-all | bytes 786432 | tf_op jit(solution)/shard_map/all_to_all | solution.py:48
  29.2 0.0 copy-done.2
  29.2 1.1 unpack.2
  30.3 0.0 copy-start
  30.3 0.6 while.10
  31.0 6.0 %collective-permute-start = (bf16[512,256]{1,0:T(8,128)(2,1)S(1)}, bf16[512,256]{1,0:T(8,128)(2,1)S(1)}, u32[]{:S(2)}, u32[]{:S(2)}) collective-permute-start(bf16[512,256]{1,0:T(8,128)(2,1)S(1)} %get-tuple-element.46.basis.refs_4_), channel_id=1, source_target_pairs={{0,8},{8,0},{16,24},{24,16},{32,40},{40,32},{48,56},{56,48},{64,72... | collective-permute-start | bytes 786440 | tf_op jit(solution)/shard_map/ppermute | solution.py:455
  37.0 0.0 copy-done
  37.0 0.8 gram.2.other
  37.9 0.3 collective-permute-done.basis
  38.1 0.8 gram.3
  39.0 23.2 %all_to_all.32.pieces = f32[32,24,128]{2,1,0:T(8,128)S(1)} all-to-all(f32[32,24,128]{2,1,0:T(8,128)S(1)} %bitcast.28), channel_id=1, replica_groups={{0,16,32,48,64,80,96,112,128,144,160,176,192,208,224,240,256,272,288,30..., dimensions={0} | all-to-all | bytes 786432 | tf_op jit(solution)/shard_map/all_to_all | solution.py:48
  62.1 0.1 totals.2
  62.2 19.0 %all_to_all.33 = f32[32,24,128]{2,1,0:T(8,128)S(1)} all-to-all(f32[32,24,128]{2,1,0:T(8,128)S(1)} %totals.2), channel_id=1, replica_groups={{0,16,32,48,64,80,96,112,128,144,160,176,192,208,224,240,256,272,288,30..., dimensions={0} | all-to-all | bytes 786432 | tf_op jit(solution)/shard_map/all_to_all | solution.py:48
  81.2 0.0 copy-start.1
  81.2 5.2 %collective-permute-start.1 = (f32[768,128]{1,0:T(8,128)S(1)}, f32[768,128]{1,0:T(8,128)S(1)}, u32[]{:S(2)}, u32[]{:S(2)}) collective-permute-start(f32[768,128]{1,0:T(8,128)S(1)} %bitcast.24), channel_id=1, source_target_pairs={{0,8},{8,0},{16,24},{24,16},{32,40},{40,32},{48,56},{56,48},{64,72... | collective-permute-start | bytes 1179656 | tf_op jit(solution)/shard_map/ppermute | solution.py:460
  86.5 3.2 %first_inverse.1.refs_2_ = f32[128,128]{1,0:T(8,128)S(1)} custom-call(f32[768,128]{1,0:T(8,128)S(1)} %bitcast.25), custom_call_target="tpu_custom_call" | custom-call | flops 2000000000 | bytes 100000 | tf_op jit(solution)/shard_map/first_inverse/pallas_call | solution.py:322
  89.6 0.0 collective-permute-done.1.refs_1_
  89.7 0.0 copy-done.1
  89.7 13.9 %finish.1 = (f32[8,256]{1,0:T(8,128)}, f32[64,8,128]{2,1,0:T(8,128)S(1)}) custom-call(s32[3]{0:T(128)S(1)} %pad_add_fusion.1.place, f32[768,128]{1,0:T(8,128)S(1)} %bitcast.26, f32[768,128]{1,0:T(8,128)S(1)} %collective-permute-done.1.refs_1_, f32[128,128]{1,0:T(8,128)S(1)} %first_inverse.1.refs_2_, f32[8,256]{1,0:T(8,128)S(1)} %copy-done, ...), custom_call_target="tpu_custom_call" | custom-call | tf_op jit(solution)/shard_map/finish/pallas_call | solution.py:404
  103.5 17.4 %all_to_all.34.pieces = f32[64,8,128]{2,1,0:T(8,128)S(1)} all-to-all(f32[64,8,128]{2,1,0:T(8,128)S(1)} %get-tuple-element.48), channel_id=1, replica_groups=mesh['runs'=64,'terms'=8] {'runs'}, dimensions={0} | all-to-all | bytes 524288 | tf_op jit(solution)/shard_map/all_to_all | solution.py:48
  120.9 0.1 totals.3
  121.0 15.3 %all_to_all.35 = bf16[64,8,128]{2,1,0:T(8,128)(2,1)S(1)} all-to-all(bf16[64,8,128]{2,1,0:T(8,128)(2,1)S(1)} %totals.3), channel_id=1, replica_groups=mesh['runs'=64,'terms'=8] {'runs'}, dimensions={0} | all-to-all | bytes 262144 | tf_op jit(solution)/shard_map/all_to_all | solution.py:48
  136.3 0.7 convert_bitcast_fusion
Async XLA Ops:
  0.6 28.6 %copy-start.2 = (s32[2,256]{1,0:T(2,128)S(1)}, s32[2,256]{1,0:T(2,128)}, u32[]{:S(2)}) copy-start(s32[2,256]{1,0:T(2,128)} %picks.3) | copy-start | bytes 6148
  30.3 6.7 %copy-start = (f32[8,256]{1,0:T(8,128)S(1)}, f32[8,256]{1,0:T(8,128)}, u32[]{:S(2)}) copy-start(f32[8,256]{1,0:T(8,128)} %refs_3_.1) | copy-start | bytes 24580
  31.0 7.2 %collective-permute-start = (bf16[512,256]{1,0:T(8,128)(2,1)S(1)}, bf16[512,256]{1,0:T(8,128)(2,1)S(1)}, u32[]{:S(2)}, u32[]{:S(2)}) collective-permute-start(bf16[512,256]{1,0:T(8,128)(2,1)S(1)} %get-tuple-element.46.basis.refs_4_), channel_id=1, source_target_pairs={{0,8},{8,0},{16,24},{24,16},{32,40},{40,32},{48,56},{56,48},{64,72... | collective-permute-start | bytes 786440 | tf_op jit(solution)/shard_map/ppermute | solution.py:455
  81.2 8.4 %copy-start.1 = (bf16[256,6656]{1,0:T(8,128)(2,1)S(1)}, bf16[256,6656]{1,0:T(8,128)(2,1)}, u32[]{:S(2)}) copy-start(bf16[256,6656]{1,0:T(8,128)(2,1)} %get-tuple-element.129) | copy-start | bytes 10223620
  81.2 8.4 %collective-permute-start.1 = (f32[768,128]{1,0:T(8,128)S(1)}, f32[768,128]{1,0:T(8,128)S(1)}, u32[]{:S(2)}, u32[]{:S(2)}) collective-permute-start(f32[768,128]{1,0:T(8,128)S(1)} %bitcast.24), channel_id=1, source_target_pairs={{0,8},{8,0},{16,24},{24,16},{32,40},{40,32},{48,56},{56,48},{64,72... | collective-permute-start | bytes 1179656 | tf_op jit(solution)/shard_map/ppermute | solution.py:460

commit v11 on v10

--- a/solution.py
+++ b/solution.py
@@ -66,7 +66,7 @@
     return owned, rank
 
 
-def pack_kernel(place, picks, design, packed, most, held, where, sems):
+def pack_kernel(place, picks, design, packed, most, target, held, where, sems):
     devices = packed.shape[0]
     local_terms = design.shape[1]
     chunk = local_terms // CHUNKS
@@ -83,10 +83,13 @@
     owned, rank = owners(line, devices, local_terms)
     counts = jnp.sum(owned, axis=1, keepdims=True)
     most[0] = jnp.max(counts).astype(jnp.int32)
-    me = lax.broadcasted_iota(jnp.int32, owned.shape, 0) == place[0]
-    mine = jnp.where(me, owned, 0.0)
-    slot = jnp.sum(mine * rank, axis=0, keepdims=True)
+    device = lax.broadcasted_iota(jnp.int32, owned.shape, 0)
+    slot = jnp.sum(owned * rank, axis=0, keepdims=True)
     slot = slot - (place[1] * SLOTS).astype(F32)
+    start = jnp.sum(owned * device.astype(F32), axis=0, keepdims=True) * SLOTS
+    received = jnp.where((slot >= 0.0) & (slot < SLOTS), slot + start, -1.0)
+    target[...] = jnp.broadcast_to(received, target.shape)
+    mine = jnp.where(device == place[0], owned, 0.0)
     slot = jnp.where(jnp.sum(mine, axis=0, keepdims=True) > 0.0, slot, -1.0)
     slots = lax.broadcasted_iota(jnp.int32, (SLOTS, slot.shape[1]), 0).astype(F32)
     inner = (line - place[0] * local_terms + 1).astype(F32)
@@ -116,9 +119,10 @@
         (
             jax.ShapeDtypeStruct((devices, SLOTS, rows), BF16),
             jax.ShapeDtypeStruct((1,), jnp.int32),
+            jax.ShapeDtypeStruct((SUB, picks.size), F32),
         ),
         [SCALAR, WHOLE, pl.BlockSpec(memory_space=pltpu.HBM)],
-        (WHOLE, SCALAR),
+        (WHOLE, SCALAR, WHOLE),
         [
             pltpu.VMEM(design.shape, design.dtype),
             pltpu.VMEM((SLOTS, 1), jnp.int32),
@@ -127,16 +131,10 @@
     )(place, picks, design)
 
 
-def unpack_kernel(local_terms, devices, place, picks, slots, *refs):
-    owned, rank = owners(as_line(picks), devices, local_terms)
-    first = lax.broadcasted_iota(jnp.int32, owned.shape, 0).astype(F32) * SLOTS
-    slot = jnp.sum(owned * rank, axis=0, keepdims=True)
-    slot = slot - (place[1] * SLOTS).astype(F32)
-    target = slot + jnp.sum(owned * first, axis=0, keepdims=True)
-    target = jnp.where((slot >= 0.0) & (slot < SLOTS), target, -1.0)
+def unpack_kernel(target, slots, *refs):
     shape = (slots.shape[0], target.shape[1])
     lines = lax.broadcasted_iota(jnp.int32, shape, 0).astype(F32)
-    moved = (lines == target).astype(F32).astype(BF16)
+    moved = (lines == target[:1, :]).astype(F32).astype(BF16)
     columns = lax.dot_general(
         moved, slots[...], (((0,), (0,)), ((), ())), preferred_element_type=F32
     )
@@ -145,14 +143,14 @@
     refs[-1][...] = columns.astype(BF16)
 
 
-def unpack(place, picks, slots, local_terms, *earlier):
-    devices, _, rows = slots.shape
-    operands = (place, picks, slots.reshape(-1, rows), *earlier)
+def unpack(target, slots, *earlier):
+    rows = slots.shape[-1]
+    operands = (target, slots.reshape(-1, rows), *earlier)
     return call(
-        functools.partial(unpack_kernel, local_terms, devices),
+        unpack_kernel,
         "unpack",
-        jax.ShapeDtypeStruct((picks.size, rows), BF16),
-        [SCALAR] + [WHOLE] * (len(operands) - 1),
+        jax.ShapeDtypeStruct((target.shape[1], rows), BF16),
+        [WHOLE] * len(operands),
         WHOLE,
     )(*operands)
 
@@ -435,21 +433,21 @@
 
     def fetch(turn):
         where = jnp.stack([lax.axis_index("terms"), jnp.int32(turn), core])
-        packed, most = pack(where, picks, design, term_devices)
-        return where, exchange(packed, "terms"), most
-
-    at, slots, most = fetch(0)
+        packed, most, target = pack(where, picks, design, term_devices)
+        return where, target, exchange(packed, "terms"), most
+
+    at, target, slots, most = fetch(0)
     first, slots = lax.optimization_barrier((jnp.int32(1), slots))
 
     def another(carry):
         turn, basis = carry
-        where, more, _ = fetch(turn)
-        return turn + 1, unpack(where, picks, more, local_terms, basis)
+        _, lines, more, _ = fetch(turn)
+        return turn + 1, unpack(lines, more, basis)
 
     _, basis = lax.while_loop(
         lambda carry: carry[0] * SLOTS < most[0],
         another,
-        (first, unpack(at, picks, slots, local_terms)),
+        (first, unpack(target, slots)),
     )
 
     partner = lax.ppermute(basis, "runs", swap)

time: 137 us -> 137 us (level)
  no operation moved by 1% of the time
where the time goes in v11:
time: 137 us; the launch traced here: 136 us
  blocking collectives  99.5 us (73%)
  Pallas kernels  23.1 us (17%)
  starting transfers between devices  11.3 us (8%)
    all_to_all x5, blocking collectives, exchange(): return lax.all_to_all(pieces, axis, 0, 0, axis_index_groups=groups)  99.5 us
    pallas_call x1, Pallas kernels, finish(): call(functools.partial(finish_kernel, scale), 'finish', (jax.ShapeDtypeSt...  13.9 us
    ppermute x1, starting transfers between devices, local(): partner = lax.ppermute(basis, 'runs', swap)  6.03 us
    ppermute x1, starting transfers between devices, local(): other = lax.ppermute(mine, 'runs', swap)  5.23 us
    pallas_call x1, Pallas kernels, pack(): call(pack_kernel, 'pack', (jax.ShapeDtypeStruct((devices, SLOTS, rows), B...  3.86 us
    pallas_call x1, Pallas kernels, first_inverse(): call(first_kernel, 'first_inverse', jax.ShapeDtypeStruct((BLOCK, BLOCK),...  3.18 us
  transfers between devices with their start and end apart: 2, of which 1 were waited for; matrix products, arithmetic and copies ran while one was open for 0% of the time, Pallas kernels for 3%

profile of v11, /device:TPU:1, one launch (start us, length us, event | category | flops | bytes accessed | tf_op | source)
XLA Modules:
  0.0 136.3 jit_solution(17713533033789469136)
XLA Ops:
  0.6 0.0 copy-start.2
  0.7 0.1 pad_add_fusion.1.place
  0.7 3.9 %pack.2 = (bf16[8,96,256]{2,1,0:T(8,128)(2,1)S(1)}, s32[1]{0:T(128)}, f32[8,512]{1,0:T(8,128)S(1)}) custom-call(s32[3]{0:T(128)S(1)} %pad_add_fusion.1.place, s32[2,256]{1,0:T(2,128)} %picks.1, bf16[256,6656]{1,0:T(8,128)(2,1)} %refs_5_.1), custom_call_target="tpu_custom_call" | custom-call | tf_op jit(solution)/shard_map/pack/pallas_call | solution.py:116
  4.6 24.6 %all_to_all.31 = bf16[8,96,256]{2,1,0:T(8,128)(2,1)S(1)} all-to-all(bf16[8,96,256]{2,1,0:T(8,128)(2,1)S(1)} %get-tuple-element.44), channel_id=1, replica_groups=mesh['runs'=64,'terms'=8] {'terms'}, dimensions={0} | all-to-all | bytes 786432 | tf_op jit(solution)/shard_map/all_to_all | solution.py:48
  29.2 0.4 unpack.2
  29.6 0.0 copy-done.2
  29.7 0.0 copy-start
  29.7 0.6 while.10
  30.3 6.0 %collective-permute-start = (bf16[512,256]{1,0:T(8,128)(2,1)S(1)}, bf16[512,256]{1,0:T(8,128)(2,1)S(1)}, u32[]{:S(2)}, u32[]{:S(2)}) collective-permute-start(bf16[512,256]{1,0:T(8,128)(2,1)S(1)} %get-tuple-element.49.basis.refs_4_), channel_id=1, source_target_pairs={{0,8},{8,0},{16,24},{24,16},{32,40},{40,32},{48,56},{56,48},{64,72... | collective-permute-start | bytes 786440 | tf_op jit(solution)/shard_map/ppermute | solution.py:453
  36.3 0.0 copy-done
  36.3 0.8 gram.2.other
  37.2 0.3 collective-permute-done.basis
  37.5 0.8 gram.3
  38.3 23.2 %all_to_all.32.pieces = f32[32,24,128]{2,1,0:T(8,128)S(1)} all-to-all(f32[32,24,128]{2,1,0:T(8,128)S(1)} %bitcast.28), channel_id=1, replica_groups={{0,16,32,48,64,80,96,112,128,144,160,176,192,208,224,240,256,272,288,30..., dimensions={0} | all-to-all | bytes 786432 | tf_op jit(solution)/shard_map/all_to_all | solution.py:48
  61.4 0.1 totals.2
  61.5 19.0 %all_to_all.33 = f32[32,24,128]{2,1,0:T(8,128)S(1)} all-to-all(f32[32,24,128]{2,1,0:T(8,128)S(1)} %totals.2), channel_id=1, replica_groups={{0,16,32,48,64,80,96,112,128,144,160,176,192,208,224,240,256,272,288,30..., dimensions={0} | all-to-all | bytes 786432 | tf_op jit(solution)/shard_map/all_to_all | solution.py:48
  80.5 0.0 copy-start.1
  80.5 5.2 %collective-permute-start.1 = (f32[768,128]{1,0:T(8,128)S(1)}, f32[768,128]{1,0:T(8,128)S(1)}, u32[]{:S(2)}, u32[]{:S(2)}) collective-permute-start(f32[768,128]{1,0:T(8,128)S(1)} %bitcast.24), channel_id=1, source_target_pairs={{0,8},{8,0},{16,24},{24,16},{32,40},{40,32},{48,56},{56,48},{64,72... | collective-permute-start | bytes 1179656 | tf_op jit(solution)/shard_map/ppermute | solution.py:458
  85.8 3.2 %first_inverse.1.refs_2_ = f32[128,128]{1,0:T(8,128)S(1)} custom-call(f32[768,128]{1,0:T(8,128)S(1)} %bitcast.25), custom_call_target="tpu_custom_call" | custom-call | flops 2000000000 | bytes 100000 | tf_op jit(solution)/shard_map/first_inverse/pallas_call | solution.py:320
  89.0 0.0 collective-permute-done.1.refs_1_
  89.0 0.0 copy-done.1
  89.0 13.9 %finish.1 = (f32[8,256]{1,0:T(8,128)}, f32[64,8,128]{2,1,0:T(8,128)S(1)}) custom-call(s32[3]{0:T(128)S(1)} %pad_add_fusion.1.place, f32[768,128]{1,0:T(8,128)S(1)} %bitcast.26, f32[768,128]{1,0:T(8,128)S(1)} %collective-permute-done.1.refs_1_, f32[128,128]{1,0:T(8,128)S(1)} %first_inverse.1.refs_2_, f32[8,256]{1,0:T(8,128)S(1)} %copy-done, ...), custom_call_target="tpu_custom_call" | custom-call | tf_op jit(solution)/shard_map/finish/pallas_call | solution.py:402
  102.8 17.4 %all_to_all.34.pieces = f32[64,8,128]{2,1,0:T(8,128)S(1)} all-to-all(f32[64,8,128]{2,1,0:T(8,128)S(1)} %get-tuple-element.51), channel_id=1, replica_groups=mesh['runs'=64,'terms'=8] {'runs'}, dimensions={0} | all-to-all | bytes 524288 | tf_op jit(solution)/shard_map/all_to_all | solution.py:48
  120.2 0.1 totals.3
  120.3 15.3 %all_to_all.35 = bf16[64,8,128]{2,1,0:T(8,128)(2,1)S(1)} all-to-all(bf16[64,8,128]{2,1,0:T(8,128)(2,1)S(1)} %totals.3), channel_id=1, replica_groups=mesh['runs'=64,'terms'=8] {'runs'}, dimensions={0} | all-to-all | bytes 262144 | tf_op jit(solution)/shard_map/all_to_all | solution.py:48
  135.6 0.7 convert_bitcast_fusion
Async XLA Ops:
  0.6 29.0 %copy-start.2 = (s32[2,256]{1,0:T(2,128)S(1)}, s32[2,256]{1,0:T(2,128)}, u32[]{:S(2)}) copy-start(s32[2,256]{1,0:T(2,128)} %picks.1) | copy-start | bytes 6148
  29.7 6.7 %copy-start = (f32[8,256]{1,0:T(8,128)S(1)}, f32[8,256]{1,0:T(8,128)}, u32[]{:S(2)}) copy-start(f32[8,256]{1,0:T(8,128)} %refs_3_.1) | copy-start | bytes 24580
  30.3 7.2 %collective-permute-start = (bf16[512,256]{1,0:T(8,128)(2,1)S(1)}, bf16[512,256]{1,0:T(8,128)(2,1)S(1)}, u32[]{:S(2)}, u32[]{:S(2)}) collective-permute-start(bf16[512,256]{1,0:T(8,128)(2,1)S(1)} %get-tuple-element.49.basis.refs_4_), channel_id=1, source_target_pairs={{0,8},{8,0},{16,24},{24,16},{32,40},{40,32},{48,56},{56,48},{64,72... | collective-permute-start | bytes 786440 | tf_op jit(solution)/shard_map/ppermute | solution.py:453
  80.5 8.4 %copy-start.1 = (bf16[256,6656]{1,0:T(8,128)(2,1)S(1)}, bf16[256,6656]{1,0:T(8,128)(2,1)}, u32[]{:S(2)}) copy-start(bf16[256,6656]{1,0:T(8,128)(2,1)} %get-tuple-element.134) | copy-start | bytes 10223620
  80.5 8.4 %collective-permute-start.1 = (f32[768,128]{1,0:T(8,128)S(1)}, f32[768,128]{1,0:T(8,128)S(1)}, u32[]{:S(2)}, u32[]{:S(2)}) collective-permute-start(f32[768,128]{1,0:T(8,128)S(1)} %bitcast.24), channel_id=1, source_target_pairs={{0,8},{8,0},{16,24},{24,16},{32,40},{40,32},{48,56},{56,48},{64,72... | collective-permute-start | bytes 1179656 | tf_op jit(solution)/shard_map/ppermute | solution.py:458
